TPU v7x, 32 devices: a whole 2x2x4 slice. The times are simulated.
32 devices in a mesh: dp: 8 (over z, x), section: 4 (over y, core).
Axes of the slice: x: 2, y: 2, z: 4, core: 2. Of those that a mesh axis runs over, the one named last changes fastest.
Arguments:
- memory: float32 [512, 32, 512], P(('dp', 'section')), may hold values from -6 to 6
- enc_lengths: int32 [512, 2], P(('dp', 'section')), may hold values from 1 to 24, 32 in all within a row
- frame_segment: int32 [512, 8], P(('dp', 'section')), may hold values from 0 to 1, never falling along the last dimension, each value on 1 to 6 neighbouring positions
- mel_target: float32 [512, 8, 80], P(('dp', 'section')), may hold values from -6 to 6
- prenet_keep: int32 [512, 8, 2, 256], P(('dp', 'section')), may hold values 0 or 1
- zone_keep: int32 [512, 8, 4, 1024], P(('dp', 'section')), may hold values 0 or 1
- pre_first: float32 [80, 256], replicated, may hold values from -0.625 to 0.625
- pre_second: float32 [256, 256], replicated, may hold values from -0.375 to 0.375
- att_weight: float32 [1792, 4096], P(None, ('dp', 'section')), may hold values from -0.125 to 0.125
- att_bias: float32 [4096], replicated, may hold values from -3 to 3
- query_weight: float32 [1024, 128], replicated, may hold values from -0.1875 to 0.1875
- memory_weight: float32 [512, 128], replicated, may hold values from -0.25 to 0.25
- loc_filters: float32 [32, 2, 31], replicated, may hold values from -3 to 3
- loc_dense: float32 [32, 128], replicated, may hold values from -1 to 1
- energy_v: float32 [128], replicated, may hold values from -1 to 1
- dec_weight: float32 [2560, 4096], P(None, ('dp', 'section')), may hold values from -0.125 to 0.125
- dec_bias: float32 [4096], replicated, may hold values from -3 to 3
- proj_weight: float32 [1536, 80], replicated, may hold values from -0.15625 to 0.15625
- proj_bias: float32 [80], replicated, may hold values from -3 to 3
- stop_weight: float32 [1536], replicated, may hold values from -0.15625 to 0.15625
- post_first: float32 [5, 80, 512], replicated, may hold values from -0.3125 to 0.3125
- post_mid: float32 [3, 5, 512, 512], P(None, None, None, 'section'), may hold values from -0.125 to 0.125
- post_last: float32 [5, 512, 80], replicated, may hold values from -0.125 to 0.125
- norm_gain: float32 [4, 512], replicated, may hold values from 0.5 to 1.5
- norm_shift: float32 [4, 512], replicated, may hold values from -2 to 2
- last_gain: float32 [80], replicated, may hold values from 0.5 to 1.5
- last_shift: float32 [80], replicated, may hold values from -2 to 2
- grad_after: float32 [512, 8, 80], P(('dp', 'section')), may hold values from -6 to 6
- grad_stop: float32 [512, 8], P(('dp', 'section')), may hold values from -6 to 6
Outputs:
- mel_after: float32 [512, 8, 80], P(('dp', 'section'))
- stop_logit: float32 [512, 8], P(('dp', 'section'))
- grad_memory: float32 [512, 32, 512], P(('dp', 'section'))
- g_pre_first: float32 [80, 256], replicated
- g_pre_second: float32 [256, 256], replicated
- g_att_weight: float32 [1792, 4096], P(None, ('dp', 'section'))
- g_att_bias: float32 [4096], replicated
- g_query_weight: float32 [1024, 128], replicated
- g_memory_weight: float32 [512, 128], replicated
- g_loc_filters: float32 [32, 2, 31], replicated
- g_loc_dense: float32 [32, 128], replicated
- g_energy_v: float32 [128], replicated
- g_dec_weight: float32 [2560, 4096], P(None, ('dp', 'section'))
- g_dec_bias: float32 [4096], replicated
- g_proj_weight: float32 [1536, 80], replicated
- g_proj_bias: float32 [80], replicated
- g_stop_weight: float32 [1536], replicated
- g_post_first: float32 [5, 80, 512], replicated
- g_post_mid: float32 [3, 5, 512, 512], P(None, None, None, 'section')
- g_post_last: float32 [5, 512, 80], replicated
- g_norm_gain: float32 [4, 512], replicated
- g_norm_shift: float32 [4, 512], replicated
- g_last_gain: float32 [80], replicated
- g_last_shift: float32 [80], replicated
Inputs may be any that keep to these rules, and one draw needn't show every extreme that they name: `enc_lengths`: the two lengths of a row add up to 32. `frame_segment`: never falls along a row; both utterances occur in every row, each with at most 6 frames. `zone_keep`: 1 keeps the previous state.
All inputs are finite; a program needn't handle non-finite values. No bound on the sum of `prenet_keep` or of `zone_keep` on one device may be relied on, other than what follows from the above.
Results may differ from a plain program's by a relative error of at most 0.0003.
Values sent between devices are 32-bit elements; how exact they have to be, the bound alone decides.
No kernel may reach another device: no remote copies, remote signals or barrier semaphores. Data moves between devices by JAX's collectives and lax.ppermute only.
A program may use at most 448 MiB of HBM per device.

v0:
```python
import functools
import math

import jax
import jax.numpy as jnp
from jax import lax
from jax.experimental import pallas as pl
from jax.experimental.pallas import tpu as pltpu
from jax.sharding import PartitionSpec as P

high = lax.Precision.HIGH
norm_eps = 1e-05
f32 = jnp.float32
bf16 = jnp.bfloat16
both = ("dp", "section")
lanes = 128
vmem_limit = 62 * 1024 * 1024

span = 6
shard_block = 4


def split(values):
    upper = values.astype(bf16)
    lower = (values - upper.astype(f32)).astype(bf16)
    return upper, lower


def product(left, upper, lower, transposed=False):
    rows = left.shape[0]
    left_upper, left_lower = split(left)
    stacked = jnp.concatenate([left_upper, left_lower], axis=0)
    dims = (((1,), (1,)), ((), ())) if transposed else (((1,), (0,)), ((), ()))
    first = lax.dot_general(stacked, upper, dims, preferred_element_type=f32)
    second = lax.dot_general(left_upper, lower, dims, preferred_element_type=f32)
    return first[:rows] + first[rows:] + second


def sigmoid(values):
    return 0.5 * jnp.tanh(0.5 * values) + 0.5


def lane_index(shape):
    return lax.broadcasted_iota(jnp.int32, shape, 1)


def fold_lanes(values, positions):
    copies = values
    shift = positions
    while shift < lanes:
        copies = copies + pltpu.roll(copies, shift, 1)
        shift *= 2
    return copies


def diagonal_mask(rows, positions):
    shape = (2 * rows, rows * positions)
    row = lax.broadcasted_iota(jnp.int32, shape, 0)
    group = lax.broadcasted_iota(jnp.int32, shape, 1) // positions
    return group == jnp.where(row >= rows, row - rows, row)


def spread(weights, rows, positions):
    copies = fold_lanes(weights, positions)
    wide = jnp.concatenate([copies] * (rows * positions // lanes), axis=1)
    return jnp.where(diagonal_mask(rows, positions), wide, 0.0)


def collect(wide, rows, positions):
    kept = jnp.where(diagonal_mask(rows, positions), wide, 0.0)
    total = kept[:, :lanes]
    for start in range(lanes, rows * positions, lanes):
        total = total + kept[:, start : start + lanes]
    shift = positions
    while shift < lanes:
        total = total + pltpu.roll(total, shift, 1)
        shift *= 2
    return jnp.where(lane_index(total.shape) < positions, total, 0.0)


def store_parts(block_ref, first, last, upper_ref, lower_ref, index):
    for place in range(shard_block):
        upper, lower = split(block_ref[place, first:last, :])
        upper_ref[index, :, place * lanes : (place + 1) * lanes] = upper
        lower_ref[index, :, place * lanes : (place + 1) * lanes] = lower


def gate_forward(gate_sums, cell, hidden, zone_hidden, zone_cell):
    units = cell.shape[1]
    gate_in = sigmoid(gate_sums[:, :units])
    gate_keep = sigmoid(gate_sums[:, units : 2 * units])
    update = jnp.tanh(gate_sums[:, 2 * units : 3 * units])
    gate_out = sigmoid(gate_sums[:, 3 * units :])
    new_cell = gate_keep * cell + gate_in * update
    new_hidden = gate_out * jnp.tanh(new_cell)
    hidden = zone_hidden * hidden + (1.0 - zone_hidden) * new_hidden
    cell = zone_cell * cell + (1.0 - zone_cell) * new_cell
    return hidden, cell, (gate_in, gate_keep, update, gate_out)


def gate_backward(gates, cell, zone_hidden, zone_cell, grad_hidden, grad_cell):
    units = cell.shape[1]
    gate_in = gates[:, :units]
    gate_keep = gates[:, units : 2 * units]
    update = gates[:, 2 * units : 3 * units]
    gate_out = gates[:, 3 * units :]
    bent = jnp.tanh(gate_keep * cell + gate_in * update)
    grad_new = (1.0 - zone_hidden) * grad_hidden
    grad_new_cell = grad_new * gate_out * (1.0 - bent * bent) + (1.0 - zone_cell) * grad_cell
    grad_sums = (
        grad_new_cell * update * gate_in * (1.0 - gate_in),
        grad_new_cell * cell * gate_keep * (1.0 - gate_keep),
        grad_new_cell * gate_in * (1.0 - update * update),
        grad_new * bent * gate_out * (1.0 - gate_out),
    )
    return grad_sums, zone_hidden * grad_hidden, zone_cell * grad_cell + grad_new_cell * gate_keep


def zone_masks(early_ref, late_ref):
    masks = []
    for which in range(2):
        pair = jnp.concatenate([early_ref[0, which], late_ref[0, which]], axis=0)
        masks.append(pair.astype(f32))
    return masks


def attention_forward_kernel(
    blocks,
    rows,
    positions,
    lag,
    weight_ref,
    prenet_ref,
    bias_ref,
    loc_map_ref,
    processed_ref,
    memory_ref,
    query_ref,
    energy_ref,
    zone_early_ref,
    zone_late_ref,
    resume_ref,
    allowed_ref,
    awaited,
    hidden_out,
    cell_out,
    context_out,
    gates_out,
    bent_out,
    weights_out,
    window_out,
    upper,
    lower,
    inputs,
    loc_upper,
    loc_lower,
    memory_upper,
    memory_lower,
    query_upper,
    query_lower,
    sums,
    hidden,
    cell,
    context,
    window,
):
    step = pl.program_id(0)
    prenet_width = prenet_ref.shape[1]
    context_width = context.shape[1]
    units = hidden.shape[1]
    width = shard_block * lanes

    @pl.when(step == 0)
    def prepare():
        loc_upper[...], loc_lower[...] = split(loc_map_ref[...])
        memory_upper[...], memory_lower[...] = split(memory_ref[...])
        query_upper[...], query_lower[...] = split(query_ref[...])
        hidden[...] = jnp.zeros_like(hidden)
        cell[...] = jnp.zeros_like(cell)
        context[...] = jnp.zeros_like(context)
        window[...] = jnp.zeros_like(window)

    @pl.when(step < blocks)
    def load():
        store_parts(weight_ref, prenet_width, weight_ref.shape[1], upper, lower, step)
        first = jnp.concatenate([weight_ref[place, :prenet_width, :] for place in range(shard_block)], axis=1)
        first_upper, first_lower = split(first)
        inputs[step] = product(prenet_ref[...], first_upper, first_lower) + bias_ref[0]

    @pl.when(step >= blocks)
    def advance():
        frame = step - blocks
        resume = resume_ref[0]
        hidden_now = hidden[...] * resume
        cell_now = cell[...] * resume
        context_now = context[...] * resume
        window_now = window[...] * resume
        early = pl.multiple_of(frame * rows, rows)
        late = pl.multiple_of((frame + lag) * rows, rows)
        for block in range(blocks):
            taken = slice(block * width, (block + 1) * width)
            sums[:rows, taken] = inputs[block, pl.ds(early, rows), :]
            sums[rows:, taken] = inputs[block, pl.ds(late, rows), :]

        @pl.when(frame > 0)
        def recur():
            state = jnp.concatenate([context_now, hidden_now], axis=1)
            for block in range(blocks):
                taken = slice(block * width, (block + 1) * width)
                sums[:, taken] += product(state, upper[block], lower[block])

        zone_hidden, zone_cell = zone_masks(zone_early_ref, zone_late_ref)
        hidden_new, cell_new, gates = gate_forward(sums[...], cell_now, hidden_now, zone_hidden, zone_cell)
        for place, gate in enumerate(gates):
            gates_out[0, :, place * units : (place + 1) * units] = gate
        hidden[...] = hidden_new
        cell[...] = cell_new
        hidden_out[0] = hidden_new
        cell_out[0] = cell_new
        query = product(hidden_new, query_upper[...], query_lower[...])
        located = product(window_now, loc_upper[...], loc_lower[...])
        energy_v = energy_ref[...]
        lane = lane_index((2 * rows, lanes))
        energy = jnp.zeros((2 * rows, lanes), f32)
        for place in range(positions):
            taken = slice(place * lanes, (place + 1) * lanes)
            ready = processed_ref[:, taken]
            bent = jnp.tanh(query + jnp.concatenate([ready, ready], axis=0) + located[:, taken])
            bent_out[0, :, taken] = bent
            energy = jnp.where(lane == place, jnp.sum(bent * energy_v, axis=1, keepdims=True), energy)
        masked = jnp.where(allowed_ref[...] > 0.5, energy, -1000000000.0)
        exponent = jnp.exp(masked - jnp.max(masked, axis=1, keepdims=True))
        weights = exponent / jnp.sum(exponent, axis=1, keepdims=True)
        weights = jnp.where(lane < positions, weights, 0.0)
        weights_out[0] = weights
        window_out[0] = window_now
        second = (lane >= positions) & (lane < 2 * positions)
        window[...] = weights + pltpu.roll(weights, positions, 1) + jnp.where(second, window_now, 0.0)
        context_new = product(spread(weights, rows, positions), memory_upper[...], memory_lower[...])
        context[...] = context_new
        context_out[0] = context_new


def decoder_forward_kernel(
    blocks,
    rows,
    lag,
    awaited,
    weight_ref,
    frames_ref,
    bias_ref,
    zone_early_ref,
    zone_late_ref,
    resume_ref,
    *refs,
):
    hidden_out, cell_out, gates_out, upper, lower, inputs, sums, hidden, cell = refs[awaited:]
    step = pl.program_id(0)
    units = hidden.shape[1]
    width = shard_block * lanes

    @pl.when(step == 0)
    def prepare():
        hidden[...] = jnp.zeros_like(hidden)
        cell[...] = jnp.zeros_like(cell)

    @pl.when(step < blocks)
    def load():
        split_row = frames_ref.shape[1]
        store_parts(weight_ref, split_row, weight_ref.shape[1], upper, lower, step)
        first = jnp.concatenate([weight_ref[place, :split_row, :] for place in range(shard_block)], axis=1)
        first_upper, first_lower = split(first)
        inputs[step] = product(frames_ref[...], first_upper, first_lower) + bias_ref[0]

    @pl.when(step >= blocks)
    def advance():
        frame = step - blocks
        resume = resume_ref[0]
        hidden_now = hidden[...] * resume
        cell_now = cell[...] * resume
        early = pl.multiple_of(frame * rows, rows)
        late = pl.multiple_of((frame + lag) * rows, rows)
        for block in range(blocks):
            taken = slice(block * width, (block + 1) * width)
            sums[:rows, taken] = inputs[block, pl.ds(early, rows), :]
            sums[rows:, taken] = inputs[block, pl.ds(late, rows), :]

        @pl.when(frame > 0)
        def recur():
            for block in range(blocks):
                taken = slice(block * width, (block + 1) * width)
                sums[:, taken] += product(hidden_now, upper[block], lower[block])

        zone_hidden, zone_cell = zone_masks(zone_early_ref, zone_late_ref)
        hidden_new, cell_new, gates = gate_forward(sums[...], cell_now, hidden_now, zone_hidden, zone_cell)
        for place, gate in enumerate(gates):
            gates_out[0, :, place * units : (place + 1) * units] = gate
        hidden[...] = hidden_new
        cell[...] = cell_new
        hidden_out[0] = hidden_new
        cell_out[0] = cell_new


def add_frames(total_ref, grads, frame, rows, lag):
    early = pl.multiple_of(frame * rows, rows)
    late = pl.multiple_of((frame + lag) * rows, rows)
    total_ref[pl.ds(early, rows), :] += grads[:rows]
    total_ref[pl.ds(late, rows), :] += grads[rows:]


def decoder_backward_kernel(
    blocks,
    rows,
    lag,
    own_parts,
    in_parts,
    awaited,
    *refs,
):
    own_refs = refs[:own_parts]
    in_refs = refs[own_parts : own_parts + in_parts]
    (
        grad_ref,
        gates_ref,
        cell_ref,
        zone_early_ref,
        zone_late_ref,
        resume_ref,
        valid_ref,
    ) = refs[own_parts + in_parts : own_parts + in_parts + 7]
    grad_sums_out, grad_in_out, upper, lower, frame_sums, grad_hidden, grad_cell = refs[
        own_parts + in_parts + 7 + awaited :
    ]
    step = pl.program_id(0)
    units = grad_hidden.shape[1]
    width = shard_block * lanes

    @pl.when(step == 0)
    def prepare():
        grad_hidden[...] = jnp.zeros_like(grad_hidden)
        grad_cell[...] = jnp.zeros_like(grad_cell)
        frame_sums[...] = jnp.zeros_like(frame_sums)
        grad_in_out[...] = jnp.zeros_like(grad_in_out)

    @pl.when(step < blocks)
    def load():
        for which, own_ref in enumerate(own_refs):
            part = own_ref.shape[1]
            for place in range(shard_block):
                taken = slice(place * lanes, (place + 1) * lanes)
                own_upper, own_lower = split(own_ref[place])
                upper[step, which * part : (which + 1) * part, taken] = own_upper
                lower[step, which * part : (which + 1) * part, taken] = own_lower

    @pl.when((step >= blocks) & (step < blocks + span))
    def retreat():
        frame = span - 1 - (step - blocks)
        resume = resume_ref[0]
        early = pl.multiple_of(frame * rows, rows)
        late = pl.multiple_of((frame + lag) * rows, rows)
        arriving = jnp.concatenate([grad_ref[pl.ds(early, rows), :], grad_ref[pl.ds(late, rows), :]], axis=0)
        total = grad_hidden[...] + arriving * valid_ref[0]
        cell_now = cell_ref[0] * jnp.where(frame > 0, resume, 0.0)
        zone_hidden, zone_cell = zone_masks(zone_early_ref, zone_late_ref)
        grad_sums, passed_hidden, passed_cell = gate_backward(
            gates_ref[0], cell_now, zone_hidden, zone_cell, total, grad_cell[...]
        )
        grad_cell[...] = passed_cell * resume
        grad_hidden[...] = passed_hidden
        for place, grads in enumerate(grad_sums):
            for part in range(units // width):
                block = place * (units // width) + part
                add_frames(frame_sums.at[block], grads[:, part * width : (part + 1) * width], frame, rows, lag)

        @pl.when(frame > 0)
        def recur():
            carried = grad_hidden[...]
            for place, grads in enumerate(grad_sums):
                for part in range(units // width):
                    block = place * (units // width) + part
                    taken = grads[:, part * width : (part + 1) * width]
                    carried = carried + product(taken, upper[block], lower[block], transposed=True)
            grad_hidden[...] = carried * resume

    @pl.when(step >= blocks + span)
    def pass_on():
        block = step - blocks - span
        grads = frame_sums[block]
        for place in range(shard_block):
            grad_sums_out[place] = grads[:, place * lanes : (place + 1) * lanes]
        for which, in_ref in enumerate(in_refs):
            part = in_ref.shape[1]
            taken = slice(which * part, (which + 1) * part)
            first = jnp.concatenate([in_ref[place] for place in range(shard_block)], axis=1)
            first_upper, first_lower = split(first)
            grad_in_out[:, taken] += product(grads, first_upper, first_lower, transposed=True)


def attention_backward_kernel(
    blocks,
    rows,
    positions,
    lag,
    weight_ref,
    grad_hidden_ref,
    grad_context_ref,
    gates_ref,
    cell_ref,
    bent_ref,
    weights_ref,
    window_ref,
    loc_map_ref,
    memory_ref,
    query_ref,
    energy_ref,
    zone_early_ref,
    zone_late_ref,
    resume_ref,
    valid_ref,
    next_resume_ref,
    awaited,
    grad_sums_out,
    grad_bias_out,
    grad_prenet_out,
    grad_query_out,
    grad_processed_out,
    grad_memory_out,
    grad_loc_out,
    grad_energy_out,
    upper,
    lower,
    first_upper,
    first_lower,
    frame_sums,
    loc_upper,
    loc_lower,
    memory_upper,
    memory_lower,
    query_upper,
    query_lower,
    grad_bent,
    grad_contexts,
    diagonals,
    windows,
    grad_hidden,
    grad_cell,
    grad_context,
    grad_window,
):
    step = pl.program_id(0)
    units = grad_hidden.shape[1]
    context_width = grad_context.shape[1]
    prenet_width = first_upper.shape[1]
    width = shard_block * lanes
    pair = 2 * rows

    @pl.when(step == 0)
    def prepare():
        loc_upper[...], loc_lower[...] = split(loc_map_ref[...])
        memory_upper[...], memory_lower[...] = split(memory_ref[...])
        query_upper[...], query_lower[...] = split(query_ref[...])
        grad_hidden[...] = jnp.zeros_like(grad_hidden)
        grad_cell[...] = jnp.zeros_like(grad_cell)
        grad_context[...] = jnp.zeros_like(grad_context)
        grad_window[...] = jnp.zeros_like(grad_window)
        frame_sums[...] = jnp.zeros_like(frame_sums)
        grad_query_out[...] = jnp.zeros_like(grad_query_out)
        grad_processed_out[...] = jnp.zeros_like(grad_processed_out)
        grad_energy_out[...] = jnp.zeros_like(grad_energy_out)

    @pl.when(step < blocks)
    def load():
        store_parts(weight_ref, prenet_width, weight_ref.shape[1], upper, lower, step)
        store_parts(weight_ref, 0, prenet_width, first_upper, first_lower, step)

    @pl.when(step >= blocks)
    def retreat():
        frame = span - 1 - (step - blocks)
        resume = resume_ref[0]
        valid = valid_ref[0]
        early = pl.multiple_of(frame * rows, rows)
        late = pl.multiple_of((frame + lag) * rows, rows)
        here = pl.multiple_of(frame * pair, pair)
        lane = lane_index((pair, lanes))
        arriving = jnp.concatenate(
            [grad_context_ref[pl.ds(early, rows), :], grad_context_ref[pl.ds(late, rows), :]], axis=0
        )
        context_total = grad_context[...] + arriving * valid
        grad_contexts[pl.ds(here, pair), :] = context_total
        weights = weights_ref[0]
        diagonals[pl.ds(here, pair), :] = spread(weights, rows, positions)
        windows[pl.ds(here, pair), :] = window_ref[0]
        window_grad = grad_window[...]
        wide = product(context_total, memory_upper[...], memory_lower[...], transposed=True)
        grad_weights = collect(wide, rows, positions) + jnp.where(
            lane < positions, window_grad + pltpu.roll(window_grad, lanes - positions, 1), 0.0
        )
        inner = jnp.sum(weights * grad_weights, axis=1, keepdims=True)
        grad_energy = weights * (grad_weights - inner)
        energy_v = energy_ref[...]
        energy_total = jnp.zeros((pair, lanes), f32)
        query_total = jnp.zeros((pair, lanes), f32)
        for place in range(positions):
            taken = slice(place * lanes, (place + 1) * lanes)
            bent = bent_ref[0, :, taken]
            column = jnp.sum(jnp.where(lane == place, grad_energy, 0.0), axis=1, keepdims=True)
            energy_total = energy_total + column * bent
            slope = column * energy_v * (1.0 - bent * bent)
            query_total = query_total + slope
            grad_bent[pl.ds(here, pair), taken] = slope
            grad_processed_out[:, taken] += slope[:rows] + slope[rows:]
        grad_energy_out[...] += energy_total
        add_frames(grad_query_out, query_total, frame, rows, lag)
        slopes = grad_bent[pl.ds(here, pair), :]
        moved = product(slopes, loc_upper[...], loc_lower[...], transposed=True)
        second = (lane >= positions) & (lane < 2 * positions)
        grad_window[...] = resume * (moved + jnp.where(second, window_grad, 0.0))

        arriving = jnp.concatenate(
            [grad_hidden_ref[pl.ds(early, rows), :], grad_hidden_ref[pl.ds(late, rows), :]], axis=0
        )
        total = grad_hidden[...] + arriving * valid
        total = total + product(query_total, query_upper[...], query_lower[...], transposed=True)
        cell_now = cell_ref[0] * jnp.where(frame > 0, resume, 0.0)
        zone_hidden, zone_cell = zone_masks(zone_early_ref, zone_late_ref)
        grad_sums, passed_hidden, passed_cell = gate_backward(
            gates_ref[0], cell_now, zone_hidden, zone_cell, total, grad_cell[...]
        )
        grad_cell[...] = passed_cell * resume
        for place, grads in enumerate(grad_sums):
            for part in range(units // width):
                block = place * (units // width) + part
                add_frames(frame_sums.at[block], grads[:, part * width : (part + 1) * width], frame, rows, lag)

        @pl.when(frame > 0)
        def recur():
            carried = jnp.zeros((pair, context_width + units), f32)
            for place, grads in enumerate(grad_sums):
                for part in range(units // width):
                    block = place * (units // width) + part
                    taken = grads[:, part * width : (part + 1) * width]
                    carried = carried + product(taken, upper[block], lower[block], transposed=True)
            grad_context[...] = carried[:, :context_width] * resume
            grad_hidden[...] = (carried[:, context_width:] + passed_hidden) * resume

    @pl.when(step == blocks + span - 1)
    def finish():
        prenet_grad = jnp.zeros(grad_prenet_out.shape, f32)
        frame_rows = frame_sums.shape[1]
        for block in range(blocks):
            grads = frame_sums[block]
            prenet_grad = prenet_grad + product(grads, first_upper[block], first_lower[block], transposed=True)
            grad_bias_out[:, block * width : (block + 1) * width] = jnp.sum(grads, axis=0, keepdims=True)
            later = jnp.concatenate([grads[rows:], jnp.zeros((rows, width), f32)], axis=0) * next_resume_ref[...]
            for place in range(shard_block):
                grad_sums_out[block * shard_block + place] = later[:, place * lanes : (place + 1) * lanes]
        grad_prenet_out[...] = prenet_grad
        context_upper, context_lower = split(grad_contexts[...])
        grad_memory_out[...] = product(diagonals[...].T, context_upper, context_lower)
        window_turned = windows[...].T
        for block in range(blocks):
            taken = slice(block * width, (block + 1) * width)
            bent_upper, bent_lower = split(grad_bent[:, taken])
            grad_loc_out[:, taken] = product(window_turned, bent_upper, bent_lower)


def split_kernel(values_ref, upper_ref, lower_ref):
    upper_ref[...], lower_ref[...] = split(values_ref[...])


def split_matrix(values):
    shape = jax.ShapeDtypeStruct(values.shape, bf16)
    return pl.pallas_call(
        split_kernel,
        out_shape=[shape, shape],
        compiler_params=pltpu.CompilerParams(vmem_limit_bytes=vmem_limit),
        name="split_matrix",
    )(values)


def join_kernel(count, *refs):
    out_ref, token_ref = refs[-2:]
    start = 0
    for ref in refs[:count]:
        out_ref[start : start + ref.shape[0]] = ref[...]
        start += ref.shape[0]
    token_ref[...] = jnp.zeros_like(token_ref)


def join_rows(arrays, awaited):
    total = sum(array.shape[0] for array in arrays)
    return pl.pallas_call(
        functools.partial(join_kernel, len(arrays)),
        in_specs=[pl.BlockSpec(memory_space=pltpu.VMEM)] * len(arrays)
        + [pl.BlockSpec(memory_space=pl.ANY)] * len(awaited),
        out_shape=[jax.ShapeDtypeStruct((total, lanes), f32), jax.ShapeDtypeStruct((8, lanes), f32)],
        compiler_params=pltpu.CompilerParams(vmem_limit_bytes=vmem_limit),
        name="join_rows",
    )(*arrays, *awaited)


def pack_sums(*sums):
    rows = []
    for row in sums:
        channels = row.shape[1]
        if channels % lanes:
            row = jnp.concatenate([row, jnp.zeros((1, -channels % lanes), f32)], axis=1)
        rows += [row[:, start : start + lanes] for start in range(0, row.shape[1], lanes)]
    if len(rows) < 8:
        rows.append(jnp.zeros((8 - len(rows), lanes), f32))
    return jnp.concatenate(rows, axis=0)


def unpack_sums(packed, channels, number=2):
    count = -(-channels // lanes)
    rows = []
    for row in range(number):
        pieces = [packed[row * count + place : row * count + place + 1] for place in range(count)]
        rows.append(jnp.concatenate(pieces, axis=1)[:, :channels])
    return rows


def moved_rows(values, shift):
    if shift > 0:
        return jnp.concatenate([jnp.zeros((shift, values.shape[1]), f32), values[:-shift]], axis=0)
    if shift < 0:
        return jnp.concatenate([values[-shift:], jnp.zeros((-shift, values.shape[1]), f32)], axis=0)
    return values


def convolve(values, same, upper_ref, lower_ref, rows):
    kernel = upper_ref.shape[0] // values.shape[1]
    channels = values.shape[1]
    total = None
    for tap in range(kernel):
        taken = slice(tap * channels, (tap + 1) * channels)
        moved = moved_rows(values, (kernel // 2 - tap) * rows) * same[:, tap : tap + 1]
        piece = product(moved, upper_ref[taken, :], lower_ref[taken, :])
        total = piece if total is None else total + piece
    return total


def send_sums(copies_ref, *values):
    packed = pack_sums(*[jnp.sum(value, axis=0, keepdims=True) for value in values])
    for place in range(copies_ref.shape[0]):
        copies_ref[place] = packed


def post_first_kernel(rows, values_ref, same_ref, upper_ref, lower_ref, conv_out, copies_out):
    conv = convolve(values_ref[...], same_ref[...], upper_ref, lower_ref, rows)
    conv_out[...] = conv
    send_sums(copies_out, conv, conv * conv)


def post_next_kernel(
    rows,
    frame_count,
    conv_ref,
    sums_ref,
    gain_ref,
    shift_ref,
    same_ref,
    upper_ref,
    lower_ref,
    *refs,
):
    *grad_refs, scaled_out, active_out, inverse_out, conv_out, copies_out = refs
    conv = conv_ref[...]
    first, second = unpack_sums(jnp.sum(sums_ref[...], axis=0), conv.shape[1])
    average = first / frame_count
    inverse = lax.rsqrt(second / frame_count - average * average + norm_eps)
    scaled = (conv - average) * inverse
    active = jnp.tanh(scaled * gain_ref[...] + shift_ref[...])
    scaled_out[...] = scaled
    active_out[...] = active
    inverse_out[...] = inverse
    conv = convolve(active, same_ref[...], upper_ref, lower_ref, rows)
    conv_out[...] = conv
    grads = [piece for ref in grad_refs for piece in (ref[...], ref[...] * conv)]
    send_sums(copies_out, conv, conv * conv, *grads)


def conv_back(grad_conv, same, upper_ref, lower_ref, channels, rows):
    kernel = upper_ref.shape[0] // channels
    total = None
    for tap in range(kernel):
        taken = slice(tap * channels, (tap + 1) * channels)
        piece = product(grad_conv, upper_ref[taken, :], lower_ref[taken, :], transposed=True)
        piece = moved_rows(piece * same[:, tap : tap + 1], (tap - kernel // 2) * rows)
        total = piece if total is None else total + piece
    return total


def post_turn_kernel(
    rows,
    frame_count,
    grad_ref,
    conv_ref,
    sums_ref,
    before_ref,
    gain_ref,
    shift_ref,
    same_ref,
    upper_ref,
    lower_ref,
    active_ref,
    scaled_below_ref,
    after_out,
    conv_out,
    sums_out,
    grad_out,
    copies_out,
):
    conv = conv_ref[...]
    grad = grad_ref[...]
    gain = gain_ref[...]
    first, second, shift_grad, mixed = unpack_sums(jnp.sum(sums_ref[...], axis=0), conv.shape[1], 4)
    average = first / frame_count
    inverse = lax.rsqrt(second / frame_count - average * average + norm_eps)
    scaled = (conv - average) * inverse
    after_out[...] = before_ref[...] + scaled * gain + shift_ref[...]
    gain_grad = inverse * (mixed - average * shift_grad)
    sums_out[...] = pack_sums(shift_grad, gain_grad)
    grad_conv = inverse * gain * (grad - (shift_grad + scaled * gain_grad) / frame_count)
    conv_out[...] = jnp.concatenate([grad_conv, jnp.zeros((conv.shape[0], -conv.shape[1] % lanes), f32)], axis=1)
    active = active_ref[...]
    total = conv_back(grad_conv, same_ref[...], upper_ref, lower_ref, active.shape[1], rows)
    total = total * (1.0 - active * active)
    send_sums(copies_out, total, total * scaled_below_ref[...])
    grad_out[...] = total


def post_back_kernel(
    rows,
    frame_count,
    has_lower,
    awaited,
    grad_ref,
    scaled_ref,
    sums_ref,
    inverse_ref,
    gain_ref,
    same_ref,
    upper_ref,
    lower_ref,
    *refs,
):
    if has_lower:
        active_ref, scaled_below_ref = refs[:2]
        conv_out, sums_out, grad_out, copies_out = refs[2 + awaited :]
    else:
        conv_out, sums_out, grad_out = refs[awaited:]
    grad = grad_ref[...]
    scaled = scaled_ref[...]
    same = same_ref[...]
    packed = jnp.sum(sums_ref[...], axis=0)
    sums_out[...] = packed
    shift_grad, gain_grad = unpack_sums(packed, grad.shape[1])
    grad_conv = inverse_ref[...] * gain_ref[...] * (grad - (shift_grad + scaled * gain_grad) / frame_count)
    conv_out[...] = grad_conv
    total = conv_back(grad_conv, same, upper_ref, lower_ref, grad_out.shape[1], rows)
    if has_lower:
        active = active_ref[...]
        total = total * (1.0 - active * active)
        send_sums(copies_out, total, total * scaled_below_ref[...])
    grad_out[...] = total


def post_call(kernel, outs, name, operands, awaited=()):
    shapes = [jax.ShapeDtypeStruct(shape, f32) for shape in outs]
    in_specs = [pl.BlockSpec(memory_space=pltpu.VMEM)] * len(operands)
    in_specs += [pl.BlockSpec(memory_space=pl.ANY)] * len(awaited)
    return pl.pallas_call(
        kernel,
        in_specs=in_specs,
        out_specs=[pl.BlockSpec(memory_space=pltpu.VMEM)] * len(outs),
        out_shape=shapes,
        compiler_params=pltpu.CompilerParams(vmem_limit_bytes=vmem_limit),
        name=name,
    )(*operands, *awaited)


def share_sums(copies):
    return lax.all_to_all(copies, both, 0, 0)


def tap_gradient_kernel(rows, inputs_ref, grads_ref, same_ref, out_ref):
    groups, frame_rows, columns = grads_ref.shape
    kernel = out_ref.shape[0]
    margin = kernel // 2
    moved = []
    for tap in range(kernel):
        pieces = []
        for group in range(groups):
            masked = grads_ref[group] * same_ref[group][:, tap : tap + 1]
            pieces.append(moved_rows(masked, (tap - margin) * rows))
        moved.append(jnp.concatenate(pieces, axis=0))
    upper, lower = split(jnp.concatenate(moved, axis=1))
    inputs = inputs_ref[...].reshape(groups * frame_rows, -1)
    result = product(inputs.T, upper, lower)
    for tap in range(kernel):
        out_ref[tap] = result[:, tap * columns : (tap + 1) * columns]


def tap_gradient(inputs, grads, same_segment, kernel, rows):
    out = jax.ShapeDtypeStruct((kernel, inputs.shape[2], grads.shape[2]), f32)
    return pl.pallas_call(
        functools.partial(tap_gradient_kernel, rows),
        out_shape=out,
        compiler_params=pltpu.CompilerParams(vmem_limit_bytes=vmem_limit),
        name="tap_gradient",
    )(inputs, grads, same_segment)


def frame_product_kernel(pieces, *refs):
    inputs = refs[:-3]
    grads_ref, out_ref, total = refs[-3:]
    step = pl.program_id(0)

    @pl.when(step == 0)
    def prepare():
        total[...] = jnp.zeros_like(total)

    blocks, groups = grads_ref.shape[:2]
    grads = jnp.concatenate(
        [jnp.concatenate([grads_ref[block, group] for group in range(groups)], axis=1) for block in range(blocks)],
        axis=0,
    )
    columns = grads.shape[1]
    turned_upper, turned_lower = split(grads.T)
    stacked = jnp.concatenate([turned_upper, turned_lower], axis=0)
    start = 0
    for which, first, last in pieces:
        upper, lower = split(inputs[which][:, first:last])
        one = jnp.dot(stacked, upper, preferred_element_type=f32)
        two = jnp.dot(turned_upper, lower, preferred_element_type=f32)
        total[:, start : start + last - first] += one[:columns] + one[columns:] + two
        start += last - first

    @pl.when(step == pl.num_programs(0) - 1)
    def finish():
        parts, _, width = out_ref.shape
        for part in range(parts):
            out_ref[part] = total[part * width : (part + 1) * width].T


def frame_product(inputs, grads, pieces):
    sources, groups, frames = grads.shape[:3]
    parts = lax.axis_size("section")
    block = 4 if sources % 4 == 0 else 1
    columns = groups // parts * lanes
    depth = sum(last - first for _, first, last in pieces)

    def block_spec(array):
        return pl.BlockSpec((block * frames, array.shape[1]), lambda step: (step, 0))

    return pl.pallas_call(
        functools.partial(frame_product_kernel, pieces),
        grid=(sources // block,),
        in_specs=[block_spec(array) for array in inputs]
        + [pl.BlockSpec((block, groups, frames, lanes), lambda step: (step, 0, 0, 0))],
        out_specs=pl.BlockSpec((parts, depth, columns), lambda step: (0, 0, 0)),
        out_shape=jax.ShapeDtypeStruct((parts, depth, columns), f32),
        scratch_shapes=[pltpu.VMEM((parts * columns, depth), f32)],
        compiler_params=params(),
        name="frame_product",
    )(*inputs, grads)


def whole_spec(array):
    rank = len(array.shape)
    return pl.BlockSpec(array.shape, lambda step: (0,) * rank)


def timed_spec(array, place, depth=None):
    shape = (1,) + tuple(array.shape[1:])
    rank = len(array.shape)
    return pl.BlockSpec(shape, lambda step: (place(step),) + (0,) * (rank - 1))


def shard_spec(array, place):
    shape = (shard_block,) + tuple(array.shape[1:])
    return pl.BlockSpec(shape, lambda step: (place(step), 0, 0))


def zone_spec(zone, place, which):
    shape = (1, 2) + tuple(zone.shape[2:])
    return pl.BlockSpec(shape, lambda step: (place(step), which, 0, 0))


def out_spec(shape):
    rank = len(shape)
    return pl.BlockSpec(shape, lambda step: (0,) * rank)


def cost(weights, passes):
    return pl.CostEstimate(flops=2 * 256 * weights * 2 * passes, bytes_accessed=4 * weights, transcendentals=0)


def params():
    return pltpu.CompilerParams(vmem_limit_bytes=vmem_limit, dimension_semantics=("arbitrary",))


def attention_forward(
    weight, prenet_out, bias, loc_map, processed, memory, query_weight, energy_v, zone, resume, allowed, lag, awaited
):
    groups, depth = weight.shape[:2]
    blocks = groups // shard_block
    rows = memory.shape[0] // (processed.shape[1] // lanes)
    positions = processed.shape[1] // lanes
    columns = groups * lanes
    units = columns // 4
    context_width = memory.shape[1]
    frame_rows = prenet_out.shape[0]
    rest = depth - prenet_out.shape[1]
    width = shard_block * lanes
    pair = 2 * rows

    def shard(step):
        return jnp.minimum(step, blocks - 1)

    def timed(step):
        return jnp.clip(step - blocks, 0, span - 1)

    def later(step):
        return timed(step) + lag

    timed_shapes = [
        (span, pair, units),
        (span, pair, units),
        (span, pair, context_width),
        (span, pair, columns),
        (span, pair, positions * lanes),
        (span, pair, lanes),
        (span, pair, lanes),
    ]
    out_shape = [jax.ShapeDtypeStruct(shape, f32) for shape in timed_shapes]
    bias_blocks = bias.reshape(blocks, 1, width)
    return pl.pallas_call(
        functools.partial(attention_forward_kernel, blocks, rows, positions, lag),
        grid=(blocks + span,),
        in_specs=[
            shard_spec(weight, shard),
            whole_spec(prenet_out),
            timed_spec(bias_blocks, shard),
            whole_spec(loc_map),
            whole_spec(processed),
            whole_spec(memory),
            whole_spec(query_weight),
            whole_spec(energy_v),
            zone_spec(zone, timed, 0),
            zone_spec(zone, later, 0),
            timed_spec(resume, timed),
            whole_spec(allowed),
            pl.BlockSpec(memory_space=pl.ANY),
        ],
        out_specs=[timed_spec(shape, timed) for shape in out_shape],
        out_shape=out_shape,
        scratch_shapes=[
            pltpu.VMEM((blocks, rest, width), bf16),
            pltpu.VMEM((blocks, rest, width), bf16),
            pltpu.VMEM((blocks, frame_rows, width), f32),
            pltpu.VMEM(loc_map.shape, bf16),
            pltpu.VMEM(loc_map.shape, bf16),
            pltpu.VMEM(memory.shape, bf16),
            pltpu.VMEM(memory.shape, bf16),
            pltpu.VMEM(query_weight.shape, bf16),
            pltpu.VMEM(query_weight.shape, bf16),
            pltpu.VMEM((pair, columns), f32),
            pltpu.VMEM((pair, units), f32),
            pltpu.VMEM((pair, units), f32),
            pltpu.VMEM((pair, context_width), f32),
            pltpu.VMEM((pair, lanes), f32),
        ],
        compiler_params=params(),
        cost_estimate=cost(depth * columns, span),
        name="attention_forward",
    )(
        weight,
        prenet_out,
        bias_blocks,
        loc_map,
        processed,
        memory,
        query_weight,
        energy_v,
        zone,
        zone,
        resume,
        allowed,
        awaited,
    )


def decoder_forward(weight, frames, bias, zone, resume, rows, lag, awaited):
    groups = weight.shape[0]
    blocks = groups // shard_block
    columns = groups * lanes
    units = columns // 4
    width = shard_block * lanes
    pair = 2 * rows

    def shard(step):
        return jnp.minimum(step, blocks - 1)

    def timed(step):
        return jnp.clip(step - blocks, 0, span - 1)

    def later(step):
        return timed(step) + lag

    timed_shapes = [(span, pair, units), (span, pair, units), (span, pair, columns)]
    out_shape = [jax.ShapeDtypeStruct(shape, f32) for shape in timed_shapes]
    bias_blocks = bias.reshape(blocks, 1, width)
    return pl.pallas_call(
        functools.partial(decoder_forward_kernel, blocks, rows, lag, len(awaited)),
        grid=(blocks + span,),
        in_specs=[
            shard_spec(weight, shard),
            whole_spec(frames),
            timed_spec(bias_blocks, shard),
            zone_spec(zone, timed, 1),
            zone_spec(zone, later, 1),
            timed_spec(resume, timed),
        ]
        + [pl.BlockSpec(memory_space=pl.ANY)] * len(awaited),
        out_specs=[timed_spec(shape, timed) for shape in out_shape],
        out_shape=out_shape,
        scratch_shapes=[
            pltpu.VMEM((blocks, units, width), bf16),
            pltpu.VMEM((blocks, units, width), bf16),
            pltpu.VMEM((blocks, frames.shape[0], width), f32),
            pltpu.VMEM((pair, columns), f32),
            pltpu.VMEM((pair, units), f32),
            pltpu.VMEM((pair, units), f32),
        ],
        compiler_params=params(),
        cost_estimate=cost(weight.shape[1] * columns, span // 2),
        name="decoder_forward",
    )(weight, frames, bias_blocks, zone, zone, resume, *awaited)


def decoder_backward(weight, grad, gates, cells, zone, resume, valid, rows, lag, awaited):
    groups, depth = weight.shape[:2]
    blocks = groups // shard_block
    columns = groups * lanes
    units = columns // 4
    split_row = depth - units
    width = shard_block * lanes
    pair = 2 * rows
    frame_rows = grad.shape[0]
    part = math.gcd(units, split_row)
    own_parts = units // part
    in_parts = split_row // part

    def part_spec(index):
        return pl.BlockSpec((shard_block, part, lanes), index)

    def own_spec(which):
        return part_spec(lambda step: (shard(step), in_parts + which, 0))

    def in_spec(which):
        return part_spec(lambda step: (last_shard(step), which, 0))

    def shard(step):
        return jnp.minimum(step, blocks - 1)

    def last_shard(step):
        return jnp.clip(step - blocks - span, 0, blocks - 1)

    def timed(step):
        return span - 1 - jnp.clip(step - blocks, 0, span - 1)

    def later(step):
        return timed(step) + lag

    def before(step):
        return jnp.maximum(timed(step) - 1, 0)

    out_shape = [
        jax.ShapeDtypeStruct((groups, frame_rows, lanes), f32),
        jax.ShapeDtypeStruct((frame_rows, split_row), f32),
    ]
    return pl.pallas_call(
        functools.partial(decoder_backward_kernel, blocks, rows, lag, own_parts, in_parts, len(awaited)),
        grid=(2 * blocks + span,),
        in_specs=[own_spec(which) for which in range(own_parts)]
        + [in_spec(which) for which in range(in_parts)]
        + [
            whole_spec(grad),
            timed_spec(gates, timed),
            timed_spec(cells, before),
            zone_spec(zone, timed, 1),
            zone_spec(zone, later, 1),
            timed_spec(resume, timed),
            timed_spec(valid, timed),
        ]
        + [pl.BlockSpec(memory_space=pl.ANY)] * len(awaited),
        out_specs=[shard_spec(out_shape[0], last_shard), whole_spec(out_shape[1])],
        out_shape=out_shape,
        scratch_shapes=[
            pltpu.VMEM((blocks, units, width), bf16),
            pltpu.VMEM((blocks, units, width), bf16),
            pltpu.VMEM((blocks, frame_rows, width), f32),
            pltpu.VMEM((pair, units), f32),
            pltpu.VMEM((pair, units), f32),
        ],
        compiler_params=params(),
        cost_estimate=cost(depth * columns, 4 * span),
        name="decoder_backward",
    )(*[weight] * (own_parts + in_parts), grad, gates, cells, zone, zone, resume, valid, *awaited)


def attention_backward(
    weight,
    grad_hidden,
    grad_context,
    gates,
    cells,
    bent,
    weights,
    window,
    loc_map,
    memory,
    query_weight,
    energy_v,
    zone,
    resume,
    valid,
    next_resume,
    rows,
    positions,
    prenet_width,
    lag,
    awaited,
):
    groups, depth = weight.shape[:2]
    blocks = groups // shard_block
    columns = groups * lanes
    units = columns // 4
    width = shard_block * lanes
    pair = 2 * rows
    frame_rows = grad_hidden.shape[0]
    context_width = grad_context.shape[1]
    rest = depth - prenet_width

    def shard(step):
        return jnp.minimum(step, blocks - 1)

    def timed(step):
        return span - 1 - jnp.clip(step - blocks, 0, span - 1)

    def later(step):
        return timed(step) + lag

    def before(step):
        return jnp.maximum(timed(step) - 1, 0)

    shapes = [
        (groups, frame_rows, lanes),
        (1, columns),
        (frame_rows, prenet_width),
        (frame_rows, lanes),
        (rows, positions * lanes),
        (rows * positions, context_width),
        loc_map.shape,
        (pair, lanes),
    ]
    return pl.pallas_call(
        functools.partial(attention_backward_kernel, blocks, rows, positions, lag),
        grid=(blocks + span,),
        in_specs=[
            shard_spec(weight, shard),
            whole_spec(grad_hidden),
            whole_spec(grad_context),
            timed_spec(gates, timed),
            timed_spec(cells, before),
            timed_spec(bent, timed),
            timed_spec(weights, timed),
            timed_spec(window, timed),
            whole_spec(loc_map),
            whole_spec(memory),
            whole_spec(query_weight),
            whole_spec(energy_v),
            zone_spec(zone, timed, 0),
            zone_spec(zone, later, 0),
            timed_spec(resume, timed),
            timed_spec(valid, timed),
            whole_spec(next_resume),
        ]
        + [pl.BlockSpec(memory_space=pl.ANY)] * len(awaited),
        out_specs=[out_spec(shape) for shape in shapes],
        out_shape=[jax.ShapeDtypeStruct(shape, f32) for shape in shapes],
        scratch_shapes=[
            pltpu.VMEM((blocks, rest, width), bf16),
            pltpu.VMEM((blocks, rest, width), bf16),
            pltpu.VMEM((blocks, prenet_width, width), bf16),
            pltpu.VMEM((blocks, prenet_width, width), bf16),
            pltpu.VMEM((blocks, frame_rows, width), f32),
            pltpu.VMEM(loc_map.shape, bf16),
            pltpu.VMEM(loc_map.shape, bf16),
            pltpu.VMEM(memory.shape, bf16),
            pltpu.VMEM(memory.shape, bf16),
            pltpu.VMEM(query_weight.shape, bf16),
            pltpu.VMEM(query_weight.shape, bf16),
            pltpu.VMEM((span * pair, positions * lanes), f32),
            pltpu.VMEM((span * pair, context_width), f32),
            pltpu.VMEM((span * pair, rows * positions), f32),
            pltpu.VMEM((span * pair, lanes), f32),
            pltpu.VMEM((pair, units), f32),
            pltpu.VMEM((pair, units), f32),
            pltpu.VMEM((pair, context_width), f32),
            pltpu.VMEM((pair, lanes), f32),
        ],
        compiler_params=params(),
        cost_estimate=cost(lanes * lanes, 1),
        name="attention_backward",
    )(
        weight,
        grad_hidden,
        grad_context,
        gates,
        cells,
        bent,
        weights,
        window,
        loc_map,
        memory,
        query_weight,
        energy_v,
        zone,
        zone,
        resume,
        valid,
        next_resume,
        *awaited,
    )


def dot(left, right, left_dim=1, right_dim=0):
    return lax.dot_general(
        left, right, (((left_dim,), (right_dim,)), ((), ())), precision=high, preferred_element_type=f32
    )


def gather_columns(shard):
    depth, width = shard.shape
    if width % lanes:
        full = lax.all_gather(shard, both, axis=1, tiled=True)
        return full.reshape(depth, -1, lanes).swapaxes(0, 1)
    stacked = lax.all_gather(shard, both, axis=0)
    if width == lanes:
        return stacked
    return stacked.reshape(-1, depth, width // lanes, lanes).swapaxes(1, 2).reshape(-1, depth, lanes)


def along_core(values):
    return lax.ppermute(values, "section", [(place, place ^ 1) for place in range(4)])


def along_y(values):
    return lax.ppermute(values, "section", [(place, place ^ 2) for place in range(4)])


def gather_y(values):
    return jnp.stack([values, along_y(values)])


def gather_core(two):
    return jnp.concatenate([two, along_core(two)], axis=0)


def gather_section(values):
    return gather_core(gather_y(values))


def section_order(four, own):
    entries = []
    for place in range(4):
        offset = own ^ place
        held = (offset % 2) * 2 + offset // 2
        entries.append(lax.dynamic_index_in_dim(four, held, 0, keepdims=False))
    return entries


def section_columns(pair, layers):
    own = lax.axis_index("section")
    four = gather_core(pair)
    depth = four.shape[1] // layers
    whole = []
    for layer in range(layers):
        blocks = section_order(four[:, layer * depth : (layer + 1) * depth], own)
        whole.append(jnp.concatenate(blocks, axis=1))
    return whole


def own_columns(values, columns):
    own = lax.axis_index("section")
    total = values[..., :columns]
    for place in range(1, values.shape[-1] // columns):
        total = jnp.where(own == place, values[..., place * columns : (place + 1) * columns], total)
    return total


def flat_join(arrays, devices):
    pieces = []
    for array in arrays:
        flat = array.reshape(-1)
        flat = jnp.pad(flat, (0, -flat.shape[0] % lanes))
        pieces.append(flat.reshape(-1, lanes))
    joined = jnp.concatenate(pieces, axis=0)
    joined = jnp.pad(joined, ((0, -joined.shape[0] % (8 * devices)), (0, 0)))
    return joined.reshape(devices, -1, lanes)


def part_sum(joined):
    return jnp.sum(lax.all_to_all(joined, both, 0, 0), axis=0)


def flat_whole(part, devices):
    return lax.all_to_all(jnp.broadcast_to(part[None], (devices,) + part.shape), both, 0, 0)


def flat_split(whole, arrays):
    whole = whole.reshape(-1, lanes)
    sums = []
    start = 0
    for array in arrays:
        count = -(-array.size // lanes)
        flat = whole[start : start + count].reshape(-1)
        sums.append(flat[: array.size].reshape(array.shape))
        start += count
    return sums


def exchange_ring(grads, extra=None):
    groups, frames, width = grads.shape
    size = lax.axis_size("dp")
    if extra is None:
        return lax.all_to_all(grads.reshape(size, groups // size, frames, width), "dp", 0, 0)
    joined = jnp.concatenate([grads.reshape(size, -1, width), extra], axis=1)
    received = lax.all_to_all(joined, "dp", 0, 0)
    count = groups // size * frames
    return received[:, :count].reshape(size, -1, frames, width), jnp.sum(received[:, count:], axis=0)


def sum_section(parts):
    own = lax.axis_index("section")
    core, place = own % 2, own // 2
    pairs = parts.reshape((2, 2) + parts.shape[1:])
    mine = jnp.where(core == 0, pairs[:, 0], pairs[:, 1])
    other = jnp.where(core == 0, pairs[:, 1], pairs[:, 0])
    pair = mine + along_core(other)
    mine = jnp.where(place == 0, pair[0], pair[1])
    other = jnp.where(place == 0, pair[1], pair[0])
    return mine + along_y(other)


def gathers_inputs(frame_rows, columns, devices):
    return frame_rows * devices <= columns


def column_gradients(inputs, pieces, received, grads):
    if received is not None:
        return sum_section(frame_product(inputs, received, pieces))
    groups, frames, width = grads.shape
    flat = grads.swapaxes(0, 1).reshape(frames, groups * width)
    parts = [
        lax.psum_scatter(dot(inputs[which][:, first:last], flat, 0, 0), both, scatter_dimension=1, tiled=True)
        for which, first, last in pieces
    ]
    return jnp.concatenate(parts, axis=0)


def gelu_slope(values):
    return jax.vjp(jax.nn.gelu, values)


def location_map(loc_filters, loc_dense, positions):
    filters, channels, taps = loc_filters.shape
    features = loc_dense.shape[1]
    joined = dot(loc_filters.reshape(filters, channels * taps), loc_dense, 0, 0)
    joined = joined.reshape(channels, taps, features)
    margin = taps // 2
    padded = jnp.pad(joined, ((0, 0), (positions, positions), (0, 0)))
    columns = [
        padded[:, positions + margin - place : 2 * positions + margin - place] for place in range(positions)
    ]
    spread_map = jnp.stack(columns, axis=2).reshape(channels * positions, positions * features)
    return jnp.pad(spread_map, ((0, lanes - channels * positions), (0, 0)))


def location_unmap(grad_map, channels, taps, positions, features):
    grads = grad_map[: channels * positions].reshape(channels, positions, positions, features)
    turned = jnp.flip(grads.swapaxes(1, 2), axis=1)
    padded = jnp.pad(turned, ((0, 0), (0, 0), (0, positions), (0, 0))).reshape(channels, -1, features)
    length = 2 * positions - 1
    skewed = padded[:, : positions * length].reshape(channels, positions, length, features)
    start = positions - 1 - taps // 2
    return jnp.sum(skewed[:, :, start : start + taps], axis=1)


def per_device(
    memory,
    enc_lengths,
    frame_segment,
    mel_target,
    prenet_keep,
    zone_keep,
    pre_first,
    pre_second,
    att_weight,
    att_bias,
    query_weight,
    memory_weight,
    loc_filters,
    loc_dense,
    energy_v,
    dec_weight,
    dec_bias,
    proj_weight,
    proj_bias,
    stop_weight,
    post_first,
    post_mid,
    post_last,
    norm_gain,
    norm_shift,
    last_gain,
    last_shift,
    grad_after,
    grad_stop,
):
    devices = lax.axis_size("dp") * lax.axis_size("section")
    rows, positions, context_width = memory.shape
    frames = frame_segment.shape[1]
    mel = mel_target.shape[2]
    units = att_bias.shape[0] // 4
    prenet_width = pre_first.shape[1]
    features = memory_weight.shape[1]
    lag = frames - span
    frame_rows = frames * rows

    att_all = gather_columns(att_weight)
    dec_all = gather_columns(dec_weight)
    mid_pair = gather_y(post_mid.reshape(-1, post_mid.shape[3]))
    mid_all = section_columns(mid_pair, 3)
    post_split = [split_matrix(weight.reshape(-1, weight.shape[-1])) for weight in [post_first] + mid_all + [post_last]]

    segment = frame_segment.T
    earlier = jnp.concatenate([segment[:1] - 1, segment[:-1]], axis=0)
    resume = (segment == earlier).astype(f32)
    shifted = jnp.concatenate([jnp.zeros_like(mel_target[:, :1]), mel_target[:, :-1]], axis=1)
    frames_in = (shifted.swapaxes(0, 1) * resume[:, :, None]).reshape(frame_rows, mel)
    keep = prenet_keep.transpose(1, 2, 0, 3).astype(f32) * 2.0
    keep_first = keep[:, 0].reshape(frame_rows, prenet_width)
    keep_second = keep[:, 1].reshape(frame_rows, prenet_width)
    gelu_first, first_back = gelu_slope(dot(frames_in, pre_first))
    pre_hidden = gelu_first * keep_first
    gelu_second, second_back = gelu_slope(dot(pre_hidden, pre_second))
    prenet_out = gelu_second * keep_second
    memory_flat = memory.reshape(rows * positions, context_width)
    processed = dot(memory_flat, memory_weight)
    loc_map = location_map(loc_filters, loc_dense, positions)
    zone = zone_keep.transpose(1, 2, 0, 3)

    first_part = segment == 0
    steps = jnp.arange(span)
    never = jnp.ones((span, rows), f32)
    resume_pair = jnp.concatenate([never, resume[lag:]], axis=1)[:, :, None]
    valid_pair = jnp.concatenate([first_part[:span], ~first_part[lag:]], axis=1).astype(f32)[:, :, None]
    encoder_first = jnp.arange(lanes)[None, :] < enc_lengths[:, :1]
    inside = jnp.arange(lanes)[None, :] < positions
    allowed = jnp.concatenate([encoder_first, inside & ~encoder_first], axis=0).astype(f32)
    next_resume = jnp.concatenate([resume[1:], jnp.zeros((1, rows), f32)], axis=0).reshape(frame_rows, 1)

    def to_frames(pairs):
        early = jnp.pad(pairs[:, :rows], ((0, lag), (0, 0), (0, 0)))
        late = jnp.pad(pairs[:, rows:], ((lag, 0), (0, 0), (0, 0)))
        return jnp.where(first_part[:, :, None], early, late).reshape(frame_rows, -1)

    energy_row = energy_v.reshape(1, features)
    processed_wide = processed.reshape(rows, positions * features)
    hidden, cells, contexts, gates, bent, weights, window = attention_forward(
        att_all,
        prenet_out,
        att_bias,
        loc_map,
        processed_wide,
        memory_flat,
        query_weight,
        energy_row,
        zone,
        resume_pair,
        allowed,
        lag,
        mid_pair,
    )
    att_frames = to_frames(hidden)
    context_frames = to_frames(contexts)
    dec_inputs = jnp.concatenate([att_frames, context_frames], axis=1)
    dec_hidden, dec_cells, dec_gates = decoder_forward(
        dec_all, dec_inputs, dec_bias, zone, resume_pair, rows, lag, [part for pair in post_split for part in pair]
    )
    dec_frames = to_frames(dec_hidden)

    prenet_later = jnp.concatenate([prenet_out[rows:], jnp.zeros((rows, prenet_width), f32)], axis=0)
    att_inputs_all = jnp.concatenate([prenet_later, context_frames, att_frames], axis=1)
    dec_earlier = jnp.concatenate([jnp.zeros((rows, units), f32), dec_frames[:-rows]], axis=0)
    dec_earlier = dec_earlier * resume.reshape(frame_rows, 1)
    dec_inputs_all = dec_earlier
    input_width = att_inputs_all.shape[1]
    input_pieces = []
    rings = gathers_inputs(frame_rows, 4 * units, devices)
    if rings:
        att_inputs_all = lax.all_gather(att_inputs_all, "dp", axis=0, tiled=True)
        dec_inputs_all = lax.all_gather(dec_inputs_all, "dp", axis=0, tiled=True)
        input_pieces = [att_inputs_all, dec_inputs_all]

    out_frames = jnp.concatenate([dec_frames, context_frames], axis=1)
    mel_before = dot(out_frames, proj_weight) + proj_bias
    stop_logit = jnp.sum(out_frames * stop_weight, axis=1).reshape(frames, rows).T

    section_size = lax.axis_size("section")
    kernel = post_first.shape[0]
    margin = kernel // 2
    padded = jnp.pad(segment, ((margin, margin), (0, 0)), constant_values=-1)
    same_segment = jnp.stack(
        [padded[offset : offset + frames] == segment for offset in range(kernel)], axis=2
    ).astype(f32)
    same = jnp.pad(same_segment, ((0, 0), (0, 0), (0, 8 - kernel))).reshape(frame_rows, 8)
    same_all = gather_section(same)
    frame_count = frame_rows * devices
    gains = [norm_gain[layer : layer + 1] for layer in range(4)] + [last_gain.reshape(1, mel)]
    shifts = [norm_shift[layer : layer + 1] for layer in range(4)] + [last_shift.reshape(1, mel)]
    widths = [post_first.shape[2]] * 4 + [mel]
    grad_after_frames = grad_after.swapaxes(0, 1).reshape(frame_rows, mel)
    conv, copies = post_call(
        functools.partial(post_first_kernel, rows),
        [(frame_rows, widths[0]), (devices, 8, lanes)],
        "post_first",
        (mel_before, same, *post_split[0]),
    )
    scaled, inverse, active, inputs_all = [], [], [], []
    inputs_all.append(gather_section(jnp.pad(mel_before, ((0, 0), (0, lanes - mel)))))
    for layer in range(4):
        scaled_now, active_now, inverse_now, conv, copies = post_call(
            functools.partial(post_next_kernel, rows, frame_count),
            [
                (frame_rows, widths[layer]),
                (frame_rows, widths[layer]),
                (1, widths[layer]),
                (frame_rows, widths[layer + 1]),
                (devices, 8, lanes),
            ],
            "post_next",
            (conv, share_sums(copies), gains[layer], shifts[layer], same, *post_split[layer + 1])
            + ((grad_after_frames,) if layer == 3 else ()),
        )
        scaled.append(scaled_now)
        active.append(active_now)
        inverse.append(inverse_now)
        inputs_all.append(gather_section(active_now))
    mel_after, grad_conv, packed, upstream, copies = post_call(
        functools.partial(post_turn_kernel, rows, frame_count),
        [(frame_rows, mel), (frame_rows, lanes), (8, lanes), (frame_rows, widths[3]), (devices, 8, lanes)],
        "post_turn",
        (
            grad_after_frames,
            conv,
            share_sums(copies),
            mel_before,
            gains[4],
            shifts[4],
            same,
            *post_split[4],
            active[3],
            scaled[3],
        ),
    )
    weight_grads = [None] * 5
    gain_grads = [None] * 5
    shift_grads = [None] * 5
    shift_grads[4], gain_grads[4] = [row.reshape(-1) for row in unpack_sums(packed, mel)]
    weight_grads[4] = tap_gradient(
        own_columns(inputs_all[4], inputs_all[4].shape[2] // section_size),
        gather_section(grad_conv),
        same_all,
        kernel,
        rows,
    )
    for layer in reversed(range(4)):
        below = (active[layer - 1], scaled[layer - 1]) if layer else ()
        awaited = (weight_grads[layer + 2],) if layer < 3 else ()
        outs = [(frame_rows, widths[layer]), (8, lanes), (frame_rows, widths[layer - 1] if layer else mel)]
        if layer:
            outs.append((devices, 8, lanes))
        results = post_call(
            functools.partial(post_back_kernel, rows, frame_count, layer > 0, len(awaited)),
            outs,
            "post_back",
            (
                upstream,
                scaled[layer],
                share_sums(copies),
                inverse[layer],
                gains[layer],
                same,
                *post_split[layer],
                *below,
            ),
            awaited,
        )
        grad_conv, packed, upstream = results[:3]
        if layer:
            copies = results[3]
        shift_grads[layer], gain_grads[layer] = [row.reshape(-1) for row in unpack_sums(packed, widths[layer])]
        weight_grads[layer] = tap_gradient(
            inputs_all[layer],
            own_columns(gather_section(grad_conv), grad_conv.shape[1] // section_size),
            same_all,
            kernel,
            rows,
        )

    grad_mel = grad_after_frames + upstream
    grad_stop_frames = grad_stop.T.reshape(frame_rows, 1)
    grad_out = dot(grad_mel, proj_weight, 1, 1) + grad_stop_frames * stop_weight
    mel_grads = jnp.pad(
        jnp.concatenate([grad_mel, grad_stop_frames], axis=1), ((0, 0), (0, lanes - mel - 1))
    )
    mel_pair = gather_y(mel_grads)
    mel_grads_all = gather_core(mel_pair).reshape(-1, lanes)
    outs_own = own_columns(gather_section(out_frames), out_frames.shape[1] // section_size)
    outs_own = outs_own.reshape(mel_grads_all.shape[0], -1)
    g_proj_part = dot(outs_own, mel_grads_all, 0, 0)
    group_grads, group_token = join_rows(
        [grad.reshape(-1, lanes) for grad in weight_grads + [g_proj_part]]
        + [jnp.pad(jnp.sum(mel_grads_all, axis=0, keepdims=True), ((0, 7), (0, 0)))],
        input_pieces,
    )
    group_sums = lax.psum(group_grads, "dp")
    dec_sums, grad_dec_inputs = decoder_backward(
        dec_all,
        grad_out[:, :units],
        dec_gates,
        dec_cells,
        zone,
        resume_pair,
        valid_pair,
        rows,
        lag,
        [group_token],
    )
    g_dec_bias = jnp.sum(dec_sums, axis=1).reshape(-1)
    grad_context = grad_out[:, units:] + grad_dec_inputs[:, units:]
    dec_columns = exchange_ring(dec_sums) if rings else None
    (
        att_sums,
        g_att_bias,
        grad_prenet,
        grad_query,
        grad_processed,
        grad_memory,
        grad_loc,
        grad_energy,
    ) = attention_backward(
        att_all,
        grad_dec_inputs[:, :units],
        grad_context,
        gates,
        cells,
        bent,
        weights,
        window,
        loc_map,
        memory_flat,
        query_weight,
        energy_row,
        zone,
        resume_pair,
        valid_pair,
        next_resume,
        rows,
        positions,
        prenet_width,
        lag,
        (group_token,),
    )

    grad_processed = grad_processed.reshape(rows * positions, features)
    grad_memory = grad_memory + dot(grad_processed, memory_weight, 1, 1)
    g_memory_weight = dot(memory_flat, grad_processed, 0, 0)
    g_query_weight = dot(att_frames, grad_query, 0, 0)
    (grad_second,) = second_back(grad_prenet * keep_second)
    g_pre_second = dot(pre_hidden, grad_second, 0, 0)
    (grad_first,) = first_back(dot(grad_second, pre_second, 1, 1) * keep_first)
    g_pre_first = dot(frames_in, grad_first, 0, 0)
    filters, channels, taps = loc_filters.shape
    grad_joined = location_unmap(grad_loc, channels, taps, positions, features)
    late_grads = (
        g_pre_first,
        g_pre_second,
        g_att_bias,
        g_query_weight,
        g_memory_weight,
        grad_joined,
        jnp.sum(grad_energy, axis=0),
        g_dec_bias,
    )
    context_end = prenet_width + context_width
    dec_part = column_gradients(
        [att_inputs_all, dec_inputs_all],
        ((0, context_end, input_width), (0, prenet_width, context_end), (1, 0, units)),
        dec_columns,
        dec_sums,
    )
    late_joined = flat_join(late_grads, devices)
    if rings:
        late_ring = sum_section(late_joined.reshape((-1, 4) + late_joined.shape[1:]).swapaxes(0, 1))
        late_ring = late_ring + 0.0 * (dec_columns[0, 0, 0, 0] + group_sums[0, 0])
        att_columns, late_part = exchange_ring(att_sums, late_ring)
    else:
        att_columns = None
        late_part = part_sum(late_joined)
    att_part = column_gradients([att_inputs_all], ((0, 0, input_width),), att_columns, att_sums)

    late_sums = flat_split(flat_whole(late_part, devices), late_grads)
    grad_joined = late_sums[5].reshape(channels * taps, features)
    g_loc_filters = dot(loc_dense, grad_joined, 1, 1).reshape(loc_filters.shape)
    g_loc_dense = dot(loc_filters.reshape(filters, channels * taps), grad_joined)

    first_rows = kernel * lanes
    mid_end = first_rows + post_mid.size // lanes
    proj_start = mid_end + first_rows
    proj_end = proj_start + out_frames.shape[1] // section_size
    mid_part = group_sums[first_rows:mid_end].reshape(post_mid.shape)
    own = lax.axis_index("section")
    shared = jnp.concatenate([group_sums[:first_rows], group_sums[mid_end:proj_end]], axis=0)
    shared_all = section_order(gather_section(shared), own)
    g_post_first = jnp.concatenate(
        [piece[:first_rows].reshape(kernel, lanes, lanes)[:, :mel] for piece in shared_all], axis=2
    )
    g_post_last = jnp.concatenate(
        [piece[first_rows : 2 * first_rows].reshape(kernel, lanes, lanes)[:, :, :mel] for piece in shared_all], axis=1
    )
    g_proj = jnp.concatenate([piece[2 * first_rows :] for piece in shared_all], axis=0)
    g_proj_bias = group_sums[proj_end, :mel]
    return (
        mel_after.reshape(frames, rows, mel).swapaxes(0, 1),
        stop_logit,
        grad_memory.reshape(memory.shape),
        late_sums[0],
        late_sums[1],
        att_part,
        late_sums[2].reshape(-1),
        late_sums[3],
        late_sums[4],
        g_loc_filters,
        g_loc_dense,
        late_sums[6],
        dec_part,
        late_sums[7],
        g_proj[:, :mel],
        g_proj_bias,
        g_proj[:, mel],
        g_post_first,
        mid_part,
        g_post_last,
        jnp.stack(gain_grads[:4]),
        jnp.stack(shift_grads[:4]),
        gain_grads[4],
        shift_grads[4],
    )


def solution(mesh):
    rows_only = P(both)
    columns_only = P(None, both)
    mid_spec = P(None, None, None, "section")
    placed = (
        (rows_only,) * 6
        + (P(), P(), columns_only)
        + (P(),) * 6
        + (columns_only,)
        + (P(),) * 5
        + (mid_spec,)
        + (P(),) * 5
        + (rows_only, rows_only)
    )
    given = (
        (rows_only,) * 3
        + (P(), P(), columns_only)
        + (P(),) * 6
        + (columns_only,)
        + (P(),) * 5
        + (mid_spec,)
        + (P(),) * 5
    )
    return jax.shard_map(per_device, mesh=mesh, in_specs=placed, out_specs=given, check_vma=False)
```

profile of v0, /device:TPU:0, one launch (start us, length us, event | category | flops | bytes accessed | tf_op | source)
XLA Modules:
  0.0 1045.5 jit_solution(13457780008998076544)
XLA Ops:
  8.8 3.0 collective-permute-start
  17.7 4.1 copy.269
  29.8 95.9 %collective-permute-done = f32[7680,128]{1,0:T(8,128)} collective-permute-done((f32[7680,128]{1,0:T(8,128)}, f32[7680,128]{1,0:T(8,128)}, u32[]{:S(2)}, u32[]{:S(2)}) %collective-permute-start) | collective-permute-done | bytes 3932192 | tf_op jit(solution)/shard_map/ppermute | solution.py:1262
  125.6 5.8 pad_maximum_fusion.1.awaited
  131.5 71.6 %all-gather.13.cloned.1.call-done = f32[57344,128]{1,0:T(8,128)} async-done(((f32[1792,128]{1,0:T(8,128)}), f32[57344,128]{1,0:T(8,128)}) %all-gather.13.cloned.1.call-update) | async-done | bytes 29360144 | tf_op jit(solution)/shard_map/all_gather | solution.py:1251
  203.0 49.6 %attention_forward.1 = (f32[6,32,1024]{2,1,0:T(8,128)}, f32[6,32,1024]{2,1,0:T(8,128)}, f32[6,32,512]{2,1,0:T(8,128)}, f32[6,32,4096]{2,1,0:T(8,128)}, f32[6,32,...) custom-call(f32[32,1792,128]{2,1,0:T(8,128)} %bitcast.427, f32[128,256]{1,0:T(8,128)} %copy-done.56, ...), custom_call_target="tpu_custom_call" | custom-call | flops 45097156608 | bytes 29360128 | tf_op jit(solution)/shard_map/attention_forward/pallas_call | solution.py:939
  263.1 10.9 %pad_maximum_fusion = f32[4,7680,128]{2,1,0:T(8,128)} fusion(f32[2,7680,128]{2,1,0:T(8,128)} %collective-permute-done.1, f32[1,7680,128]{2,1,0:T(8,128)} %bitcast.52, f32[1,7680,128]{2,1,0:T(8,128)} %bitcast.438), kind=kLoop, calls=%fused_computation | loop fusion | flops 7864320 | bytes 31457280 | tf_op jit(solution)/shard_map/concatenate | solution.py:1270
  274.0 11.5 %fusion.115 = (f32[4,2560,128]{2,1,0:T(8,128)}, f32[4,2560,128]{2,1,0:T(8,128)}, f32[4,2560,128]{2,1,0:T(8,128)}) fusion(f32[4,7680,128]{2,1,0:T(8,128)} %pad_maximum_fusion), kind=kLoop, calls=%fused_computation.330 | loop fusion | bytes 31457280 | tf_op jit(solution)/shard_map/slice | solution.py:1292
  285.5 6.8 dynamic-slice_bitcast_fusion.3
  294.9 5.2 split_matrix.8
  300.1 5.2 pad_maximum_fusion.3.values_ref
  305.3 5.5 split_matrix.7
  310.8 2.8 dynamic-slice_bitcast_fusion.11
  313.7 2.6 pad_maximum_fusion.2.values_ref
  316.3 7.3 split_matrix.6
  324.6 115.8 %all-gather.11.cloned.1.call-done = f32[81920,128]{1,0:T(8,128)} async-done(((f32[2560,128]{1,0:T(8,128)}), f32[81920,128]{1,0:T(8,128)}) %all-gather.11.cloned.1.call-update) | async-done | bytes 41943056 | tf_op jit(solution)/shard_map/all_gather | solution.py:1251
  440.4 37.4 %decoder_forward.1 = (f32[6,32,1024]{2,1,0:T(8,128)}, f32[6,32,1024]{2,1,0:T(8,128)}, f32[6,32,4096]{2,1,0:T(8,128)}) custom-call(f32[32,2560,128]{2,1,0:T(8,128)} %bitcast.540, f32[128,1536]{1,0:T(8,128)} %pad_maximum_fusion.19.frames_ref, f32[8,1,512]{2,1,0:T(1,128)} %bitcast.547, s32[8,4,16,1024]{3,2,1,0:T(8,128)} %bitcast.431, ...), custom_call_target="tpu_custom_call" | custom-call | flops 32212254720 | bytes 41943040 | tf_op jit(solution)/shard_map/decoder_forward/pallas_call | solution.py:1015
  481.9 2.7 post_first.1
  484.6 3.2 all-to-all-start
  489.0 10.2 all-to-all-done.sums_ref
  499.9 4.8 post_next.4
  509.0 7.8 all-to-all-done.1.sums_ref
  517.4 4.7 post_next.5
  522.2 4.8 all-to-all-start.2
  533.6 4.9 all-to-all-done.2.sums_ref
  539.2 4.8 post_next.6
  544.0 3.3 all-to-all-start.3
  547.3 5.2 collective-permute-done.16
  559.4 2.9 post_next.7
  562.3 6.0 all-to-all-start.4
  576.7 3.1 post_turn.1
  579.8 4.9 all-to-all-start.5
  595.8 5.3 post_back.4
  613.4 2.7 tap_gradient.5.refs_2_
  616.1 5.2 all-to-all-done.6.sums_ref
  622.0 5.5 post_back.5
  633.4 2.8 all-to-all-start.7
  639.1 4.2 tap_gradient.6.refs_2_
  645.1 5.3 post_back.6
  650.4 4.7 all-to-all-start.8
  657.0 3.5 pad_maximum_fusion.6
  662.4 4.2 tap_gradient.7.refs_0_
  667.3 2.7 post_back.7
  678.3 3.0 collective-permute-done.18
  681.5 3.3 convolution_bitcast_fusion.1.refs_5_
  686.6 4.2 tap_gradient.9
  692.7 2.7 tap_gradient.8
  695.5 4.8 join_rows.1
  700.3 52.9 %decoder_backward.1 = (f32[32,128,128]{2,1,0:T(8,128)}, f32[128,1536]{1,0:T(8,128)}) custom-call(f32[32,2560,128]{2,1,0:T(8,128)} %bitcast.541, f32[32,2560,128]{2,1,0:T(8,128)} %bitcast.542, f32[32,2560,128]{2,1,0:T(8,128)} %bitcast.543, f32[32,2560,128]{2,1,0:T(8,128)} %bitcast.544, f32[32,2560,128]{2,1,0:T(8,128)} %bitcast.545, ...), custom_call_target="tpu_custom_call" | custom-call | flops 257698037760 | bytes 41943040 | tf_op jit(solution)/shard_map/decoder_backward/pallas_call | solution.py:1084
  753.2 6.5 all-to-all-start.9
  763.7 70.1 %attention_backward.1 = (f32[32,128,128]{2,1,0:T(8,128)}, f32[1,4096]{1,0:T(1,128)}, f32[128,256]{1,0:T(8,128)}, f32[128,128]{1,0:T(8,128)}, f32[16,4096]{1,0:T(...) custom-call(f32[32,1792,128]{2,1,0:T(8,128)} %bitcast.428, ...), custom_call_target="tpu_custom_call" | custom-call | flops 16777216 | bytes 65536 | tf_op jit(solution)/shard_map/attention_backward/pallas_call | solution.py:1169
  850.7 15.6 %frame_product.3 = f32[4,2560,128]{2,1,0:T(8,128)} custom-call(f32[1024,1792]{1,0:T(8,128)} %all-gather.7.cloned.1.call-done.refs_7_.refs_0_, f32[1024,1024]{1,0:T(8,128)} %all-gather.9.cloned.1.call-done.refs_8_.refs_1_, f32[8,4,128,128]{3,2,1,0:T(8,128)} %all-to-all-done.9.refs_2_), custom_call_target="tpu_custom_call" | custom-call | tf_op jit(solution)/shard_map/frame_product/pallas_call | solution.py:857
  866.2 4.4 select_bitcast_fusion
  871.8 26.6 %all-reduce.22.cloned.1.call-done = f32[9352,128]{1,0:T(8,128)} async-done(((f32[9352,128]{1,0:T(8,128)}), f32[9352,128]{1,0:T(8,128)}) %all-reduce.22.cloned.1.call-update) | async-done | bytes 4788240 | tf_op jit(solution)/shard_map/psum | solution.py:1642
  900.9 3.3 pad_maximum_fusion.7
  904.2 4.0 all-to-all-start.10
  914.9 16.3 %collective-permute-done.34 = f32[1664,128]{1,0:T(8,128)S(1)} collective-permute-done((f32[1664,128]{1,0:T(8,128)S(1)}, f32[1664,128]{1,0:T(8,128)S(1)}, u32[]{:S(2)}, u32[]{:S(2)}) %collective-permute-start.34) | collective-permute-done | bytes 852000 | tf_op jit(solution)/shard_map/ppermute | solution.py:1262
  932.7 4.4 slice.834
  945.6 18.0 %all-to-all-done.10 = f32[8,592,128]{2,1,0:T(8,128)S(1)} async-done(((f32[8,592,128]{2,1,0:T(8,128)}), f32[8,592,128]{2,1,0:T(8,128)S(1)}, u32[]{:S(2)}, u32[]{:S(2)}) %all-to-all-start.10) | async-done | bytes 2424864 | tf_op jit(solution)/shard_map/all_to_all | solution.py:1342
  966.5 11.8 %frame_product.2 = f32[4,1792,128]{2,1,0:T(8,128)} custom-call(f32[1024,1792]{1,0:T(8,128)} %all-gather.7.cloned.1.call-done.refs_7_.refs_0_, f32[8,4,128,128]{3,2,1,0:T(8,128)} %bitcast.449), custom_call_target="tpu_custom_call" | custom-call | tf_op jit(solution)/shard_map/frame_product/pallas_call | solution.py:857
  978.3 3.6 select_bitcast_fusion.1
  989.1 3.8 all-to-all-start.11
  1000.5 2.7 bitcast_add_fusion.2
  1006.9 17.9 %all-to-all-done.11 = f32[32,80,128]{2,1,0:T(8,128)} async-done(((f32[32,80,128]{2,1,0:T(8,128)}), f32[32,80,128]{2,1,0:T(8,128)}, u32[]{:S(2)}, u32[]{:S(2)}) %all-to-all-start.11) | async-done | bytes 1310752 | tf_op jit(solution)/shard_map/all_to_all | solution.py:1321
  (485 shorter events, 187.8 us)
Async XLA Ops:
  7.2 473.6 %copy-start = (f32[1536,80]{0,1:T(8,128)S(1)}, f32[1536,80]{0,1:T(8,128)}, u32[]{:S(2)}) copy-start(f32[1536,80]{0,1:T(8,128)} %param.46) | copy-start | bytes 1474564
  7.2 195.8 %all-gather.13.cloned.1.call-start = ((), (), s32[]{:S(2)}) async-start(), calls=%async_computation.16 | async-start | bytes 30277632 | tf_op jit(solution)/shard_map/all_gather | solution.py:1251
  8.0 432.4 %all-gather.11.cloned.1.call-start = ((), (), s32[]{:S(2)}) async-start(), calls=%async_computation.15 | async-start | bytes 43253760 | tf_op jit(solution)/shard_map/all_gather | solution.py:1251
  8.7 686.8 %all-gather.7.cloned.1.call-start = ((), (), s32[]{:S(2)}) async-start(), calls=%async_computation.12 | async-start | bytes 8257536 | tf_op jit(solution)/shard_map/all_gather | solution.py:1516
  8.8 116.9 %collective-permute-start = (f32[7680,128]{1,0:T(8,128)}, f32[7680,128]{1,0:T(8,128)}, u32[]{:S(2)}, u32[]{:S(2)}) collective-permute-start(f32[7680,128]{1,0:T(8,128)} %bitcast.437), channel_id=1, source_target_pairs={{0,2},{1,3},{2,0},{3,1},{4,6},{5,7},{6,4},{7,5},{8,10},{9,11},{10,... | collective-permute-start | bytes 11796488 | tf_op jit(solution)/shard_map/ppermute | solution.py:1262
  14.6 242.3 %copy-start.67 = (f32[8,16]{1,0:T(8,128)}, f32[8,16]{1,0:T(8,128)S(1)}, u32[]{:S(2)}) copy-start(f32[8,16]{1,0:T(8,128)S(1)} %get-tuple-element.383) | copy-start | bytes 1540
  25.8 99.9 %copy-start.5 = (f32[3,5,512,128]{3,2,1,0:T(8,128)S(1)}, f32[3,5,512,128]{3,2,1,0:T(8,128)}, u32[]{:S(2)}) copy-start(f32[3,5,512,128]{3,2,1,0:T(8,128)} %param.50) | copy-start | bytes 11796484
  26.7 104.8 %copy-start.28 = (f32[128,256]{1,0:T(8,128)}, f32[128,256]{1,0:T(8,128)S(1)}, u32[]{:S(2)}) copy-start(f32[128,256]{1,0:T(8,128)S(1)} %get-tuple-element.388) | copy-start | bytes 393220
  27.6 103.9 %copy-start.56 = (f32[128,256]{1,0:T(8,128)}, f32[128,256]{1,0:T(8,128)S(1)}, u32[]{:S(2)}) copy-start(f32[128,256]{1,0:T(8,128)S(1)} %get-tuple-element.390.prenet_ref) | copy-start | bytes 393220
  131.5 131.7 %collective-permute-start.1 = (f32[2,7680,128]{2,1,0:T(8,128)}, f32[2,7680,128]{2,1,0:T(8,128)}, u32[]{:S(2)}, u32[]{:S(2)}) collective-permute-start(f32[2,7680,128]{2,1,0:T(8,128)} %pad_maximum_fusion.1.awaited), channel_id=1, source_target_pairs={{0,1},{1,0},{2,3},{3,2},{4,5},{5,4},{6,7},{7,6},{8,9},{9,8},{10,11... | collective-permute-start | bytes 23592968 | tf_op jit(solution)/shard_map/ppermute | solution.py:1258
  253.9 226.9 %copy-start.14 = (f32[8,16,512]{2,1,0:T(8,128)}, f32[8,16,512]{2,1,0:T(8,128)S(1)}, u32[]{:S(2)}) copy-start(f32[8,16,512]{2,1,0:T(8,128)S(1)} %pad_select_fusion.2) | copy-start | bytes 786436
  255.3 68.3 %copy-start.10 = (f32[8,16,1024]{2,1,0:T(8,128)}, f32[8,16,1024]{2,1,0:T(8,128)S(1)}, u32[]{:S(2)}) copy-start(f32[8,16,1024]{2,1,0:T(8,128)S(1)} %pad_select_fusion.1) | copy-start | bytes 1572868
  256.3 439.2 %all-gather.9.cloned.1.call-start = ((), (), s32[]{:S(2)}) async-start(), calls=%async_computation.13 | async-start | bytes 4718592 | tf_op jit(solution)/shard_map/all_gather | solution.py:1517
  484.6 14.6 %all-to-all-start = ((f32[32,8,128]{2,1,0:T(8,128)}), f32[32,8,128]{2,1,0:T(8,128)S(1)}, u32[]{:S(2)}, u32[]{:S(2)}) async-start(f32[32,8,128]{2,1,0:T(8,128)} %get-tuple-element.112), calls=%async_computation | async-start | bytes 262144 | tf_op jit(solution)/shard_map/all_to_all | solution.py:784
  504.7 12.1 %all-to-all-start.1 = ((f32[32,8,128]{2,1,0:T(8,128)}), f32[32,8,128]{2,1,0:T(8,128)S(1)}, u32[]{:S(2)}, u32[]{:S(2)}) async-start(f32[32,8,128]{2,1,0:T(8,128)} %get-tuple-element.114), calls=%async_computation.1 | async-start | bytes 262144 | tf_op jit(solution)/shard_map/all_to_all | solution.py:784
  507.2 24.9 %collective-permute-start.6 = (f32[128,8]{1,0:T(8,128)}, f32[128,8]{1,0:T(8,128)S(1)}, u32[]{:S(2)}, u32[]{:S(2)}) collective-permute-start(f32[128,8]{1,0:T(8,128)} %bitcast.75.same_ref), channel_id=1, source_target_pairs={{0,2},{1,3},{2,0},{3,1},{4,6},{5,7},{6,4},{7,5},{8,10},{9,11},{10,... | collective-permute-start | bytes 12296 | tf_op jit(solution)/shard_map/ppermute | solution.py:1262
  522.2 16.4 %all-to-all-start.2 = ((f32[32,8,128]{2,1,0:T(8,128)}), f32[32,8,128]{2,1,0:T(8,128)S(1)}, u32[]{:S(2)}, u32[]{:S(2)}) async-start(f32[32,8,128]{2,1,0:T(8,128)} %get-tuple-element.116), calls=%async_computation.2 | async-start | bytes 262144 | tf_op jit(solution)/shard_map/all_to_all | solution.py:784
  530.1 54.6 %collective-permute-start.24 = (f32[128,1536]{1,0:T(8,128)}, f32[128,1536]{1,0:T(8,128)}, u32[]{:S(2)}, u32[]{:S(2)}) collective-permute-start(f32[128,1536]{1,0:T(8,128)} %get-tuple-element.329), channel_id=1, source_target_pairs={{0,2},{1,3},{2,0},{3,1},{4,6},{5,7},{6,4},{7,5},{8,10},{9,11},{10,... | collective-permute-start | bytes 2359304 | tf_op jit(solution)/shard_map/ppermute | solution.py:1262
  531.9 20.7 %collective-permute-start.16 = (f32[128,128]{1,0:T(8,128)}, f32[128,128]{1,0:T(8,128)S(1)}, u32[]{:S(2)}, u32[]{:S(2)}) collective-permute-start(f32[128,128]{1,0:T(8,128)} %get-tuple-element.339), channel_id=1, source_target_pairs={{0,2},{1,3},{2,0},{3,1},{4,6},{5,7},{6,4},{7,5},{8,10},{9,11},{10,... | collective-permute-start | bytes 196616 | tf_op jit(solution)/shard_map/ppermute | solution.py:1262
  533.6 24.1 %collective-permute-start.7 = (f32[2,128,8]{2,1,0:T(8,128)}, f32[2,128,8]{2,1,0:T(8,128)}, u32[]{:S(2)}, u32[]{:S(2)}) collective-permute-start(f32[2,128,8]{2,1,0:T(8,128)} %pad_maximum_fusion.36), channel_id=1, source_target_pairs={{0,1},{1,0},{2,3},{3,2},{4,5},{5,4},{6,7},{7,6},{8,9},{9,8},{10,11... | collective-permute-start | bytes 24584 | tf_op jit(solution)/shard_map/ppermute | solution.py:1258
  539.2 15.8 %copy-start.77 = (f32[16,8]{0,1:T(8,128)S(1)}, f32[16,8]{0,1:T(8,128)}, u32[]{:S(2)}) copy-start(f32[16,8]{0,1:T(8,128)} %param.57) | copy-start | bytes 1540
  539.2 18.2 %copy-start.20 = (f32[128,512]{1,0:T(8,128)S(1)}, f32[128,512]{1,0:T(8,128)}, u32[]{:S(2)}) copy-start(f32[128,512]{1,0:T(8,128)} %get-tuple-element.132.refs_0_) | copy-start | bytes 786436
  544.0 15.4 %all-to-all-start.3 = ((f32[32,8,128]{2,1,0:T(8,128)}), f32[32,8,128]{2,1,0:T(8,128)}, u32[]{:S(2)}, u32[]{:S(2)}) async-start(f32[32,8,128]{2,1,0:T(8,128)} %get-tuple-element.118), calls=%async_computation.3 | async-start | bytes 262144 | tf_op jit(solution)/shard_map/all_to_all | solution.py:784
  553.2 15.2 %collective-permute-start.17 = (f32[2,128,128]{2,1,0:T(8,128)}, f32[2,128,128]{2,1,0:T(8,128)}, u32[]{:S(2)}, u32[]{:S(2)}) collective-permute-start(f32[2,128,128]{2,1,0:T(8,128)} %pad_maximum_fusion.37), channel_id=1, source_target_pairs={{0,1},{1,0},{2,3},{3,2},{4,5},{5,4},{6,7},{7,6},{8,9},{9,8},{10,11... | collective-permute-start | bytes 393224 | tf_op jit(solution)/shard_map/ppermute | solution.py:1258
  553.2 16.8 %collective-permute-start.20 = (f32[128,512]{1,0:T(8,128)S(1)}, f32[128,512]{1,0:T(8,128)}, u32[]{:S(2)}, u32[]{:S(2)}) collective-permute-start(f32[128,512]{1,0:T(8,128)S(1)} %copy-done.19), channel_id=1, source_target_pairs={{0,2},{1,3},{2,0},{3,1},{4,6},{5,7},{6,4},{7,5},{8,10},{9,11},{10,... | collective-permute-start | bytes 786440 | tf_op jit(solution)/shard_map/ppermute | solution.py:1262
  557.5 16.2 %collective-permute-start.12 = (f32[128,512]{1,0:T(8,128)S(1)}, f32[128,512]{1,0:T(8,128)}, u32[]{:S(2)}, u32[]{:S(2)}) collective-permute-start(f32[128,512]{1,0:T(8,128)S(1)} %copy-done.20), channel_id=1, source_target_pairs={{0,2},{1,3},{2,0},{3,1},{4,6},{5,7},{6,4},{7,5},{8,10},{9,11},{10,... | collective-permute-start | bytes 786440 | tf_op jit(solution)/shard_map/ppermute | solution.py:1262
  562.3 14.3 %all-to-all-start.4 = ((f32[32,8,128]{2,1,0:T(8,128)}), f32[32,8,128]{2,1,0:T(8,128)}, u32[]{:S(2)}, u32[]{:S(2)}) async-start(f32[32,8,128]{2,1,0:T(8,128)} %get-tuple-element.120), calls=%async_computation.4 | async-start | bytes 262144 | tf_op jit(solution)/shard_map/all_to_all | solution.py:784
  571.8 31.5 %collective-permute-start.21 = (f32[2,128,512]{2,1,0:T(8,128)}, f32[2,128,512]{2,1,0:T(8,128)}, u32[]{:S(2)}, u32[]{:S(2)}) collective-permute-start(f32[2,128,512]{2,1,0:T(8,128)} %pad_maximum_fusion.30), channel_id=1, source_target_pairs={{0,1},{1,0},{2,3},{3,2},{4,5},{5,4},{6,7},{7,6},{8,9},{9,8},{10,11... | collective-permute-start | bytes 1572872 | tf_op jit(solution)/shard_map/ppermute | solution.py:1258
  572.0 18.9 %collective-permute-start.8 = (f32[128,512]{1,0:T(8,128)}, f32[128,512]{1,0:T(8,128)}, u32[]{:S(2)}, u32[]{:S(2)}) collective-permute-start(f32[128,512]{1,0:T(8,128)} %get-tuple-element.127.refs_0_), channel_id=1, source_target_pairs={{0,2},{1,3},{2,0},{3,1},{4,6},{5,7},{6,4},{7,5},{8,10},{9,11},{10,... | collective-permute-start | bytes 786440 | tf_op jit(solution)/shard_map/ppermute | solution.py:1262
  575.4 53.7 %collective-permute-start.13 = (f32[2,128,512]{2,1,0:T(8,128)}, f32[2,128,512]{2,1,0:T(8,128)}, u32[]{:S(2)}, u32[]{:S(2)}) collective-permute-start(f32[2,128,512]{2,1,0:T(8,128)} %pad_maximum_fusion.27), channel_id=1, source_target_pairs={{0,1},{1,0},{2,3},{3,2},{4,5},{5,4},{6,7},{7,6},{8,9},{9,8},{10,11... | collective-permute-start | bytes 1572872 | tf_op jit(solution)/shard_map/ppermute | solution.py:1258
  575.5 11.9 %collective-permute-start.2 = (f32[128,512]{1,0:T(8,128)}, f32[128,512]{1,0:T(8,128)}, u32[]{:S(2)}, u32[]{:S(2)}) collective-permute-start(f32[128,512]{1,0:T(8,128)} %get-tuple-element.121.active_ref), channel_id=1, source_target_pairs={{0,2},{1,3},{2,0},{3,1},{4,6},{5,7},{6,4},{7,5},{8,10},{9,11},{10,... | collective-permute-start | bytes 786440 | tf_op jit(solution)/shard_map/ppermute | solution.py:1262
  579.8 15.4 %all-to-all-start.5 = ((f32[32,8,128]{2,1,0:T(8,128)}), f32[32,8,128]{2,1,0:T(8,128)S(1)}, u32[]{:S(2)}, u32[]{:S(2)}) async-start(f32[32,8,128]{2,1,0:T(8,128)} %get-tuple-element.125), calls=%async_computation.5 | async-start | bytes 262144 | tf_op jit(solution)/shard_map/all_to_all | solution.py:784
  587.1 69.9 %collective-permute-start.25 = (f32[2,128,1536]{2,1,0:T(8,128)}, f32[2,128,1536]{2,1,0:T(8,128)}, u32[]{:S(2)}, u32[]{:S(2)}) collective-permute-start(f32[2,128,1536]{2,1,0:T(8,128)} %pad_maximum_fusion.9), channel_id=1, source_target_pairs={{0,1},{1,0},{2,3},{3,2},{4,5},{5,4},{6,7},{7,6},{8,9},{9,8},{10,11... | collective-permute-start | bytes 4718600 | tf_op jit(solution)/shard_map/ppermute | solution.py:1258
  587.4 13.8 %collective-permute-start.4 = (f32[128,128]{1,0:T(8,128)}, f32[128,128]{1,0:T(8,128)}, u32[]{:S(2)}, u32[]{:S(2)}) collective-permute-start(f32[128,128]{1,0:T(8,128)} %get-tuple-element.134), channel_id=1, source_target_pairs={{0,2},{1,3},{2,0},{3,1},{4,6},{5,7},{6,4},{7,5},{8,10},{9,11},{10,... | collective-permute-start | bytes 196616 | tf_op jit(solution)/shard_map/ppermute | solution.py:1262
  590.9 20.5 %collective-permute-start.3 = (f32[2,128,512]{2,1,0:T(8,128)}, f32[2,128,512]{2,1,0:T(8,128)}, u32[]{:S(2)}, u32[]{:S(2)}) collective-permute-start(f32[2,128,512]{2,1,0:T(8,128)} %pad_maximum_fusion.24), channel_id=1, source_target_pairs={{0,1},{1,0},{2,3},{3,2},{4,5},{5,4},{6,7},{7,6},{8,9},{9,8},{10,11... | collective-permute-start | bytes 1572872 | tf_op jit(solution)/shard_map/ppermute | solution.py:1258
  601.1 9.1 collective-permute-start.10
  603.3 2.5 collective-permute-start.5
  605.8 25.5 %collective-permute-start.9 = (f32[2,128,512]{2,1,0:T(8,128)}, f32[2,128,512]{2,1,0:T(8,128)}, u32[]{:S(2)}, u32[]{:S(2)}) collective-permute-start(f32[2,128,512]{2,1,0:T(8,128)} %pad_maximum_fusion.25), channel_id=1, source_target_pairs={{0,1},{1,0},{2,3},{3,2},{4,5},{5,4},{6,7},{7,6},{8,9},{9,8},{10,11... | collective-permute-start | bytes 1572872 | tf_op jit(solution)/shard_map/ppermute | solution.py:1258
  607.7 13.7 %all-to-all-start.6 = ((f32[32,8,128]{2,1,0:T(8,128)}), f32[32,8,128]{2,1,0:T(8,128)S(1)}, u32[]{:S(2)}, u32[]{:S(2)}) async-start(f32[32,8,128]{2,1,0:T(8,128)} %get-tuple-element.130), calls=%async_computation.6 | async-start | bytes 262144 | tf_op jit(solution)/shard_map/all_to_all | solution.py:784
  611.1 26.1 %collective-permute-start.11 = (f32[2,128,512]{2,1,0:T(8,128)}, f32[2,128,512]{2,1,0:T(8,128)}, u32[]{:S(2)}, u32[]{:S(2)}) collective-permute-start(f32[2,128,512]{2,1,0:T(8,128)} %pad_maximum_fusion.26), channel_id=1, source_target_pairs={{0,1},{1,0},{2,3},{3,2},{4,5},{5,4},{6,7},{7,6},{8,9},{9,8},{10,11... | collective-permute-start | bytes 1572872 | tf_op jit(solution)/shard_map/ppermute | solution.py:1258
  627.5 8.7 collective-permute-start.14
  633.4 11.0 %all-to-all-start.7 = ((f32[32,8,128]{2,1,0:T(8,128)}), f32[32,8,128]{2,1,0:T(8,128)S(1)}, u32[]{:S(2)}, u32[]{:S(2)}) async-start(f32[32,8,128]{2,1,0:T(8,128)} %get-tuple-element.136), calls=%async_computation.7 | async-start | bytes 262144 | tf_op jit(solution)/shard_map/all_to_all | solution.py:784
  637.1 23.4 %collective-permute-start.15 = (f32[2,128,512]{2,1,0:T(8,128)}, f32[2,128,512]{2,1,0:T(8,128)}, u32[]{:S(2)}, u32[]{:S(2)}) collective-permute-start(f32[2,128,512]{2,1,0:T(8,128)} %pad_maximum_fusion.28), channel_id=1, source_target_pairs={{0,1},{1,0},{2,3},{3,2},{4,5},{5,4},{6,7},{7,6},{8,9},{9,8},{10,11... | collective-permute-start | bytes 1572872 | tf_op jit(solution)/shard_map/ppermute | solution.py:1258
  650.4 16.2 %all-to-all-start.8 = ((f32[32,8,128]{2,1,0:T(8,128)}), f32[32,8,128]{2,1,0:T(8,128)S(1)}, u32[]{:S(2)}, u32[]{:S(2)}) async-start(f32[32,8,128]{2,1,0:T(8,128)} %get-tuple-element.142), calls=%async_computation.8 | async-start | bytes 262144 | tf_op jit(solution)/shard_map/all_to_all | solution.py:784
  655.1 243.2 %all-reduce.22.cloned.1.call-start = ((), (), s32[]{:S(2)}) async-start(), calls=%async_computation.14 | async-start | bytes 9576448 | tf_op jit(solution)/shard_map/psum | solution.py:1642
  655.2 16.1 %collective-permute-start.22 = (f32[128,512]{1,0:T(8,128)}, f32[128,512]{1,0:T(8,128)}, u32[]{:S(2)}, u32[]{:S(2)}) collective-permute-start(f32[128,512]{1,0:T(8,128)} %get-tuple-element.149), channel_id=1, source_target_pairs={{0,2},{1,3},{2,0},{3,1},{4,6},{5,7},{6,4},{7,5},{8,10},{9,11},{10,... | collective-permute-start | bytes 786440 | tf_op jit(solution)/shard_map/ppermute | solution.py:1262
  671.0 4.3 collective-permute-start.26
  672.3 12.5 %collective-permute-start.23 = (f32[2,128,512]{2,1,0:T(8,128)S(1)}, f32[2,128,512]{2,1,0:T(8,128)S(1)}, u32[]{:S(2)}, u32[]{:S(2)}) collective-permute-start(f32[2,128,512]{2,1,0:T(8,128)S(1)} %pad_maximum_fusion.31), channel_id=1, source_target_pairs={{0,1},{1,0},{2,3},{3,2},{4,5},{5,4},{6,7},{7,6},{8,9},{9,8},{10,11... | collective-permute-start | bytes 1572872 | tf_op jit(solution)/shard_map/ppermute | solution.py:1258
  672.4 8.9 collective-permute-start.18
  675.4 2.3 collective-permute-start.27
  681.4 9.5 collective-permute-start.19
  753.2 97.4 %all-to-all-start.9 = ((f32[8,4,128,128]{3,2,1,0:T(8,128)}), f32[8,4,128,128]{3,2,1,0:T(8,128)}, u32[]{:S(2)}, u32[]{:S(2)}) async-start(f32[8,4,128,128]{3,2,1,0:T(8,128)} %bitcast.453), calls=%async_computation.9 | async-start | bytes 4194304 | tf_op jit(solution)/shard_map/all_to_all | solution.py:1340
  845.6 2.2 collective-permute-start.28
  849.0 51.9 %collective-permute-start.29 = (f32[8,80,128]{2,1,0:T(8,128)S(1)}, f32[8,80,128]{2,1,0:T(8,128)S(1)}, u32[]{:S(2)}, u32[]{:S(2)}) collective-permute-start(f32[8,80,128]{2,1,0:T(8,128)S(1)} %select_bitcast_fusion.4), channel_id=1, source_target_pairs={{0,2},{1,3},{2,0},{3,1},{4,6},{5,7},{6,4},{7,5},{8,10},{9,11},{10,... | collective-permute-start | bytes 983048 | tf_op jit(solution)/shard_map/ppermute | solution.py:1262
  870.6 66.5 %collective-permute-start.32 = (f32[2,2560,128]{2,1,0:T(8,128)}, f32[2,2560,128]{2,1,0:T(8,128)}, u32[]{:S(2)}, u32[]{:S(2)}) collective-permute-start(f32[2,2560,128]{2,1,0:T(8,128)} %select_bitcast_fusion), channel_id=1, source_target_pairs={{0,1},{1,0},{2,3},{3,2},{4,5},{5,4},{6,7},{7,6},{8,9},{9,8},{10,11... | collective-permute-start | bytes 7864328 | tf_op jit(solution)/shard_map/ppermute | solution.py:1258
  904.2 59.4 %all-to-all-start.10 = ((f32[8,592,128]{2,1,0:T(8,128)}), f32[8,592,128]{2,1,0:T(8,128)S(1)}, u32[]{:S(2)}, u32[]{:S(2)}) async-start(f32[8,592,128]{2,1,0:T(8,128)} %pad_maximum_fusion.7), calls=%async_computation.10 | async-start | bytes 4849664 | tf_op jit(solution)/shard_map/all_to_all | solution.py:1342
  910.5 20.7 %collective-permute-start.34 = (f32[1664,128]{1,0:T(8,128)S(1)}, f32[1664,128]{1,0:T(8,128)S(1)}, u32[]{:S(2)}, u32[]{:S(2)}) collective-permute-start(f32[1664,128]{1,0:T(8,128)S(1)} %get-tuple-element.326), channel_id=1, source_target_pairs={{0,2},{1,3},{2,0},{3,1},{4,6},{5,7},{6,4},{7,5},{8,10},{9,11},{10,... | collective-permute-start | bytes 2555912 | tf_op jit(solution)/shard_map/ppermute | solution.py:1262
  931.3 12.3 %collective-permute-start.35 = (f32[2,1664,128]{2,1,0:T(8,128)S(1)}, f32[2,1664,128]{2,1,0:T(8,128)S(1)}, u32[]{:S(2)}, u32[]{:S(2)}) collective-permute-start(f32[2,1664,128]{2,1,0:T(8,128)S(1)} %pad_maximum_fusion.8), channel_id=1, source_target_pairs={{0,1},{1,0},{2,3},{3,2},{4,5},{5,4},{6,7},{7,6},{8,9},{9,8},{10,11... | collective-permute-start | bytes 5111816 | tf_op jit(solution)/shard_map/ppermute | solution.py:1258
  942.1 58.3 %collective-permute-start.33 = (f32[2560,128]{1,0:T(8,128)}, f32[2560,128]{1,0:T(8,128)}, u32[]{:S(2)}, u32[]{:S(2)}) collective-permute-start(f32[2560,128]{1,0:T(8,128)} %select_bitcast_fusion.2), channel_id=1, source_target_pairs={{0,2},{1,3},{2,0},{3,1},{4,6},{5,7},{6,4},{7,5},{8,10},{9,11},{10,... | collective-permute-start | bytes 3932168 | tf_op jit(solution)/shard_map/ppermute | solution.py:1262
  982.0 21.2 %collective-permute-start.30 = (f32[2,1792,128]{2,1,0:T(8,128)}, f32[2,1792,128]{2,1,0:T(8,128)}, u32[]{:S(2)}, u32[]{:S(2)}) collective-permute-start(f32[2,1792,128]{2,1,0:T(8,128)} %select_bitcast_fusion.1), channel_id=1, source_target_pairs={{0,1},{1,0},{2,3},{3,2},{4,5},{5,4},{6,7},{7,6},{8,9},{9,8},{10,11... | collective-permute-start | bytes 5505032 | tf_op jit(solution)/shard_map/ppermute | solution.py:1258
  989.1 35.7 %all-to-all-start.11 = ((f32[32,80,128]{2,1,0:T(8,128)}), f32[32,80,128]{2,1,0:T(8,128)}, u32[]{:S(2)}, u32[]{:S(2)}) async-start(f32[32,80,128]{2,1,0:T(8,128)} %broadcast_in_dim.26), calls=%async_computation.11 | async-start | bytes 2621440 | tf_op jit(solution)/shard_map/all_to_all | solution.py:1321
  1005.0 25.8 %copy-start.74 = (f32[32,128]{1,0:T(8,128)S(1)}, f32[32,128]{1,0:T(8,128)}, u32[]{:S(2)}) copy-start(f32[32,128]{1,0:T(8,128)} %param.42) | copy-start | bytes 49156
  1005.0 30.0 %copy-start.64 = (f32[32,62]{1,0:T(8,128)S(1)}, f32[32,62]{1,0:T(8,128)}, u32[]{:S(2)}) copy-start(f32[32,62]{1,0:T(8,128)} %copy-done.63) | copy-start | bytes 23812
  1005.1 31.4 %collective-permute-start.31 = (f32[1792,128]{1,0:T(8,128)S(1)}, f32[1792,128]{1,0:T(8,128)}, u32[]{:S(2)}, u32[]{:S(2)}) collective-permute-start(f32[1792,128]{1,0:T(8,128)S(1)} %select_bitcast_fusion.3), channel_id=1, source_target_pairs={{0,2},{1,3},{2,0},{3,1},{4,6},{5,7},{6,4},{7,5},{8,10},{9,11},{10,... | collective-permute-start | bytes 2752520 | tf_op jit(solution)/shard_map/ppermute | solution.py:1262
  (81 other events, 408.5 us)
Sparse Core Ops, SparseCore 0:
  10.9 192.0 all-gather.12
  205.9 234.4 all-gather.10
  443.2 118.8 all-gather.6
  564.1 76.9 all-gather.8
  700.4 197.9 all-reduce.21
where the time goes:
time: 1060 us; the launch traced here: 1050 us
  waiting for transfers between devices  407 us (38%)
  Pallas kernels  325 us (31%)
  other arithmetic  111 us (10%)
  local copies, waits for them, and re-layouts  92.3 us (9%)
  starting transfers between devices  77.7 us (7%)
  between operations  17.1 us (2%)
  matrix products  16.3 us (2%)
    all_gather x2, waiting for transfers between devices, gather_columns(): stacked = lax.all_gather(shard, both, axis=0)  187 us
    ppermute x18, waiting for transfers between devices, along_y(): lax.ppermute(values, 'section', [(place, place ^ 2) for place in range(4)])  122 us
    pallas_call x1, Pallas kernels, attention_backward(): pl.pallas_call(functools.partial(attention_backward_kernel, blocks, rows,...  70.1 us
    pallas_call x1, Pallas kernels, decoder_backward(): pl.pallas_call(functools.partial(decoder_backward_kernel, blocks, rows, l...  52.9 us
    pallas_call x1, Pallas kernels, attention_forward(): pl.pallas_call(functools.partial(attention_forward_kernel, blocks, rows,...  49.6 us
    pallas_call x10, Pallas kernels, post_call(): pl.pallas_call(kernel, in_specs=in_specs, out_specs=[pl.BlockSpec(memory_...  41.8 us
    pallas_call x1, Pallas kernels, decoder_forward(): pl.pallas_call(functools.partial(decoder_forward_kernel, blocks, rows, la...  37.4 us
    all_to_all x9, starting transfers between devices, share_sums(): return lax.all_to_all(copies, both, 0, 0)  34.8 us
  transfers between devices with their start and end apart: 53, of which 18 were waited for; matrix products, arithmetic and copies ran while one was open for 20% of the time, Pallas kernels for 31%

commit v1 on v0

--- a/solution.py
+++ b/solution.py
@@ -358,7 +358,9 @@
         resume = resume_ref[0]
         early = pl.multiple_of(frame * rows, rows)
         late = pl.multiple_of((frame + lag) * rows, rows)
-        arriving = jnp.concatenate([grad_ref[pl.ds(early, rows), :], grad_ref[pl.ds(late, rows), :]], axis=0)
+        arriving = jnp.concatenate(
+            [grad_ref[pl.ds(early, rows), :units], grad_ref[pl.ds(late, rows), :units]], axis=0
+        )
         total = grad_hidden[...] + arriving * valid_ref[0]
         cell_now = cell_ref[0] * jnp.where(frame > 0, resume, 0.0)
         zone_hidden, zone_cell = zone_masks(zone_early_ref, zone_late_ref)
@@ -402,8 +404,8 @@
     positions,
     lag,
     weight_ref,
-    grad_hidden_ref,
-    grad_context_ref,
+    grad_in_ref,
+    grad_out_ref,
     gates_ref,
     cell_ref,
     bent_ref,
@@ -483,7 +485,11 @@
         here = pl.multiple_of(frame * pair, pair)
         lane = lane_index((pair, lanes))
         arriving = jnp.concatenate(
-            [grad_context_ref[pl.ds(early, rows), :], grad_context_ref[pl.ds(late, rows), :]], axis=0
+            [
+                grad_in_ref[pl.ds(start, rows), units:] + grad_out_ref[pl.ds(start, rows), units:]
+                for start in (early, late)
+            ],
+            axis=0,
         )
         context_total = grad_context[...] + arriving * valid
         grad_contexts[pl.ds(here, pair), :] = context_total
@@ -517,7 +523,7 @@
         grad_window[...] = resume * (moved + jnp.where(second, window_grad, 0.0))
 
         arriving = jnp.concatenate(
-            [grad_hidden_ref[pl.ds(early, rows), :], grad_hidden_ref[pl.ds(late, rows), :]], axis=0
+            [grad_in_ref[pl.ds(early, rows), :units], grad_in_ref[pl.ds(late, rows), :units]], axis=0
         )
         total = grad_hidden[...] + arriving * valid
         total = total + product(query_total, query_upper[...], query_lower[...], transposed=True)
@@ -784,32 +790,42 @@
     return lax.all_to_all(copies, both, 0, 0)
 
 
-def tap_gradient_kernel(rows, inputs_ref, grads_ref, same_ref, out_ref):
-    groups, frame_rows, columns = grads_ref.shape
-    kernel = out_ref.shape[0]
+def tap_gradient_kernel(rows, kernel, split_inputs, own_ref, *refs):
+    count = (len(refs) - 1) // 3
+    input_refs, grad_refs, same_refs = refs[:count], refs[count : 2 * count], refs[2 * count : 3 * count]
+    out_ref = refs[-1]
     margin = kernel // 2
+    place = pl.ds(pl.multiple_of(own_ref[0] * lanes, lanes), lanes)
+    if split_inputs:
+        inputs = [ref[:, place] for ref in input_refs]
+        grads = [ref[...] for ref in grad_refs]
+    else:
+        inputs = [ref[...] for ref in input_refs]
+        grads = [ref[:, place] for ref in grad_refs]
     moved = []
     for tap in range(kernel):
-        pieces = []
-        for group in range(groups):
-            masked = grads_ref[group] * same_ref[group][:, tap : tap + 1]
-            pieces.append(moved_rows(masked, (tap - margin) * rows))
+        pieces = [
+            moved_rows(grad * same[:, tap : tap + 1], (tap - margin) * rows) for grad, same in zip(grads, same_refs)
+        ]
         moved.append(jnp.concatenate(pieces, axis=0))
     upper, lower = split(jnp.concatenate(moved, axis=1))
-    inputs = inputs_ref[...].reshape(groups * frame_rows, -1)
-    result = product(inputs.T, upper, lower)
+    result = product(jnp.concatenate(inputs, axis=0).T, upper, lower)
+    depth = out_ref.shape[1]
     for tap in range(kernel):
-        out_ref[tap] = result[:, tap * columns : (tap + 1) * columns]
-
-
-def tap_gradient(inputs, grads, same_segment, kernel, rows):
-    out = jax.ShapeDtypeStruct((kernel, inputs.shape[2], grads.shape[2]), f32)
+        block = result[:, tap * lanes : (tap + 1) * lanes]
+        out_ref[tap] = block.T[:depth] if split_inputs else block[:depth]
+
+
+def tap_gradient(inputs, grads, same, kernel, rows, depth, split_inputs=False):
+    own = lax.axis_index("section").astype(jnp.int32).reshape(1)
     return pl.pallas_call(
-        functools.partial(tap_gradient_kernel, rows),
-        out_shape=out,
+        functools.partial(tap_gradient_kernel, rows, kernel, split_inputs),
+        in_specs=[pl.BlockSpec(memory_space=pltpu.SMEM)]
+        + [pl.BlockSpec(memory_space=pltpu.VMEM)] * (len(inputs) + len(grads) + len(same)),
+        out_shape=jax.ShapeDtypeStruct((kernel, depth, lanes), f32),
         compiler_params=pltpu.CompilerParams(vmem_limit_bytes=vmem_limit),
         name="tap_gradient",
-    )(inputs, grads, same_segment)
+    )(own, *inputs, *grads, *same)
 
 
 def frame_product_kernel(pieces, *refs):
@@ -1113,8 +1129,8 @@
 
 def attention_backward(
     weight,
-    grad_hidden,
-    grad_context,
+    grad_in,
+    grad_out,
     gates,
     cells,
     bent,
@@ -1140,8 +1156,8 @@
     units = columns // 4
     width = shard_block * lanes
     pair = 2 * rows
-    frame_rows = grad_hidden.shape[0]
-    context_width = grad_context.shape[1]
+    frame_rows = grad_in.shape[0]
+    context_width = memory.shape[1]
     rest = depth - prenet_width
 
     def shard(step):
@@ -1171,8 +1187,8 @@
         grid=(blocks + span,),
         in_specs=[
             shard_spec(weight, shard),
-            whole_spec(grad_hidden),
-            whole_spec(grad_context),
+            whole_spec(grad_in),
+            whole_spec(grad_out),
             timed_spec(gates, timed),
             timed_spec(cells, before),
             timed_spec(bent, timed),
@@ -1217,8 +1233,8 @@
         name="attention_backward",
     )(
         weight,
-        grad_hidden,
-        grad_context,
+        grad_in,
+        grad_out,
         gates,
         cells,
         bent,
@@ -1268,6 +1284,11 @@
 
 def gather_core(two):
     return jnp.concatenate([two, along_core(two)], axis=0)
+
+
+def list_section(values):
+    other = along_y(values)
+    return [values, other, along_core(values), along_core(other)]
 
 
 def gather_section(values):
@@ -1529,7 +1550,7 @@
         [padded[offset : offset + frames] == segment for offset in range(kernel)], axis=2
     ).astype(f32)
     same = jnp.pad(same_segment, ((0, 0), (0, 0), (0, 8 - kernel))).reshape(frame_rows, 8)
-    same_all = gather_section(same)
+    same_all = list_section(same)
     frame_count = frame_rows * devices
     gains = [norm_gain[layer : layer + 1] for layer in range(4)] + [last_gain.reshape(1, mel)]
     shifts = [norm_shift[layer : layer + 1] for layer in range(4)] + [last_shift.reshape(1, mel)]
@@ -1542,7 +1563,7 @@
         (mel_before, same, *post_split[0]),
     )
     scaled, inverse, active, inputs_all = [], [], [], []
-    inputs_all.append(gather_section(jnp.pad(mel_before, ((0, 0), (0, lanes - mel)))))
+    inputs_all.append(list_section(jnp.pad(mel_before, ((0, 0), (0, lanes - mel)))))
     for layer in range(4):
         scaled_now, active_now, inverse_now, conv, copies = post_call(
             functools.partial(post_next_kernel, rows, frame_count),
@@ -1560,7 +1581,7 @@
         scaled.append(scaled_now)
         active.append(active_now)
         inverse.append(inverse_now)
-        inputs_all.append(gather_section(active_now))
+        inputs_all.append(list_section(active_now))
     mel_after, grad_conv, packed, upstream, copies = post_call(
         functools.partial(post_turn_kernel, rows, frame_count),
         [(frame_rows, mel), (frame_rows, lanes), (8, lanes), (frame_rows, widths[3]), (devices, 8, lanes)],
@@ -1583,11 +1604,7 @@
     shift_grads = [None] * 5
     shift_grads[4], gain_grads[4] = [row.reshape(-1) for row in unpack_sums(packed, mel)]
     weight_grads[4] = tap_gradient(
-        own_columns(inputs_all[4], inputs_all[4].shape[2] // section_size),
-        gather_section(grad_conv),
-        same_all,
-        kernel,
-        rows,
+        inputs_all[4], list_section(grad_conv), same_all, kernel, rows, mel, split_inputs=True
     )
     for layer in reversed(range(4)):
         below = (active[layer - 1], scaled[layer - 1]) if layer else ()
@@ -1615,13 +1632,8 @@
         if layer:
             copies = results[3]
         shift_grads[layer], gain_grads[layer] = [row.reshape(-1) for row in unpack_sums(packed, widths[layer])]
-        weight_grads[layer] = tap_gradient(
-            inputs_all[layer],
-            own_columns(gather_section(grad_conv), grad_conv.shape[1] // section_size),
-            same_all,
-            kernel,
-            rows,
-        )
+        depth = widths[layer - 1] if layer else mel
+        weight_grads[layer] = tap_gradient(inputs_all[layer], list_section(grad_conv), same_all, kernel, rows, depth)
 
     grad_mel = grad_after_frames + upstream
     grad_stop_frames = grad_stop.T.reshape(frame_rows, 1)
@@ -1629,10 +1641,10 @@
     mel_grads = jnp.pad(
         jnp.concatenate([grad_mel, grad_stop_frames], axis=1), ((0, 0), (0, lanes - mel - 1))
     )
-    mel_pair = gather_y(mel_grads)
-    mel_grads_all = gather_core(mel_pair).reshape(-1, lanes)
-    outs_own = own_columns(gather_section(out_frames), out_frames.shape[1] // section_size)
-    outs_own = outs_own.reshape(mel_grads_all.shape[0], -1)
+    mel_grads_all = jnp.concatenate(list_section(mel_grads), axis=0)
+    outs_own = jnp.concatenate(
+        [own_columns(outs, out_frames.shape[1] // section_size) for outs in list_section(out_frames)], axis=0
+    )
     g_proj_part = dot(outs_own, mel_grads_all, 0, 0)
     group_grads, group_token = join_rows(
         [grad.reshape(-1, lanes) for grad in weight_grads + [g_proj_part]]
@@ -1642,7 +1654,7 @@
     group_sums = lax.psum(group_grads, "dp")
     dec_sums, grad_dec_inputs = decoder_backward(
         dec_all,
-        grad_out[:, :units],
+        grad_out,
         dec_gates,
         dec_cells,
         zone,
@@ -1653,7 +1665,6 @@
         [group_token],
     )
     g_dec_bias = jnp.sum(dec_sums, axis=1).reshape(-1)
-    grad_context = grad_out[:, units:] + grad_dec_inputs[:, units:]
     dec_columns = exchange_ring(dec_sums) if rings else None
     (
         att_sums,
@@ -1666,8 +1677,8 @@
         grad_energy,
     ) = attention_backward(
         att_all,
-        grad_dec_inputs[:, :units],
-        grad_context,
+        grad_dec_inputs,
+        grad_out,
         gates,
         cells,
         bent,
@@ -1730,7 +1741,7 @@
     g_loc_filters = dot(loc_dense, grad_joined, 1, 1).reshape(loc_filters.shape)
     g_loc_dense = dot(loc_filters.reshape(filters, channels * taps), grad_joined)
 
-    first_rows = kernel * lanes
+    first_rows = kernel * mel
     mid_end = first_rows + post_mid.size // lanes
     proj_start = mid_end + first_rows
     proj_end = proj_start + out_frames.shape[1] // section_size
@@ -1739,11 +1750,11 @@
     shared = jnp.concatenate([group_sums[:first_rows], group_sums[mid_end:proj_end]], axis=0)
     shared_all = section_order(gather_section(shared), own)
     g_post_first = jnp.concatenate(
-        [piece[:first_rows].reshape(kernel, lanes, lanes)[:, :mel] for piece in shared_all], axis=2
+        [piece[:first_rows].reshape(kernel, mel, lanes) for piece in shared_all], axis=2
     )
     g_post_last = jnp.concatenate(
-        [piece[first_rows : 2 * first_rows].reshape(kernel, lanes, lanes)[:, :, :mel] for piece in shared_all], axis=1
-    )
+        [piece[first_rows : 2 * first_rows].reshape(kernel, mel, lanes) for piece in shared_all], axis=2
+    ).swapaxes(1, 2)
     g_proj = jnp.concatenate([piece[2 * first_rows :] for piece in shared_all], axis=0)
     g_proj_bias = group_sums[proj_end, :mel]
     return (

time: 1060 us -> 1040 us (0.981)
  other arithmetic: 111 us -> 70.2 us
  blocking collectives: 0 us -> 29.2 us
    all_to_all x0 -> x2, blocking collectives: none -> 29.2 us  [share_sums(): return lax.all_to_all(copies, both, 0, 0)]
    concatenate x14 -> x2, other arithmetic: 33.4 us -> 12.4 us  [gather_core(): return jnp.concatenate([two, along_core(two)], axis=0)]
    another operation x17 -> x3, other arithmetic: 23.9 us -> 6.02 us  [gather_y(): return jnp.stack([values, along_y(values)])]
    all_to_all x1, waiting for transfers between devices: 18 us -> 28.9 us  [exchange_ring(): received = lax.all_to_all(joined, 'dp', 0, 0)]
    all_to_all x9 -> x7, starting transfers between devices: 34.8 us -> 27.1 us  [share_sums(): return lax.all_to_all(copies, both, 0, 0)]
    unnamed x224 -> x236, local copies, waits for them, and re-layouts: 25.5 us -> 23.3 us
    all_to_all x9 -> x7, waiting for transfers between devices: 32.6 us -> 32.4 us  [share_sums(): return lax.all_to_all(copies, both, 0, 0)]
  transfers between devices with their start and end apart: 53 -> 64, of which waited for: 18 -> 20; matrix products, arithmetic and copies ran while one was open for 20% -> 15% of each run, Pallas kernels for 31% -> 31%
where the time goes in v1:
time: 1040 us; the launch traced here: 1030 us
  waiting for transfers between devices  415 us (40%)
  Pallas kernels  325 us (31%)
  local copies, waits for them, and re-layouts  86.6 us (8%)
  starting transfers between devices  71.1 us (7%)
  other arithmetic  70.2 us (7%)
  blocking collectives  29.2 us (3%)
  between operations  17.3 us (2%)
  matrix products  14.5 us (1%)
    all_gather x2, waiting for transfers between devices, gather_columns(): stacked = lax.all_gather(shard, both, axis=0)  188 us
    ppermute x18, waiting for transfers between devices, along_y(): lax.ppermute(values, 'section', [(place, place ^ 2) for place in range(4)])  118 us
    pallas_call x1, Pallas kernels, attention_backward(): pl.pallas_call(functools.partial(attention_backward_kernel, blocks, rows,...  70.3 us
    pallas_call x1, Pallas kernels, decoder_backward(): pl.pallas_call(functools.partial(decoder_backward_kernel, blocks, rows, l...  52.8 us
    pallas_call x1, Pallas kernels, attention_forward(): pl.pallas_call(functools.partial(attention_forward_kernel, blocks, rows,...  49.6 us
    pallas_call x10, Pallas kernels, post_call(): pl.pallas_call(kernel, in_specs=in_specs, out_specs=[pl.BlockSpec(memory_...  41.5 us
    pallas_call x1, Pallas kernels, decoder_forward(): pl.pallas_call(functools.partial(decoder_forward_kernel, blocks, rows, la...  37.4 us
    all_to_all x7, waiting for transfers between devices, share_sums(): return lax.all_to_all(copies, both, 0, 0)  32.4 us
  transfers between devices with their start and end apart: 64, of which 20 were waited for; matrix products, arithmetic and copies ran while one was open for 15% of the time, Pallas kernels for 31%

profile of v1, /device:TPU:0, one launch (start us, length us, event | category | flops | bytes accessed | tf_op | source)
XLA Modules:
  0.0 1028.4 jit_solution(12501697336308095356)
XLA Ops:
  8.8 3.0 collective-permute-start
  16.2 4.2 copy.159
  27.5 98.2 %collective-permute-done = f32[7680,128]{1,0:T(8,128)} collective-permute-done((f32[7680,128]{1,0:T(8,128)}, f32[7680,128]{1,0:T(8,128)}, u32[]{:S(2)}, u32[]{:S(2)}) %collective-permute-start) | collective-permute-done | bytes 3932192 | tf_op jit(solution)/shard_map/ppermute | solution.py:1278
  125.7 5.9 pad_maximum_fusion.1.awaited
  131.5 71.5 %all-gather.13.cloned.1.call-done = f32[57344,128]{1,0:T(8,128)} async-done(((f32[1792,128]{1,0:T(8,128)}), f32[57344,128]{1,0:T(8,128)}) %all-gather.13.cloned.1.call-update) | async-done | bytes 29360144 | tf_op jit(solution)/shard_map/all_gather | solution.py:1267
  203.1 49.6 %attention_forward.1 = (f32[6,32,1024]{2,1,0:T(8,128)}, f32[6,32,1024]{2,1,0:T(8,128)}, f32[6,32,512]{2,1,0:T(8,128)}, f32[6,32,4096]{2,1,0:T(8,128)}, f32[6,32,...) custom-call(f32[32,1792,128]{2,1,0:T(8,128)} %bitcast.396, f32[128,256]{1,0:T(8,128)} %copy-done.43, ...), custom_call_target="tpu_custom_call" | custom-call | flops 45097156608 | bytes 29360128 | tf_op jit(solution)/shard_map/attention_forward/pallas_call | solution.py:955
  262.7 10.8 %pad_maximum_fusion = f32[4,7680,128]{2,1,0:T(8,128)} fusion(f32[2,7680,128]{2,1,0:T(8,128)} %collective-permute-done.1, f32[1,7680,128]{2,1,0:T(8,128)} %bitcast.52, f32[1,7680,128]{2,1,0:T(8,128)} %bitcast.427), kind=kLoop, calls=%fused_computation | loop fusion | flops 7864320 | bytes 31457280 | tf_op jit(solution)/shard_map/concatenate | solution.py:1286
  273.5 11.5 %fusion.114 = (f32[4,2560,128]{2,1,0:T(8,128)}, f32[4,2560,128]{2,1,0:T(8,128)}, f32[4,2560,128]{2,1,0:T(8,128)}) fusion(f32[4,7680,128]{2,1,0:T(8,128)} %pad_maximum_fusion), kind=kLoop, calls=%fused_computation.302 | loop fusion | bytes 31457280 | tf_op jit(solution)/shard_map/slice | solution.py:1313
  285.0 6.8 dynamic-slice_bitcast_fusion.3
  291.8 2.6 pad_maximum_fusion.4.values_ref
  294.4 5.2 split_matrix.8
  299.6 5.2 pad_maximum_fusion.3.values_ref
  304.8 5.4 split_matrix.7
  310.3 2.8 dynamic-slice_bitcast_fusion.11
  313.1 2.7 pad_maximum_fusion.2.values_ref
  315.8 6.8 split_matrix.6
  323.5 117.0 %all-gather.11.cloned.1.call-done = f32[81920,128]{1,0:T(8,128)} async-done(((f32[2560,128]{1,0:T(8,128)}), f32[81920,128]{1,0:T(8,128)}) %all-gather.11.cloned.1.call-update) | async-done | bytes 41943056 | tf_op jit(solution)/shard_map/all_gather | solution.py:1267
  440.4 37.4 %decoder_forward.1 = (f32[6,32,1024]{2,1,0:T(8,128)}, f32[6,32,1024]{2,1,0:T(8,128)}, f32[6,32,4096]{2,1,0:T(8,128)}) custom-call(f32[32,2560,128]{2,1,0:T(8,128)} %bitcast.500, f32[128,1536]{1,0:T(8,128)} %pad_maximum_fusion.8.frames_ref, f32[8,1,512]{2,1,0:T(1,128)} %bitcast.507, s32[8,4,16,1024]{3,2,1,0:T(8,128)} %bitcast.400, ...), custom_call_target="tpu_custom_call" | custom-call | flops 32212254720 | bytes 41943040 | tf_op jit(solution)/shard_map/decoder_forward/pallas_call | solution.py:1031
  482.0 2.7 post_first.1
  484.7 3.2 all-to-all-start
  489.1 10.2 all-to-all-done.sums_ref
  500.0 4.7 post_next.4
  504.7 13.9 %all_to_all.60.sums_ref = f32[32,8,128]{2,1,0:T(8,128)} all-to-all(f32[32,8,128]{2,1,0:T(8,128)} %get-tuple-element.114), channel_id=1, replica_groups=mesh['dp'=8,'section'=4] {'dp','section'}, dimensions={0} | all-to-all | bytes 262144 | tf_op jit(solution)/shard_map/all_to_all | solution.py:790
  518.6 4.7 post_next.5
  523.4 15.3 %all_to_all.61.sums_ref = f32[32,8,128]{2,1,0:T(8,128)} all-to-all(f32[32,8,128]{2,1,0:T(8,128)} %get-tuple-element.116), channel_id=1, replica_groups=mesh['dp'=8,'section'=4] {'dp','section'}, dimensions={0} | all-to-all | bytes 262144 | tf_op jit(solution)/shard_map/all_to_all | solution.py:790
  538.7 4.7 post_next.6
  546.6 8.9 all-to-all-done.3.sums_ref
  556.2 2.9 post_next.7
  559.1 4.6 all-to-all-start.4
  565.8 6.2 all-to-all-done.4.sums_ref
  572.7 3.1 post_turn.1
  580.4 4.4 collective-permute-done.8.refs_9_
  589.2 5.3 post_back.4
  594.6 5.1 all-to-all-start.6
  605.7 3.0 tap_gradient.5.refs_2_
  611.0 5.3 post_back.5
  616.3 3.9 all-to-all-start.7
  624.8 4.4 tap_gradient.6.refs_2_
  629.2 5.0 all-to-all-done.7.sums_ref
  634.8 5.3 post_back.6
  640.1 5.1 all-to-all-start.8
  652.0 4.4 tap_gradient.7.refs_0_
  657.1 2.7 post_back.7
  669.0 3.9 collective-permute-done.32.refs_5_
  672.9 4.9 collective-permute-done.26.refs_5_
  681.3 4.4 tap_gradient.9
  687.2 2.9 tap_gradient.8
  690.1 4.6 join_rows.1
  694.7 52.8 %decoder_backward.1 = (f32[32,128,128]{2,1,0:T(8,128)}, f32[128,1536]{1,0:T(8,128)}) custom-call(f32[32,2560,128]{2,1,0:T(8,128)} %bitcast.501, f32[32,2560,128]{2,1,0:T(8,128)} %bitcast.502, f32[32,2560,128]{2,1,0:T(8,128)} %bitcast.503, f32[32,2560,128]{2,1,0:T(8,128)} %bitcast.504, f32[32,2560,128]{2,1,0:T(8,128)} %bitcast.505, ...), custom_call_target="tpu_custom_call" | custom-call | flops 257698037760 | bytes 41943040 | tf_op jit(solution)/shard_map/decoder_backward/pallas_call | solution.py:1100
  747.5 5.5 all-to-all-start.9
  753.9 70.3 %attention_backward.1 = (f32[32,128,128]{2,1,0:T(8,128)}, f32[1,4096]{1,0:T(1,128)}, f32[128,256]{1,0:T(8,128)}, f32[128,128]{1,0:T(8,128)}, f32[16,4096]{1,0:T(...) custom-call(f32[32,1792,128]{2,1,0:T(8,128)} %bitcast.397, ...), custom_call_target="tpu_custom_call" | custom-call | flops 16777216 | bytes 65536 | tf_op jit(solution)/shard_map/attention_backward/pallas_call | solution.py:1185
  842.9 15.6 %frame_product.3 = f32[4,2560,128]{2,1,0:T(8,128)} custom-call(f32[1024,1792]{1,0:T(8,128)} %all-gather.7.cloned.1.call-done.refs_7_.refs_0_, f32[1024,1024]{1,0:T(8,128)} %all-gather.9.cloned.1.call-done.refs_8_.refs_1_, f32[8,4,128,128]{3,2,1,0:T(8,128)} %all-to-all-done.9.refs_2_), custom_call_target="tpu_custom_call" | custom-call | tf_op jit(solution)/shard_map/frame_product/pallas_call | solution.py:873
  858.5 4.3 select_bitcast_fusion
  864.0 22.7 %all-reduce.22.cloned.1.call-done = f32[8872,128]{1,0:T(8,128)} async-done(((f32[8872,128]{1,0:T(8,128)}), f32[8872,128]{1,0:T(8,128)}) %all-reduce.22.cloned.1.call-update) | async-done | bytes 4542480 | tf_op jit(solution)/shard_map/psum | solution.py:1654
  889.4 3.2 pad_maximum_fusion.5
  892.6 4.0 all-to-all-start.10
  903.1 4.4 slice.741
  908.7 6.1 collective-permute-done.47
  923.1 28.9 %all-to-all-done.10 = f32[8,592,128]{2,1,0:T(8,128)S(1)} async-done(((f32[8,592,128]{2,1,0:T(8,128)}), f32[8,592,128]{2,1,0:T(8,128)S(1)}, u32[]{:S(2)}, u32[]{:S(2)}) %all-to-all-start.10) | async-done | bytes 2424864 | tf_op jit(solution)/shard_map/all_to_all | solution.py:1363
  954.0 11.8 %frame_product.2 = f32[4,1792,128]{2,1,0:T(8,128)} custom-call(f32[1024,1792]{1,0:T(8,128)} %all-gather.7.cloned.1.call-done.refs_7_.refs_0_, f32[8,4,128,128]{3,2,1,0:T(8,128)} %bitcast.443), custom_call_target="tpu_custom_call" | custom-call | tf_op jit(solution)/shard_map/frame_product/pallas_call | solution.py:873
  965.9 3.7 select_bitcast_fusion.1
  971.8 3.7 all-to-all-start.11
  981.7 2.7 bitcast_add_fusion.2
  988.2 19.2 %all-to-all-done.11 = f32[32,80,128]{2,1,0:T(8,128)} async-done(((f32[32,80,128]{2,1,0:T(8,128)}), f32[32,80,128]{2,1,0:T(8,128)}, u32[]{:S(2)}, u32[]{:S(2)}) %all-to-all-start.11) | async-done | bytes 1310752 | tf_op jit(solution)/shard_map/all_to_all | solution.py:1342
  (489 shorter events, 145.6 us)
Async XLA Ops:
  7.2 195.8 %all-gather.13.cloned.1.call-start = ((), (), s32[]{:S(2)}) async-start(), calls=%async_computation.16 | async-start | bytes 30277632 | tf_op jit(solution)/shard_map/all_gather | solution.py:1267
  8.0 432.4 %all-gather.11.cloned.1.call-start = ((), (), s32[]{:S(2)}) async-start(), calls=%async_computation.15 | async-start | bytes 43253760 | tf_op jit(solution)/shard_map/all_gather | solution.py:1267
  8.7 681.3 %all-gather.7.cloned.1.call-start = ((), (), s32[]{:S(2)}) async-start(), calls=%async_computation.12 | async-start | bytes 8257536 | tf_op jit(solution)/shard_map/all_gather | solution.py:1537
  8.8 116.9 %collective-permute-start = (f32[7680,128]{1,0:T(8,128)}, f32[7680,128]{1,0:T(8,128)}, u32[]{:S(2)}, u32[]{:S(2)}) collective-permute-start(f32[7680,128]{1,0:T(8,128)} %bitcast.426), channel_id=1, source_target_pairs={{0,2},{1,3},{2,0},{3,1},{4,6},{5,7},{6,4},{7,5},{8,10},{9,11},{10,... | collective-permute-start | bytes 11796488 | tf_op jit(solution)/shard_map/ppermute | solution.py:1278
  131.5 131.1 %collective-permute-start.1 = (f32[2,7680,128]{2,1,0:T(8,128)}, f32[2,7680,128]{2,1,0:T(8,128)}, u32[]{:S(2)}, u32[]{:S(2)}) collective-permute-start(f32[2,7680,128]{2,1,0:T(8,128)} %pad_maximum_fusion.1.awaited), channel_id=1, source_target_pairs={{0,1},{1,0},{2,3},{3,2},{4,5},{5,4},{6,7},{7,6},{8,9},{9,8},{10,11... | collective-permute-start | bytes 23592968 | tf_op jit(solution)/shard_map/ppermute | solution.py:1274
  256.2 433.9 %all-gather.9.cloned.1.call-start = ((), (), s32[]{:S(2)}) async-start(), calls=%async_computation.13 | async-start | bytes 4718592 | tf_op jit(solution)/shard_map/all_gather | solution.py:1538
  484.7 14.7 %all-to-all-start = ((f32[32,8,128]{2,1,0:T(8,128)}), f32[32,8,128]{2,1,0:T(8,128)S(1)}, u32[]{:S(2)}, u32[]{:S(2)}) async-start(f32[32,8,128]{2,1,0:T(8,128)} %get-tuple-element.112), calls=%async_computation | async-start | bytes 262144 | tf_op jit(solution)/shard_map/all_to_all | solution.py:790
  543.4 12.1 %all-to-all-start.3 = ((f32[32,8,128]{2,1,0:T(8,128)}), f32[32,8,128]{2,1,0:T(8,128)S(1)}, u32[]{:S(2)}, u32[]{:S(2)}) async-start(f32[32,8,128]{2,1,0:T(8,128)} %get-tuple-element.118), calls=%async_computation.3 | async-start | bytes 262144 | tf_op jit(solution)/shard_map/all_to_all | solution.py:790
  559.1 13.0 %all-to-all-start.4 = ((f32[32,8,128]{2,1,0:T(8,128)}), f32[32,8,128]{2,1,0:T(8,128)S(1)}, u32[]{:S(2)}, u32[]{:S(2)}) async-start(f32[32,8,128]{2,1,0:T(8,128)} %get-tuple-element.120), calls=%async_computation.4 | async-start | bytes 262144 | tf_op jit(solution)/shard_map/all_to_all | solution.py:790
  563.7 24.2 %collective-permute-start.2 = (f32[128,512]{1,0:T(8,128)}, f32[128,512]{1,0:T(8,128)S(1)}, u32[]{:S(2)}, u32[]{:S(2)}) collective-permute-start(f32[128,512]{1,0:T(8,128)} %get-tuple-element.121.active_ref.refs_0_), channel_id=1, source_target_pairs={{0,2},{1,3},{2,0},{3,1},{4,6},{5,7},{6,4},{7,5},{8,10},{9,11},{10,... | collective-permute-start | bytes 786440 | tf_op jit(solution)/shard_map/ppermute | solution.py:1278
  565.6 34.1 %collective-permute-start.11 = (f32[128,512]{1,0:T(8,128)}, f32[128,512]{1,0:T(8,128)}, u32[]{:S(2)}, u32[]{:S(2)}) collective-permute-start(f32[128,512]{1,0:T(8,128)} %get-tuple-element.127.refs_0_), channel_id=1, source_target_pairs={{0,2},{1,3},{2,0},{3,1},{4,6},{5,7},{6,4},{7,5},{8,10},{9,11},{10,... | collective-permute-start | bytes 786440 | tf_op jit(solution)/shard_map/ppermute | solution.py:1278
  565.8 35.7 %collective-permute-start.3 = (f32[128,512]{1,0:T(8,128)}, f32[128,512]{1,0:T(8,128)}, u32[]{:S(2)}, u32[]{:S(2)}) collective-permute-start(f32[128,512]{1,0:T(8,128)} %get-tuple-element.121.active_ref.refs_0_), channel_id=1, source_target_pairs={{0,1},{1,0},{2,3},{3,2},{4,5},{5,4},{6,7},{7,6},{8,9},{9,8},{10,11... | collective-permute-start | bytes 786440 | tf_op jit(solution)/shard_map/ppermute | solution.py:1274
  575.8 12.8 %all-to-all-start.5 = ((f32[32,8,128]{2,1,0:T(8,128)}), f32[32,8,128]{2,1,0:T(8,128)S(1)}, u32[]{:S(2)}, u32[]{:S(2)}) async-start(f32[32,8,128]{2,1,0:T(8,128)} %get-tuple-element.125), calls=%async_computation.5 | async-start | bytes 262144 | tf_op jit(solution)/shard_map/all_to_all | solution.py:790
  578.3 9.2 collective-permute-start.5
  580.1 4.8 collective-permute-start.8
  584.9 1.3 collective-permute-start.9
  586.1 1.3 collective-permute-start.10
  587.4 14.1 %collective-permute-start.6 = (f32[128,128]{1,0:T(8,128)}, f32[128,128]{1,0:T(8,128)S(1)}, u32[]{:S(2)}, u32[]{:S(2)}) collective-permute-start(f32[128,128]{1,0:T(8,128)} %get-tuple-element.134.refs_4_), channel_id=1, source_target_pairs={{0,1},{1,0},{2,3},{3,2},{4,5},{5,4},{6,7},{7,6},{8,9},{9,8},{10,11... | collective-permute-start | bytes 196616 | tf_op jit(solution)/shard_map/ppermute | solution.py:1274
  587.6 14.5 %collective-permute-start.7 = (f32[128,128]{1,0:T(8,128)S(1)}, f32[128,128]{1,0:T(8,128)}, u32[]{:S(2)}, u32[]{:S(2)}) collective-permute-start(f32[128,128]{1,0:T(8,128)S(1)} %collective-permute-done.5.refs_5_), channel_id=1, source_target_pairs={{0,1},{1,0},{2,3},{3,2},{4,5},{5,4},{6,7},{7,6},{8,9},{9,8},{10,11... | collective-permute-start | bytes 196616 | tf_op jit(solution)/shard_map/ppermute | solution.py:1274
  587.9 15.9 %collective-permute-start.4 = (f32[128,512]{1,0:T(8,128)S(1)}, f32[128,512]{1,0:T(8,128)}, u32[]{:S(2)}, u32[]{:S(2)}) collective-permute-start(f32[128,512]{1,0:T(8,128)S(1)} %collective-permute-done.2.refs_1_), channel_id=1, source_target_pairs={{0,1},{1,0},{2,3},{3,2},{4,5},{5,4},{6,7},{7,6},{8,9},{9,8},{10,11... | collective-permute-start | bytes 786440 | tf_op jit(solution)/shard_map/ppermute | solution.py:1274
  594.6 15.7 %all-to-all-start.6 = ((f32[32,8,128]{2,1,0:T(8,128)}), f32[32,8,128]{2,1,0:T(8,128)S(1)}, u32[]{:S(2)}, u32[]{:S(2)}) async-start(f32[32,8,128]{2,1,0:T(8,128)} %get-tuple-element.130), calls=%async_computation.6 | async-start | bytes 262144 | tf_op jit(solution)/shard_map/all_to_all | solution.py:790
  599.7 20.5 %collective-permute-start.17 = (f32[128,512]{1,0:T(8,128)}, f32[128,512]{1,0:T(8,128)}, u32[]{:S(2)}, u32[]{:S(2)}) collective-permute-start(f32[128,512]{1,0:T(8,128)} %get-tuple-element.132.refs_0_), channel_id=1, source_target_pairs={{0,2},{1,3},{2,0},{3,1},{4,6},{5,7},{6,4},{7,5},{8,10},{9,11},{10,... | collective-permute-start | bytes 786440 | tf_op jit(solution)/shard_map/ppermute | solution.py:1278
  601.5 19.1 %collective-permute-start.12 = (f32[128,512]{1,0:T(8,128)}, f32[128,512]{1,0:T(8,128)}, u32[]{:S(2)}, u32[]{:S(2)}) collective-permute-start(f32[128,512]{1,0:T(8,128)} %get-tuple-element.127.refs_0_), channel_id=1, source_target_pairs={{0,1},{1,0},{2,3},{3,2},{4,5},{5,4},{6,7},{7,6},{8,9},{9,8},{10,11... | collective-permute-start | bytes 786440 | tf_op jit(solution)/shard_map/ppermute | solution.py:1274
  601.6 19.3 %collective-permute-start.13 = (f32[128,512]{1,0:T(8,128)}, f32[128,512]{1,0:T(8,128)}, u32[]{:S(2)}, u32[]{:S(2)}) collective-permute-start(f32[128,512]{1,0:T(8,128)} %collective-permute-done.11.refs_1_), channel_id=1, source_target_pairs={{0,1},{1,0},{2,3},{3,2},{4,5},{5,4},{6,7},{7,6},{8,9},{9,8},{10,11... | collective-permute-start | bytes 786440 | tf_op jit(solution)/shard_map/ppermute | solution.py:1274
  602.1 20.7 %collective-permute-start.14 = (f32[128,512]{1,0:T(8,128)}, f32[128,512]{1,0:T(8,128)}, u32[]{:S(2)}, u32[]{:S(2)}) collective-permute-start(f32[128,512]{1,0:T(8,128)} %get-tuple-element.140.refs_4_), channel_id=1, source_target_pairs={{0,2},{1,3},{2,0},{3,1},{4,6},{5,7},{6,4},{7,5},{8,10},{9,11},{10,... | collective-permute-start | bytes 786440 | tf_op jit(solution)/shard_map/ppermute | solution.py:1278
  603.8 42.8 %collective-permute-start.35 = (f32[128,1536]{1,0:T(8,128)}, f32[128,1536]{1,0:T(8,128)}, u32[]{:S(2)}, u32[]{:S(2)}) collective-permute-start(f32[128,1536]{1,0:T(8,128)} %get-tuple-element.277), channel_id=1, source_target_pairs={{0,2},{1,3},{2,0},{3,1},{4,6},{5,7},{6,4},{7,5},{8,10},{9,11},{10,... | collective-permute-start | bytes 2359304 | tf_op jit(solution)/shard_map/ppermute | solution.py:1278
  616.3 17.8 %all-to-all-start.7 = ((f32[32,8,128]{2,1,0:T(8,128)}), f32[32,8,128]{2,1,0:T(8,128)S(1)}, u32[]{:S(2)}, u32[]{:S(2)}) async-start(f32[32,8,128]{2,1,0:T(8,128)} %get-tuple-element.136), calls=%async_computation.7 | async-start | bytes 262144 | tf_op jit(solution)/shard_map/all_to_all | solution.py:790
  620.3 25.0 %collective-permute-start.18 = (f32[128,512]{1,0:T(8,128)}, f32[128,512]{1,0:T(8,128)}, u32[]{:S(2)}, u32[]{:S(2)}) collective-permute-start(f32[128,512]{1,0:T(8,128)} %get-tuple-element.132.refs_0_), channel_id=1, source_target_pairs={{0,1},{1,0},{2,3},{3,2},{4,5},{5,4},{6,7},{7,6},{8,9},{9,8},{10,11... | collective-permute-start | bytes 786440 | tf_op jit(solution)/shard_map/ppermute | solution.py:1274
  620.7 2.9 collective-permute-start.15
  620.8 24.7 %collective-permute-start.20 = (f32[128,512]{1,0:T(8,128)}, f32[128,512]{1,0:T(8,128)}, u32[]{:S(2)}, u32[]{:S(2)}) collective-permute-start(f32[128,512]{1,0:T(8,128)} %get-tuple-element.144.refs_4_), channel_id=1, source_target_pairs={{0,2},{1,3},{2,0},{3,1},{4,6},{5,7},{6,4},{7,5},{8,10},{9,11},{10,... | collective-permute-start | bytes 786440 | tf_op jit(solution)/shard_map/ppermute | solution.py:1278
  622.7 2.1 collective-permute-start.16
  624.3 36.5 %collective-permute-start.36 = (f32[128,1536]{1,0:T(8,128)}, f32[128,1536]{1,0:T(8,128)}, u32[]{:S(2)}, u32[]{:S(2)}) collective-permute-start(f32[128,1536]{1,0:T(8,128)} %get-tuple-element.277), channel_id=1, source_target_pairs={{0,1},{1,0},{2,3},{3,2},{4,5},{5,4},{6,7},{7,6},{8,9},{9,8},{10,11... | collective-permute-start | bytes 2359304 | tf_op jit(solution)/shard_map/ppermute | solution.py:1274
  624.8 24.0 %collective-permute-start.19 = (f32[128,512]{1,0:T(8,128)}, f32[128,512]{1,0:T(8,128)}, u32[]{:S(2)}, u32[]{:S(2)}) collective-permute-start(f32[128,512]{1,0:T(8,128)} %collective-permute-done.17.refs_1_), channel_id=1, source_target_pairs={{0,1},{1,0},{2,3},{3,2},{4,5},{5,4},{6,7},{7,6},{8,9},{9,8},{10,11... | collective-permute-start | bytes 786440 | tf_op jit(solution)/shard_map/ppermute | solution.py:1274
  640.1 16.3 %all-to-all-start.8 = ((f32[32,8,128]{2,1,0:T(8,128)}), f32[32,8,128]{2,1,0:T(8,128)S(1)}, u32[]{:S(2)}, u32[]{:S(2)}) async-start(f32[32,8,128]{2,1,0:T(8,128)} %get-tuple-element.142), calls=%async_computation.8 | async-start | bytes 262144 | tf_op jit(solution)/shard_map/all_to_all | solution.py:790
  645.2 241.6 %all-reduce.22.cloned.1.call-start = ((), (), s32[]{:S(2)}) async-start(), calls=%async_computation.14 | async-start | bytes 9084928 | tf_op jit(solution)/shard_map/psum | solution.py:1654
  645.2 5.3 collective-permute-start.21
  645.6 5.6 collective-permute-start.22
  646.6 17.7 %collective-permute-start.37 = (f32[128,1536]{1,0:T(8,128)}, f32[128,1536]{1,0:T(8,128)S(1)}, u32[]{:S(2)}, u32[]{:S(2)}) collective-permute-start(f32[128,1536]{1,0:T(8,128)} %collective-permute-done.35), channel_id=1, source_target_pairs={{0,1},{1,0},{2,3},{3,2},{4,5},{5,4},{6,7},{7,6},{8,9},{9,8},{10,11... | collective-permute-start | bytes 2359304 | tf_op jit(solution)/shard_map/ppermute | solution.py:1274
  648.8 14.7 %collective-permute-start.23 = (f32[128,128]{1,0:T(8,128)S(1)}, f32[128,128]{1,0:T(8,128)S(1)}, u32[]{:S(2)}, u32[]{:S(2)}) collective-permute-start(f32[128,128]{1,0:T(8,128)S(1)} %pad.74.refs_0_), channel_id=1, source_target_pairs={{0,2},{1,3},{2,0},{3,1},{4,6},{5,7},{6,4},{7,5},{8,10},{9,11},{10,... | collective-permute-start | bytes 196616 | tf_op jit(solution)/shard_map/ppermute | solution.py:1278
  650.5 13.8 %collective-permute-start.29 = (f32[128,512]{1,0:T(8,128)S(1)}, f32[128,512]{1,0:T(8,128)}, u32[]{:S(2)}, u32[]{:S(2)}) collective-permute-start(f32[128,512]{1,0:T(8,128)S(1)} %copy-done.31), channel_id=1, source_target_pairs={{0,2},{1,3},{2,0},{3,1},{4,6},{5,7},{6,4},{7,5},{8,10},{9,11},{10,... | collective-permute-start | bytes 786440 | tf_op jit(solution)/shard_map/ppermute | solution.py:1278
  651.9 16.6 %collective-permute-start.30 = (f32[128,512]{1,0:T(8,128)S(1)}, f32[128,512]{1,0:T(8,128)}, u32[]{:S(2)}, u32[]{:S(2)}) collective-permute-start(f32[128,512]{1,0:T(8,128)S(1)} %copy-done.31), channel_id=1, source_target_pairs={{0,1},{1,0},{2,3},{3,2},{4,5},{5,4},{6,7},{7,6},{8,9},{9,8},{10,11... | collective-permute-start | bytes 786440 | tf_op jit(solution)/shard_map/ppermute | solution.py:1274
  660.8 4.9 collective-permute-start.38
  663.5 9.4 collective-permute-start.32
  664.3 1.6 collective-permute-start.39
  664.3 13.5 %collective-permute-start.26 = (f32[128,512]{1,0:T(8,128)}, f32[128,512]{1,0:T(8,128)S(1)}, u32[]{:S(2)}, u32[]{:S(2)}) collective-permute-start(f32[128,512]{1,0:T(8,128)} %get-tuple-element.148.refs_4_), channel_id=1, source_target_pairs={{0,2},{1,3},{2,0},{3,1},{4,6},{5,7},{6,4},{7,5},{8,10},{9,11},{10,... | collective-permute-start | bytes 786440 | tf_op jit(solution)/shard_map/ppermute | solution.py:1278
  665.7 1.3 collective-permute-start.40
  665.9 12.6 %collective-permute-start.31 = (f32[128,512]{1,0:T(8,128)}, f32[128,512]{1,0:T(8,128)S(1)}, u32[]{:S(2)}, u32[]{:S(2)}) collective-permute-start(f32[128,512]{1,0:T(8,128)} %collective-permute-done.29.refs_1_), channel_id=1, source_target_pairs={{0,1},{1,0},{2,3},{3,2},{4,5},{5,4},{6,7},{7,6},{8,9},{9,8},{10,11... | collective-permute-start | bytes 786440 | tf_op jit(solution)/shard_map/ppermute | solution.py:1274
  667.0 12.1 %collective-permute-start.33 = (f32[128,512]{1,0:T(8,128)S(1)}, f32[128,512]{1,0:T(8,128)S(1)}, u32[]{:S(2)}, u32[]{:S(2)}) collective-permute-start(f32[128,512]{1,0:T(8,128)S(1)} %copy-done.51), channel_id=1, source_target_pairs={{0,1},{1,0},{2,3},{3,2},{4,5},{5,4},{6,7},{7,6},{8,9},{9,8},{10,11... | collective-permute-start | bytes 786440 | tf_op jit(solution)/shard_map/ppermute | solution.py:1274
  668.6 17.2 %collective-permute-start.27 = (f32[128,512]{1,0:T(8,128)}, f32[128,512]{1,0:T(8,128)S(1)}, u32[]{:S(2)}, u32[]{:S(2)}) collective-permute-start(f32[128,512]{1,0:T(8,128)} %get-tuple-element.148.refs_4_), channel_id=1, source_target_pairs={{0,1},{1,0},{2,3},{3,2},{4,5},{5,4},{6,7},{7,6},{8,9},{9,8},{10,11... | collective-permute-start | bytes 786440 | tf_op jit(solution)/shard_map/ppermute | solution.py:1274
  672.9 7.7 collective-permute-start.34
  677.8 7.9 collective-permute-start.28
  678.5 7.2 collective-permute-start.24
  679.0 6.7 collective-permute-start.25
  747.5 95.4 %all-to-all-start.9 = ((f32[8,4,128,128]{3,2,1,0:T(8,128)}), f32[8,4,128,128]{3,2,1,0:T(8,128)}, u32[]{:S(2)}, u32[]{:S(2)}) async-start(f32[8,4,128,128]{3,2,1,0:T(8,128)} %bitcast.447), calls=%async_computation.9 | async-start | bytes 4194304 | tf_op jit(solution)/shard_map/all_to_all | solution.py:1361
  837.8 2.3 collective-permute-start.41
  841.5 47.8 %collective-permute-start.42 = (f32[8,80,128]{2,1,0:T(8,128)S(1)}, f32[8,80,128]{2,1,0:T(8,128)S(1)}, u32[]{:S(2)}, u32[]{:S(2)}) collective-permute-start(f32[8,80,128]{2,1,0:T(8,128)S(1)} %select_bitcast_fusion.4), channel_id=1, source_target_pairs={{0,2},{1,3},{2,0},{3,1},{4,6},{5,7},{6,4},{7,5},{8,10},{9,11},{10,... | collective-permute-start | bytes 983048 | tf_op jit(solution)/shard_map/ppermute | solution.py:1278
  862.9 52.1 %collective-permute-start.45 = (f32[2,2560,128]{2,1,0:T(8,128)}, f32[2,2560,128]{2,1,0:T(8,128)}, u32[]{:S(2)}, u32[]{:S(2)}) collective-permute-start(f32[2,2560,128]{2,1,0:T(8,128)} %select_bitcast_fusion), channel_id=1, source_target_pairs={{0,1},{1,0},{2,3},{3,2},{4,5},{5,4},{6,7},{7,6},{8,9},{9,8},{10,11... | collective-permute-start | bytes 7864328 | tf_op jit(solution)/shard_map/ppermute | solution.py:1274
  892.6 59.4 %all-to-all-start.10 = ((f32[8,592,128]{2,1,0:T(8,128)}), f32[8,592,128]{2,1,0:T(8,128)S(1)}, u32[]{:S(2)}, u32[]{:S(2)}) async-start(f32[8,592,128]{2,1,0:T(8,128)} %pad_maximum_fusion.5), calls=%async_computation.10 | async-start | bytes 4849664 | tf_op jit(solution)/shard_map/all_to_all | solution.py:1363
  899.4 15.4 %collective-permute-start.47 = (f32[1184,128]{1,0:T(8,128)S(1)}, f32[1184,128]{1,0:T(8,128)S(1)}, u32[]{:S(2)}, u32[]{:S(2)}) collective-permute-start(f32[1184,128]{1,0:T(8,128)S(1)} %get-tuple-element.284), channel_id=1, source_target_pairs={{0,2},{1,3},{2,0},{3,1},{4,6},{5,7},{6,4},{7,5},{8,10},{9,11},{10,... | collective-permute-start | bytes 1818632 | tf_op jit(solution)/shard_map/ppermute | solution.py:1278
  914.9 6.6 collective-permute-start.48
  920.1 61.6 %collective-permute-start.46 = (f32[2560,128]{1,0:T(8,128)}, f32[2560,128]{1,0:T(8,128)}, u32[]{:S(2)}, u32[]{:S(2)}) collective-permute-start(f32[2560,128]{1,0:T(8,128)} %select_bitcast_fusion.2), channel_id=1, source_target_pairs={{0,2},{1,3},{2,0},{3,1},{4,6},{5,7},{6,4},{7,5},{8,10},{9,11},{10,... | collective-permute-start | bytes 3932168 | tf_op jit(solution)/shard_map/ppermute | solution.py:1278
  969.5 14.9 %collective-permute-start.43 = (f32[2,1792,128]{2,1,0:T(8,128)}, f32[2,1792,128]{2,1,0:T(8,128)}, u32[]{:S(2)}, u32[]{:S(2)}) collective-permute-start(f32[2,1792,128]{2,1,0:T(8,128)} %select_bitcast_fusion.1), channel_id=1, source_target_pairs={{0,1},{1,0},{2,3},{3,2},{4,5},{5,4},{6,7},{7,6},{8,9},{9,8},{10,11... | collective-permute-start | bytes 5505032 | tf_op jit(solution)/shard_map/ppermute | solution.py:1274
  971.8 35.6 %all-to-all-start.11 = ((f32[32,80,128]{2,1,0:T(8,128)}), f32[32,80,128]{2,1,0:T(8,128)}, u32[]{:S(2)}, u32[]{:S(2)}) async-start(f32[32,80,128]{2,1,0:T(8,128)} %broadcast_in_dim.26), calls=%async_computation.11 | async-start | bytes 2621440 | tf_op jit(solution)/shard_map/all_to_all | solution.py:1342
  986.4 32.7 %collective-permute-start.44 = (f32[1792,128]{1,0:T(8,128)S(1)}, f32[1792,128]{1,0:T(8,128)}, u32[]{:S(2)}, u32[]{:S(2)}) collective-permute-start(f32[1792,128]{1,0:T(8,128)S(1)} %select_bitcast_fusion.3), channel_id=1, source_target_pairs={{0,2},{1,3},{2,0},{3,1},{4,6},{5,7},{6,4},{7,5},{8,10},{9,11},{10,... | collective-permute-start | bytes 2752520 | tf_op jit(solution)/shard_map/ppermute | solution.py:1278
  (100 other events, 1566.3 us)
Sparse Core Ops, SparseCore 0:
  11.0 192.0 all-gather.12
  205.9 234.4 all-gather.10
  443.2 118.8 all-gather.6
  564.7 78.4 all-gather.8
  694.8 191.9 all-reduce.21

commit v2 on v1

--- a/solution.py
+++ b/solution.py
@@ -828,9 +828,9 @@
     )(own, *inputs, *grads, *same)
 
 
-def frame_product_kernel(pieces, *refs):
-    inputs = refs[:-3]
-    grads_ref, out_ref, total = refs[-3:]
+def frame_product_kernel(pieces, own_ref, *refs):
+    inputs = refs[:-4]
+    grads_ref, kept_ref, sent_ref, total = refs[-4:]
     step = pl.program_id(0)
 
     @pl.when(step == 0)
@@ -855,9 +855,19 @@
 
     @pl.when(step == pl.num_programs(0) - 1)
     def finish():
-        parts, _, width = out_ref.shape
-        for part in range(parts):
-            out_ref[part] = total[part * width : (part + 1) * width].T
+        width = kept_ref.shape[2]
+        core, place = own_ref[0] % 2, own_ref[0] // 2
+        for part in range(4):
+            turned = total[part * width : (part + 1) * width].T
+            across = (place + part // 2) % 2
+
+            @pl.when(core == part % 2)
+            def keep():
+                kept_ref[across] = turned
+
+            @pl.when(core != part % 2)
+            def send():
+                sent_ref[across] = turned
 
 
 def frame_product(inputs, grads, pieces):
@@ -873,14 +883,15 @@
     return pl.pallas_call(
         functools.partial(frame_product_kernel, pieces),
         grid=(sources // block,),
-        in_specs=[block_spec(array) for array in inputs]
+        in_specs=[pl.BlockSpec(memory_space=pltpu.SMEM)]
+        + [block_spec(array) for array in inputs]
         + [pl.BlockSpec((block, groups, frames, lanes), lambda step: (step, 0, 0, 0))],
-        out_specs=pl.BlockSpec((parts, depth, columns), lambda step: (0, 0, 0)),
-        out_shape=jax.ShapeDtypeStruct((parts, depth, columns), f32),
+        out_specs=[pl.BlockSpec((2, depth, columns), lambda step: (0, 0, 0))] * 2,
+        out_shape=[jax.ShapeDtypeStruct((2, depth, columns), f32)] * 2,
         scratch_shapes=[pltpu.VMEM((parts * columns, depth), f32)],
         compiler_params=params(),
         name="frame_product",
-    )(*inputs, grads)
+    )(lax.axis_index("section").astype(jnp.int32).reshape(1), *inputs, grads)
 
 
 def whole_spec(array):
@@ -1383,7 +1394,9 @@
 
 def column_gradients(inputs, pieces, received, grads):
     if received is not None:
-        return sum_section(frame_product(inputs, received, pieces))
+        kept, sent = frame_product(inputs, received, pieces)
+        pair = kept + along_core(sent)
+        return pair[0] + along_y(pair[1])
     groups, frames, width = grads.shape
     flat = grads.swapaxes(0, 1).reshape(frames, groups * width)
     parts = [

time: 1040 us -> 1040 us (level)
    all_to_all x1, waiting for transfers between devices: 28.9 us -> 6.19 us  [exchange_ring(): received = lax.all_to_all(joined, 'dp', 0, 0)]
    psum x1, waiting for transfers between devices: 22.7 us -> 43.8 us  [per_device(): group_sums = lax.psum(group_grads, 'dp')]
  transfers between devices with their start and end apart: 64 -> 64, of which waited for: 20 -> 20; matrix products, arithmetic and copies ran while one was open for 15% -> 14% of each run, Pallas kernels for 31% -> 31%
where the time goes in v2:
time: 1040 us; the launch traced here: 1030 us
  waiting for transfers between devices  419 us (40%)
  Pallas kernels  326 us (31%)
  local copies, waits for them, and re-layouts  87.3 us (8%)
  starting transfers between devices  71.4 us (7%)
  other arithmetic  63.5 us (6%)
  blocking collectives  29.1 us (3%)
  between operations  17.1 us (2%)
  matrix products  13.6 us (1%)
    all_gather x2, waiting for transfers between devices, gather_columns(): stacked = lax.all_gather(shard, both, axis=0)  188 us
    ppermute x18, waiting for transfers between devices, along_y(): lax.ppermute(values, 'section', [(place, place ^ 2) for place in range(4)])  125 us
    pallas_call x1, Pallas kernels, attention_backward(): pl.pallas_call(functools.partial(attention_backward_kernel, blocks, rows,...  70.4 us
    pallas_call x1, Pallas kernels, decoder_backward(): pl.pallas_call(functools.partial(decoder_backward_kernel, blocks, rows, l...  52.5 us
    pallas_call x1, Pallas kernels, attention_forward(): pl.pallas_call(functools.partial(attention_forward_kernel, blocks, rows,...  49.6 us
    psum x1, waiting for transfers between devices, per_device(): group_sums = lax.psum(group_grads, 'dp')  43.8 us
    pallas_call x10, Pallas kernels, post_call(): pl.pallas_call(kernel, in_specs=in_specs, out_specs=[pl.BlockSpec(memory_...  41.7 us
    pallas_call x1, Pallas kernels, decoder_forward(): pl.pallas_call(functools.partial(decoder_forward_kernel, blocks, rows, la...  37.4 us
  transfers between devices with their start and end apart: 64, of which 20 were waited for; matrix products, arithmetic and copies ran while one was open for 14% of the time, Pallas kernels for 31%

profile of v2, /device:TPU:0, one launch (start us, length us, event | category | flops | bytes accessed | tf_op | source)
XLA Modules:
  0.0 1027.3 jit_solution(5951368054011762253)
XLA Ops:
  8.8 3.0 collective-permute-start
  16.2 4.2 copy.143
  27.5 98.2 %collective-permute-done = f32[7680,128]{1,0:T(8,128)} collective-permute-done((f32[7680,128]{1,0:T(8,128)}, f32[7680,128]{1,0:T(8,128)}, u32[]{:S(2)}, u32[]{:S(2)}) %collective-permute-start) | collective-permute-done | bytes 3932192 | tf_op jit(solution)/shard_map/ppermute | solution.py:1289
  125.7 5.9 pad_maximum_fusion.1.awaited
  131.5 71.5 %all-gather.13.cloned.1.call-done = f32[57344,128]{1,0:T(8,128)} async-done(((f32[1792,128]{1,0:T(8,128)}), f32[57344,128]{1,0:T(8,128)}) %all-gather.13.cloned.1.call-update) | async-done | bytes 29360144 | tf_op jit(solution)/shard_map/all_gather | solution.py:1278
  203.1 49.6 %attention_forward.1 = (f32[6,32,1024]{2,1,0:T(8,128)}, f32[6,32,1024]{2,1,0:T(8,128)}, f32[6,32,512]{2,1,0:T(8,128)}, f32[6,32,4096]{2,1,0:T(8,128)}, f32[6,32,...) custom-call(f32[32,1792,128]{2,1,0:T(8,128)} %bitcast.360, f32[128,256]{1,0:T(8,128)} %copy-done.43, ...), custom_call_target="tpu_custom_call" | custom-call | flops 45097156608 | bytes 29360128 | tf_op jit(solution)/shard_map/attention_forward/pallas_call | solution.py:966
  262.7 10.8 %pad_maximum_fusion = f32[4,7680,128]{2,1,0:T(8,128)} fusion(f32[2,7680,128]{2,1,0:T(8,128)} %collective-permute-done.1, f32[1,7680,128]{2,1,0:T(8,128)} %bitcast.52, f32[1,7680,128]{2,1,0:T(8,128)} %bitcast.391), kind=kLoop, calls=%fused_computation | loop fusion | flops 7864320 | bytes 31457280 | tf_op jit(solution)/shard_map/concatenate | solution.py:1297
  273.5 11.5 %fusion.116 = (f32[4,2560,128]{2,1,0:T(8,128)}, f32[4,2560,128]{2,1,0:T(8,128)}, f32[4,2560,128]{2,1,0:T(8,128)}) fusion(f32[4,7680,128]{2,1,0:T(8,128)} %pad_maximum_fusion), kind=kLoop, calls=%fused_computation.296 | loop fusion | bytes 31457280 | tf_op jit(solution)/shard_map/slice | solution.py:1324
  285.0 6.8 dynamic-slice_bitcast_fusion.3
  291.8 2.7 pad_maximum_fusion.4.values_ref
  294.4 5.2 split_matrix.8
  299.6 5.2 pad_maximum_fusion.3.values_ref
  304.8 5.4 split_matrix.7
  310.2 2.8 dynamic-slice_bitcast_fusion.11
  313.1 2.7 pad_maximum_fusion.2.values_ref
  315.7 6.8 split_matrix.6
  323.5 117.0 %all-gather.11.cloned.1.call-done = f32[81920,128]{1,0:T(8,128)} async-done(((f32[2560,128]{1,0:T(8,128)}), f32[81920,128]{1,0:T(8,128)}) %all-gather.11.cloned.1.call-update) | async-done | bytes 41943056 | tf_op jit(solution)/shard_map/all_gather | solution.py:1278
  440.4 37.4 %decoder_forward.1 = (f32[6,32,1024]{2,1,0:T(8,128)}, f32[6,32,1024]{2,1,0:T(8,128)}, f32[6,32,4096]{2,1,0:T(8,128)}) custom-call(f32[32,2560,128]{2,1,0:T(8,128)} %bitcast.465, f32[128,1536]{1,0:T(8,128)} %pad_maximum_fusion.8.frames_ref, f32[8,1,512]{2,1,0:T(1,128)} %bitcast.472, s32[8,4,16,1024]{3,2,1,0:T(8,128)} %bitcast.364, ...), custom_call_target="tpu_custom_call" | custom-call | flops 32212254720 | bytes 41943040 | tf_op jit(solution)/shard_map/decoder_forward/pallas_call | solution.py:1042
  482.0 2.7 post_first.1
  484.7 3.4 all-to-all-start
  489.3 10.1 all-to-all-done.sums_ref
  500.1 4.8 post_next.4
  504.8 14.0 %all_to_all.60.sums_ref = f32[32,8,128]{2,1,0:T(8,128)} all-to-all(f32[32,8,128]{2,1,0:T(8,128)} %get-tuple-element.118), channel_id=1, replica_groups=mesh['dp'=8,'section'=4] {'dp','section'}, dimensions={0} | all-to-all | bytes 262144 | tf_op jit(solution)/shard_map/all_to_all | solution.py:790
  518.8 4.7 post_next.5
  523.5 15.2 %all_to_all.61.sums_ref = f32[32,8,128]{2,1,0:T(8,128)} all-to-all(f32[32,8,128]{2,1,0:T(8,128)} %get-tuple-element.120), channel_id=1, replica_groups=mesh['dp'=8,'section'=4] {'dp','section'}, dimensions={0} | all-to-all | bytes 262144 | tf_op jit(solution)/shard_map/all_to_all | solution.py:790
  538.7 4.8 post_next.6
  546.6 8.9 all-to-all-done.3.sums_ref
  556.2 2.9 post_next.7
  559.1 4.7 all-to-all-start.4
  565.9 6.2 all-to-all-done.4.sums_ref
  572.8 3.1 post_turn.1
  575.8 2.6 all-to-all-start.5
  580.5 4.4 collective-permute-done.8.refs_9_
  589.2 5.4 post_back.4
  594.6 5.2 all-to-all-start.6
  605.8 2.9 tap_gradient.5.refs_2_
  611.2 5.4 post_back.5
  616.6 3.4 all-to-all-start.7
  625.3 4.4 tap_gradient.6.refs_2_
  629.6 4.6 all-to-all-done.7.sums_ref
  634.9 5.3 post_back.6
  640.2 5.1 all-to-all-start.8
  652.1 4.4 tap_gradient.7.refs_0_
  657.2 2.7 post_back.7
  669.1 3.9 collective-permute-done.32.refs_5_
  673.1 4.9 collective-permute-done.26.refs_5_
  681.5 4.4 tap_gradient.9
  687.3 2.9 tap_gradient.8
  690.2 4.6 join_rows.1
  694.9 52.5 %decoder_backward.1 = (f32[32,128,128]{2,1,0:T(8,128)}, f32[128,1536]{1,0:T(8,128)}) custom-call(f32[32,2560,128]{2,1,0:T(8,128)} %bitcast.466, f32[32,2560,128]{2,1,0:T(8,128)} %bitcast.467, f32[32,2560,128]{2,1,0:T(8,128)} %bitcast.468, f32[32,2560,128]{2,1,0:T(8,128)} %bitcast.469, f32[32,2560,128]{2,1,0:T(8,128)} %bitcast.470, ...), custom_call_target="tpu_custom_call" | custom-call | flops 257698037760 | bytes 41943040 | tf_op jit(solution)/shard_map/decoder_backward/pallas_call | solution.py:1111
  749.7 6.0 all-to-all-start.9
  755.8 70.4 %attention_backward.1 = (f32[32,128,128]{2,1,0:T(8,128)}, f32[1,4096]{1,0:T(1,128)}, f32[128,256]{1,0:T(8,128)}, f32[128,128]{1,0:T(8,128)}, f32[16,4096]{1,0:T(...) custom-call(f32[32,1792,128]{2,1,0:T(8,128)} %bitcast.361, ...), custom_call_target="tpu_custom_call" | custom-call | flops 16777216 | bytes 65536 | tf_op jit(solution)/shard_map/attention_backward/pallas_call | solution.py:1196
  844.0 43.8 %all-reduce.22.cloned.1.call-done = f32[8872,128]{1,0:T(8,128)} async-done(((f32[8872,128]{1,0:T(8,128)}), f32[8872,128]{1,0:T(8,128)}) %all-reduce.22.cloned.1.call-update) | async-done | bytes 4542480 | tf_op jit(solution)/shard_map/psum | solution.py:1667
  890.4 3.1 pad_maximum_fusion.5
  893.5 4.4 all-to-all-start.10
  898.0 16.3 %frame_product.3 = (f32[2,2560,128]{2,1,0:T(8,128)}, f32[2,2560,128]{2,1,0:T(8,128)}) custom-call(s32[1]{0:T(128)} %bitcast.81.own_ref, f32[1024,1792]{1,0:T(8,128)} %all-gather.7.cloned.1.call-done.refs_7_.refs_0_, f32[1024,1024]{1,0:T(8,128)} %all-gather.9.cloned.1.call-done.refs_8_.refs_1_, f32[8,4,128,128]{3,2,1,0:T(8,128)} %all-to-all-done.9.refs_2_), custom_call_target="tpu_custom_call" | custom-call | tf_op jit(solution)/shard_map/frame_product/pallas_call | solution.py:883
  919.8 13.3 %collective-permute-done.47 = f32[1184,128]{1,0:T(8,128)S(1)} collective-permute-done((f32[1184,128]{1,0:T(8,128)S(1)}, f32[1184,128]{1,0:T(8,128)S(1)}, u32[]{:S(2)}, u32[]{:S(2)}) %collective-permute-start.47) | collective-permute-done | bytes 606240 | tf_op jit(solution)/shard_map/ppermute | solution.py:1289
  936.0 4.4 slice.713
  947.2 6.2 all-to-all-done.10
  953.4 3.0 slice.697
  956.4 12.3 %frame_product.2 = (f32[2,1792,128]{2,1,0:T(8,128)}, f32[2,1792,128]{2,1,0:T(8,128)}) custom-call(s32[1]{0:T(128)} %bitcast.81.own_ref, f32[1024,1792]{1,0:T(8,128)} %all-gather.7.cloned.1.call-done.refs_7_.refs_0_, f32[8,4,128,128]{3,2,1,0:T(8,128)} %bitcast.407), custom_call_target="tpu_custom_call" | custom-call | tf_op jit(solution)/shard_map/frame_product/pallas_call | solution.py:883
  970.9 3.8 all-to-all-start.11
  982.6 2.7 fusion
  988.9 17.7 %all-to-all-done.11 = f32[32,80,128]{2,1,0:T(8,128)} async-done(((f32[32,80,128]{2,1,0:T(8,128)}), f32[32,80,128]{2,1,0:T(8,128)}, u32[]{:S(2)}, u32[]{:S(2)}) %all-to-all-start.11) | async-done | bytes 1310752 | tf_op jit(solution)/shard_map/all_to_all | solution.py:1353
  (487 shorter events, 141.7 us)
Async XLA Ops:
  7.2 195.8 %all-gather.13.cloned.1.call-start = ((), (), s32[]{:S(2)}) async-start(), calls=%async_computation.16 | async-start | bytes 30277632 | tf_op jit(solution)/shard_map/all_gather | solution.py:1278
  8.0 432.4 %all-gather.11.cloned.1.call-start = ((), (), s32[]{:S(2)}) async-start(), calls=%async_computation.15 | async-start | bytes 43253760 | tf_op jit(solution)/shard_map/all_gather | solution.py:1278
  8.7 681.5 %all-gather.7.cloned.1.call-start = ((), (), s32[]{:S(2)}) async-start(), calls=%async_computation.12 | async-start | bytes 8257536 | tf_op jit(solution)/shard_map/all_gather | solution.py:1550
  8.8 116.9 %collective-permute-start = (f32[7680,128]{1,0:T(8,128)}, f32[7680,128]{1,0:T(8,128)}, u32[]{:S(2)}, u32[]{:S(2)}) collective-permute-start(f32[7680,128]{1,0:T(8,128)} %bitcast.390), channel_id=1, source_target_pairs={{0,2},{1,3},{2,0},{3,1},{4,6},{5,7},{6,4},{7,5},{8,10},{9,11},{10,... | collective-permute-start | bytes 11796488 | tf_op jit(solution)/shard_map/ppermute | solution.py:1289
  131.5 131.1 %collective-permute-start.1 = (f32[2,7680,128]{2,1,0:T(8,128)}, f32[2,7680,128]{2,1,0:T(8,128)}, u32[]{:S(2)}, u32[]{:S(2)}) collective-permute-start(f32[2,7680,128]{2,1,0:T(8,128)} %pad_maximum_fusion.1.awaited), channel_id=1, source_target_pairs={{0,1},{1,0},{2,3},{3,2},{4,5},{5,4},{6,7},{7,6},{8,9},{9,8},{10,11... | collective-permute-start | bytes 23592968 | tf_op jit(solution)/shard_map/ppermute | solution.py:1285
  256.2 434.0 %all-gather.9.cloned.1.call-start = ((), (), s32[]{:S(2)}) async-start(), calls=%async_computation.13 | async-start | bytes 4718592 | tf_op jit(solution)/shard_map/all_gather | solution.py:1551
  484.7 14.8 %all-to-all-start = ((f32[32,8,128]{2,1,0:T(8,128)}), f32[32,8,128]{2,1,0:T(8,128)S(1)}, u32[]{:S(2)}, u32[]{:S(2)}) async-start(f32[32,8,128]{2,1,0:T(8,128)} %get-tuple-element.116), calls=%async_computation | async-start | bytes 262144 | tf_op jit(solution)/shard_map/all_to_all | solution.py:790
  543.4 12.1 %all-to-all-start.3 = ((f32[32,8,128]{2,1,0:T(8,128)}), f32[32,8,128]{2,1,0:T(8,128)S(1)}, u32[]{:S(2)}, u32[]{:S(2)}) async-start(f32[32,8,128]{2,1,0:T(8,128)} %get-tuple-element.122), calls=%async_computation.3 | async-start | bytes 262144 | tf_op jit(solution)/shard_map/all_to_all | solution.py:790
  559.1 13.0 %all-to-all-start.4 = ((f32[32,8,128]{2,1,0:T(8,128)}), f32[32,8,128]{2,1,0:T(8,128)S(1)}, u32[]{:S(2)}, u32[]{:S(2)}) async-start(f32[32,8,128]{2,1,0:T(8,128)} %get-tuple-element.124), calls=%async_computation.4 | async-start | bytes 262144 | tf_op jit(solution)/shard_map/all_to_all | solution.py:790
  563.8 24.2 %collective-permute-start.2 = (f32[128,512]{1,0:T(8,128)}, f32[128,512]{1,0:T(8,128)S(1)}, u32[]{:S(2)}, u32[]{:S(2)}) collective-permute-start(f32[128,512]{1,0:T(8,128)} %get-tuple-element.125.active_ref.refs_0_), channel_id=1, source_target_pairs={{0,2},{1,3},{2,0},{3,1},{4,6},{5,7},{6,4},{7,5},{8,10},{9,11},{10,... | collective-permute-start | bytes 786440 | tf_op jit(solution)/shard_map/ppermute | solution.py:1289
  565.6 34.2 %collective-permute-start.11 = (f32[128,512]{1,0:T(8,128)}, f32[128,512]{1,0:T(8,128)}, u32[]{:S(2)}, u32[]{:S(2)}) collective-permute-start(f32[128,512]{1,0:T(8,128)} %get-tuple-element.131.refs_0_), channel_id=1, source_target_pairs={{0,2},{1,3},{2,0},{3,1},{4,6},{5,7},{6,4},{7,5},{8,10},{9,11},{10,... | collective-permute-start | bytes 786440 | tf_op jit(solution)/shard_map/ppermute | solution.py:1289
  565.9 35.8 %collective-permute-start.3 = (f32[128,512]{1,0:T(8,128)}, f32[128,512]{1,0:T(8,128)}, u32[]{:S(2)}, u32[]{:S(2)}) collective-permute-start(f32[128,512]{1,0:T(8,128)} %get-tuple-element.125.active_ref.refs_0_), channel_id=1, source_target_pairs={{0,1},{1,0},{2,3},{3,2},{4,5},{5,4},{6,7},{7,6},{8,9},{9,8},{10,11... | collective-permute-start | bytes 786440 | tf_op jit(solution)/shard_map/ppermute | solution.py:1285
  575.8 12.8 %all-to-all-start.5 = ((f32[32,8,128]{2,1,0:T(8,128)}), f32[32,8,128]{2,1,0:T(8,128)S(1)}, u32[]{:S(2)}, u32[]{:S(2)}) async-start(f32[32,8,128]{2,1,0:T(8,128)} %get-tuple-element.129), calls=%async_computation.5 | async-start | bytes 262144 | tf_op jit(solution)/shard_map/all_to_all | solution.py:790
  578.4 9.2 collective-permute-start.5
  580.1 4.8 collective-permute-start.8
  584.9 1.3 collective-permute-start.9
  586.2 1.3 collective-permute-start.10
  587.5 14.2 %collective-permute-start.6 = (f32[128,128]{1,0:T(8,128)}, f32[128,128]{1,0:T(8,128)S(1)}, u32[]{:S(2)}, u32[]{:S(2)}) collective-permute-start(f32[128,128]{1,0:T(8,128)} %get-tuple-element.138.refs_4_), channel_id=1, source_target_pairs={{0,1},{1,0},{2,3},{3,2},{4,5},{5,4},{6,7},{7,6},{8,9},{9,8},{10,11... | collective-permute-start | bytes 196616 | tf_op jit(solution)/shard_map/ppermute | solution.py:1285
  587.6 14.5 %collective-permute-start.7 = (f32[128,128]{1,0:T(8,128)S(1)}, f32[128,128]{1,0:T(8,128)}, u32[]{:S(2)}, u32[]{:S(2)}) collective-permute-start(f32[128,128]{1,0:T(8,128)S(1)} %collective-permute-done.5.refs_5_), channel_id=1, source_target_pairs={{0,1},{1,0},{2,3},{3,2},{4,5},{5,4},{6,7},{7,6},{8,9},{9,8},{10,11... | collective-permute-start | bytes 196616 | tf_op jit(solution)/shard_map/ppermute | solution.py:1285
  588.0 15.9 %collective-permute-start.4 = (f32[128,512]{1,0:T(8,128)S(1)}, f32[128,512]{1,0:T(8,128)}, u32[]{:S(2)}, u32[]{:S(2)}) collective-permute-start(f32[128,512]{1,0:T(8,128)S(1)} %collective-permute-done.2.refs_1_), channel_id=1, source_target_pairs={{0,1},{1,0},{2,3},{3,2},{4,5},{5,4},{6,7},{7,6},{8,9},{9,8},{10,11... | collective-permute-start | bytes 786440 | tf_op jit(solution)/shard_map/ppermute | solution.py:1285
  594.6 15.9 %all-to-all-start.6 = ((f32[32,8,128]{2,1,0:T(8,128)}), f32[32,8,128]{2,1,0:T(8,128)S(1)}, u32[]{:S(2)}, u32[]{:S(2)}) async-start(f32[32,8,128]{2,1,0:T(8,128)} %get-tuple-element.134), calls=%async_computation.6 | async-start | bytes 262144 | tf_op jit(solution)/shard_map/all_to_all | solution.py:790
  599.8 20.2 %collective-permute-start.17 = (f32[128,512]{1,0:T(8,128)}, f32[128,512]{1,0:T(8,128)}, u32[]{:S(2)}, u32[]{:S(2)}) collective-permute-start(f32[128,512]{1,0:T(8,128)} %get-tuple-element.136.refs_0_), channel_id=1, source_target_pairs={{0,2},{1,3},{2,0},{3,1},{4,6},{5,7},{6,4},{7,5},{8,10},{9,11},{10,... | collective-permute-start | bytes 786440 | tf_op jit(solution)/shard_map/ppermute | solution.py:1289
  601.6 18.8 %collective-permute-start.12 = (f32[128,512]{1,0:T(8,128)}, f32[128,512]{1,0:T(8,128)}, u32[]{:S(2)}, u32[]{:S(2)}) collective-permute-start(f32[128,512]{1,0:T(8,128)} %get-tuple-element.131.refs_0_), channel_id=1, source_target_pairs={{0,1},{1,0},{2,3},{3,2},{4,5},{5,4},{6,7},{7,6},{8,9},{9,8},{10,11... | collective-permute-start | bytes 786440 | tf_op jit(solution)/shard_map/ppermute | solution.py:1285
  601.7 18.9 %collective-permute-start.13 = (f32[128,512]{1,0:T(8,128)}, f32[128,512]{1,0:T(8,128)}, u32[]{:S(2)}, u32[]{:S(2)}) collective-permute-start(f32[128,512]{1,0:T(8,128)} %collective-permute-done.11.refs_1_), channel_id=1, source_target_pairs={{0,1},{1,0},{2,3},{3,2},{4,5},{5,4},{6,7},{7,6},{8,9},{9,8},{10,11... | collective-permute-start | bytes 786440 | tf_op jit(solution)/shard_map/ppermute | solution.py:1285
  602.2 20.3 %collective-permute-start.14 = (f32[128,512]{1,0:T(8,128)}, f32[128,512]{1,0:T(8,128)}, u32[]{:S(2)}, u32[]{:S(2)}) collective-permute-start(f32[128,512]{1,0:T(8,128)} %get-tuple-element.144.refs_4_), channel_id=1, source_target_pairs={{0,2},{1,3},{2,0},{3,1},{4,6},{5,7},{6,4},{7,5},{8,10},{9,11},{10,... | collective-permute-start | bytes 786440 | tf_op jit(solution)/shard_map/ppermute | solution.py:1289
  603.9 42.8 %collective-permute-start.35 = (f32[128,1536]{1,0:T(8,128)}, f32[128,1536]{1,0:T(8,128)}, u32[]{:S(2)}, u32[]{:S(2)}) collective-permute-start(f32[128,1536]{1,0:T(8,128)} %get-tuple-element.285), channel_id=1, source_target_pairs={{0,2},{1,3},{2,0},{3,1},{4,6},{5,7},{6,4},{7,5},{8,10},{9,11},{10,... | collective-permute-start | bytes 2359304 | tf_op jit(solution)/shard_map/ppermute | solution.py:1289
  616.6 17.7 %all-to-all-start.7 = ((f32[32,8,128]{2,1,0:T(8,128)}), f32[32,8,128]{2,1,0:T(8,128)S(1)}, u32[]{:S(2)}, u32[]{:S(2)}) async-start(f32[32,8,128]{2,1,0:T(8,128)} %get-tuple-element.140), calls=%async_computation.7 | async-start | bytes 262144 | tf_op jit(solution)/shard_map/all_to_all | solution.py:790
  620.0 25.4 %collective-permute-start.18 = (f32[128,512]{1,0:T(8,128)}, f32[128,512]{1,0:T(8,128)}, u32[]{:S(2)}, u32[]{:S(2)}) collective-permute-start(f32[128,512]{1,0:T(8,128)} %get-tuple-element.136.refs_0_), channel_id=1, source_target_pairs={{0,1},{1,0},{2,3},{3,2},{4,5},{5,4},{6,7},{7,6},{8,9},{9,8},{10,11... | collective-permute-start | bytes 786440 | tf_op jit(solution)/shard_map/ppermute | solution.py:1285
  620.4 3.6 collective-permute-start.15
  620.6 25.1 %collective-permute-start.20 = (f32[128,512]{1,0:T(8,128)}, f32[128,512]{1,0:T(8,128)}, u32[]{:S(2)}, u32[]{:S(2)}) collective-permute-start(f32[128,512]{1,0:T(8,128)} %get-tuple-element.148.refs_4_), channel_id=1, source_target_pairs={{0,2},{1,3},{2,0},{3,1},{4,6},{5,7},{6,4},{7,5},{8,10},{9,11},{10,... | collective-permute-start | bytes 786440 | tf_op jit(solution)/shard_map/ppermute | solution.py:1289
  622.5 2.8 collective-permute-start.16
  624.8 36.2 %collective-permute-start.36 = (f32[128,1536]{1,0:T(8,128)}, f32[128,1536]{1,0:T(8,128)}, u32[]{:S(2)}, u32[]{:S(2)}) collective-permute-start(f32[128,1536]{1,0:T(8,128)} %get-tuple-element.285), channel_id=1, source_target_pairs={{0,1},{1,0},{2,3},{3,2},{4,5},{5,4},{6,7},{7,6},{8,9},{9,8},{10,11... | collective-permute-start | bytes 2359304 | tf_op jit(solution)/shard_map/ppermute | solution.py:1285
  625.3 23.7 %collective-permute-start.19 = (f32[128,512]{1,0:T(8,128)}, f32[128,512]{1,0:T(8,128)}, u32[]{:S(2)}, u32[]{:S(2)}) collective-permute-start(f32[128,512]{1,0:T(8,128)} %collective-permute-done.17.refs_1_), channel_id=1, source_target_pairs={{0,1},{1,0},{2,3},{3,2},{4,5},{5,4},{6,7},{7,6},{8,9},{9,8},{10,11... | collective-permute-start | bytes 786440 | tf_op jit(solution)/shard_map/ppermute | solution.py:1285
  640.2 16.3 %all-to-all-start.8 = ((f32[32,8,128]{2,1,0:T(8,128)}), f32[32,8,128]{2,1,0:T(8,128)S(1)}, u32[]{:S(2)}, u32[]{:S(2)}) async-start(f32[32,8,128]{2,1,0:T(8,128)} %get-tuple-element.146), calls=%async_computation.8 | async-start | bytes 262144 | tf_op jit(solution)/shard_map/all_to_all | solution.py:790
  645.3 242.5 %all-reduce.22.cloned.1.call-start = ((), (), s32[]{:S(2)}) async-start(), calls=%async_computation.14 | async-start | bytes 9084928 | tf_op jit(solution)/shard_map/psum | solution.py:1667
  645.4 5.3 collective-permute-start.21
  645.7 5.7 collective-permute-start.22
  646.7 17.7 %collective-permute-start.37 = (f32[128,1536]{1,0:T(8,128)}, f32[128,1536]{1,0:T(8,128)S(1)}, u32[]{:S(2)}, u32[]{:S(2)}) collective-permute-start(f32[128,1536]{1,0:T(8,128)} %collective-permute-done.35), channel_id=1, source_target_pairs={{0,1},{1,0},{2,3},{3,2},{4,5},{5,4},{6,7},{7,6},{8,9},{9,8},{10,11... | collective-permute-start | bytes 2359304 | tf_op jit(solution)/shard_map/ppermute | solution.py:1285
  649.0 14.7 %collective-permute-start.23 = (f32[128,128]{1,0:T(8,128)S(1)}, f32[128,128]{1,0:T(8,128)S(1)}, u32[]{:S(2)}, u32[]{:S(2)}) collective-permute-start(f32[128,128]{1,0:T(8,128)S(1)} %pad.74.refs_0_), channel_id=1, source_target_pairs={{0,2},{1,3},{2,0},{3,1},{4,6},{5,7},{6,4},{7,5},{8,10},{9,11},{10,... | collective-permute-start | bytes 196616 | tf_op jit(solution)/shard_map/ppermute | solution.py:1289
  650.6 13.8 %collective-permute-start.29 = (f32[128,512]{1,0:T(8,128)S(1)}, f32[128,512]{1,0:T(8,128)}, u32[]{:S(2)}, u32[]{:S(2)}) collective-permute-start(f32[128,512]{1,0:T(8,128)S(1)} %copy-done.32), channel_id=1, source_target_pairs={{0,2},{1,3},{2,0},{3,1},{4,6},{5,7},{6,4},{7,5},{8,10},{9,11},{10,... | collective-permute-start | bytes 786440 | tf_op jit(solution)/shard_map/ppermute | solution.py:1289
  652.1 16.6 %collective-permute-start.30 = (f32[128,512]{1,0:T(8,128)S(1)}, f32[128,512]{1,0:T(8,128)}, u32[]{:S(2)}, u32[]{:S(2)}) collective-permute-start(f32[128,512]{1,0:T(8,128)S(1)} %copy-done.32), channel_id=1, source_target_pairs={{0,1},{1,0},{2,3},{3,2},{4,5},{5,4},{6,7},{7,6},{8,9},{9,8},{10,11... | collective-permute-start | bytes 786440 | tf_op jit(solution)/shard_map/ppermute | solution.py:1285
  661.0 4.9 collective-permute-start.38
  663.6 9.4 collective-permute-start.32
  664.4 1.6 collective-permute-start.39
  664.4 13.5 %collective-permute-start.26 = (f32[128,512]{1,0:T(8,128)}, f32[128,512]{1,0:T(8,128)S(1)}, u32[]{:S(2)}, u32[]{:S(2)}) collective-permute-start(f32[128,512]{1,0:T(8,128)} %get-tuple-element.152.refs_4_), channel_id=1, source_target_pairs={{0,2},{1,3},{2,0},{3,1},{4,6},{5,7},{6,4},{7,5},{8,10},{9,11},{10,... | collective-permute-start | bytes 786440 | tf_op jit(solution)/shard_map/ppermute | solution.py:1289
  665.8 1.3 collective-permute-start.40
  666.0 12.6 %collective-permute-start.31 = (f32[128,512]{1,0:T(8,128)}, f32[128,512]{1,0:T(8,128)S(1)}, u32[]{:S(2)}, u32[]{:S(2)}) collective-permute-start(f32[128,512]{1,0:T(8,128)} %collective-permute-done.29.refs_1_), channel_id=1, source_target_pairs={{0,1},{1,0},{2,3},{3,2},{4,5},{5,4},{6,7},{7,6},{8,9},{9,8},{10,11... | collective-permute-start | bytes 786440 | tf_op jit(solution)/shard_map/ppermute | solution.py:1285
  667.1 12.1 %collective-permute-start.33 = (f32[128,512]{1,0:T(8,128)S(1)}, f32[128,512]{1,0:T(8,128)S(1)}, u32[]{:S(2)}, u32[]{:S(2)}) collective-permute-start(f32[128,512]{1,0:T(8,128)S(1)} %copy-done.52), channel_id=1, source_target_pairs={{0,1},{1,0},{2,3},{3,2},{4,5},{5,4},{6,7},{7,6},{8,9},{9,8},{10,11... | collective-permute-start | bytes 786440 | tf_op jit(solution)/shard_map/ppermute | solution.py:1285
  668.7 17.2 %collective-permute-start.27 = (f32[128,512]{1,0:T(8,128)}, f32[128,512]{1,0:T(8,128)S(1)}, u32[]{:S(2)}, u32[]{:S(2)}) collective-permute-start(f32[128,512]{1,0:T(8,128)} %get-tuple-element.152.refs_4_), channel_id=1, source_target_pairs={{0,1},{1,0},{2,3},{3,2},{4,5},{5,4},{6,7},{7,6},{8,9},{9,8},{10,11... | collective-permute-start | bytes 786440 | tf_op jit(solution)/shard_map/ppermute | solution.py:1285
  673.1 7.7 collective-permute-start.34
  678.0 7.9 collective-permute-start.28
  678.7 7.2 collective-permute-start.24
  679.2 6.7 collective-permute-start.25
  749.7 93.0 %all-to-all-start.9 = ((f32[8,4,128,128]{3,2,1,0:T(8,128)}), f32[8,4,128,128]{3,2,1,0:T(8,128)}, u32[]{:S(2)}, u32[]{:S(2)}) async-start(f32[8,4,128,128]{3,2,1,0:T(8,128)} %bitcast.111), calls=%async_computation.9 | async-start | bytes 4194304 | tf_op jit(solution)/shard_map/all_to_all | solution.py:1372
  838.2 2.2 collective-permute-start.41
  841.6 48.7 %collective-permute-start.42 = (f32[8,80,128]{2,1,0:T(8,128)S(1)}, f32[8,80,128]{2,1,0:T(8,128)S(1)}, u32[]{:S(2)}, u32[]{:S(2)}) collective-permute-start(f32[8,80,128]{2,1,0:T(8,128)S(1)} %select_bitcast_fusion), channel_id=1, source_target_pairs={{0,2},{1,3},{2,0},{3,1},{4,6},{5,7},{6,4},{7,5},{8,10},{9,11},{10,... | collective-permute-start | bytes 983048 | tf_op jit(solution)/shard_map/ppermute | solution.py:1289
  893.5 59.9 %all-to-all-start.10 = ((f32[8,592,128]{2,1,0:T(8,128)}), f32[8,592,128]{2,1,0:T(8,128)}, u32[]{:S(2)}, u32[]{:S(2)}) async-start(f32[8,592,128]{2,1,0:T(8,128)} %pad_maximum_fusion.5), calls=%async_computation.10 | async-start | bytes 4849664 | tf_op jit(solution)/shard_map/all_to_all | solution.py:1374
  914.2 26.8 %collective-permute-start.45 = (f32[2,2560,128]{2,1,0:T(8,128)}, f32[2,2560,128]{2,1,0:T(8,128)}, u32[]{:S(2)}, u32[]{:S(2)}) collective-permute-start(f32[2,2560,128]{2,1,0:T(8,128)} %get-tuple-element.174), channel_id=1, source_target_pairs={{0,1},{1,0},{2,3},{3,2},{4,5},{5,4},{6,7},{7,6},{8,9},{9,8},{10,11... | collective-permute-start | bytes 7864328 | tf_op jit(solution)/shard_map/ppermute | solution.py:1285
  917.0 16.1 %collective-permute-start.47 = (f32[1184,128]{1,0:T(8,128)S(1)}, f32[1184,128]{1,0:T(8,128)S(1)}, u32[]{:S(2)}, u32[]{:S(2)}) collective-permute-start(f32[1184,128]{1,0:T(8,128)S(1)} %get-tuple-element.292), channel_id=1, source_target_pairs={{0,2},{1,3},{2,0},{3,1},{4,6},{5,7},{6,4},{7,5},{8,10},{9,11},{10,... | collective-permute-start | bytes 1818632 | tf_op jit(solution)/shard_map/ppermute | solution.py:1289
  934.4 40.2 %collective-permute-start.48 = (f32[2,1184,128]{2,1,0:T(8,128)}, f32[2,1184,128]{2,1,0:T(8,128)}, u32[]{:S(2)}, u32[]{:S(2)}) collective-permute-start(f32[2,1184,128]{2,1,0:T(8,128)} %pad_maximum_fusion.9), channel_id=1, source_target_pairs={{0,1},{1,0},{2,3},{3,2},{4,5},{5,4},{6,7},{7,6},{8,9},{9,8},{10,11... | collective-permute-start | bytes 3637256 | tf_op jit(solution)/shard_map/ppermute | solution.py:1285
  945.7 36.9 %collective-permute-start.46 = (f32[2560,128]{1,0:T(8,128)}, f32[2560,128]{1,0:T(8,128)}, u32[]{:S(2)}, u32[]{:S(2)}) collective-permute-start(f32[2560,128]{1,0:T(8,128)} %slice_bitcast_fusion), channel_id=1, source_target_pairs={{0,2},{1,3},{2,0},{3,1},{4,6},{5,7},{6,4},{7,5},{8,10},{9,11},{10,... | collective-permute-start | bytes 3932168 | tf_op jit(solution)/shard_map/ppermute | solution.py:1289
  968.7 16.6 %collective-permute-start.43 = (f32[2,1792,128]{2,1,0:T(8,128)}, f32[2,1792,128]{2,1,0:T(8,128)}, u32[]{:S(2)}, u32[]{:S(2)}) collective-permute-start(f32[2,1792,128]{2,1,0:T(8,128)} %get-tuple-element.172), channel_id=1, source_target_pairs={{0,1},{1,0},{2,3},{3,2},{4,5},{5,4},{6,7},{7,6},{8,9},{9,8},{10,11... | collective-permute-start | bytes 5505032 | tf_op jit(solution)/shard_map/ppermute | solution.py:1285
  970.9 35.7 %all-to-all-start.11 = ((f32[32,80,128]{2,1,0:T(8,128)}), f32[32,80,128]{2,1,0:T(8,128)}, u32[]{:S(2)}, u32[]{:S(2)}) async-start(f32[32,80,128]{2,1,0:T(8,128)} %broadcast_in_dim.26), calls=%async_computation.11 | async-start | bytes 2621440 | tf_op jit(solution)/shard_map/all_to_all | solution.py:1353
  987.1 31.2 %collective-permute-start.44 = (f32[1792,128]{1,0:T(8,128)S(1)}, f32[1792,128]{1,0:T(8,128)}, u32[]{:S(2)}, u32[]{:S(2)}) collective-permute-start(f32[1792,128]{1,0:T(8,128)S(1)} %slice_bitcast_fusion.3), channel_id=1, source_target_pairs={{0,2},{1,3},{2,0},{3,1},{4,6},{5,7},{6,4},{7,5},{8,10},{9,11},{10,... | collective-permute-start | bytes 2752520 | tf_op jit(solution)/shard_map/ppermute | solution.py:1289
  (100 other events, 1411.1 us)
Sparse Core Ops, SparseCore 0:
  11.0 192.0 all-gather.12
  205.9 234.4 all-gather.10
  443.2 118.8 all-gather.6
  564.6 78.3 all-gather.8
  695.0 192.7 all-reduce.21
